TPU v7x, 32 devices: a whole 2x2x4 slice. The times are simulated.
32 devices in a mesh: dom: 8 (over y, x, core), rep: 4 (over z).
Axes of the slice: x: 2, y: 2, z: 4, core: 2. Of those that a mesh axis runs over, the one named last changes fastest.
Arguments:
- features: bfloat16 [8192, 256], P(('dom', 'rep')), may hold values from -6 to 6
- weight: bfloat16 [256, 256], replicated, may hold values from -0.375 to 0.375
- tile_cols: int32 [64, 8], P(('dom', 'rep')), may hold values from 0 to 7
- tile_vals: bfloat16 [64, 8, 128, 128], P(('dom', 'rep')), may hold values from -0.1875 to 0.1875
- tile_counts: int32 [64], P(('dom', 'rep')), may hold values from 1 to 8
- send_rows: int32 [32, 8, 16], P(('dom', 'rep')), may hold values from 0 to 255
- bnd_adj: bfloat16 [8192, 128], P(('dom', 'rep')), may hold values from -0.5 to 0.5
- cotangent: bfloat16 [8192, 256], P(('dom', 'rep')), may hold values from -6 to 6
Outputs:
- output: bfloat16 [8192, 256], P(('dom', 'rep'))
- grad_features: bfloat16 [8192, 256], P(('dom', 'rep'))
- grad_weight: float32 [256, 256], replicated
Inputs may be any that keep to these rules, and one draw needn't show every extreme that they name: `send_rows`: local row index on the sending device; rows may repeat.
All inputs are finite; a program needn't handle non-finite values.
Results may differ from a plain program's by a relative error of at most 0.0085.
Values may be sent and summed in bfloat16 or wider, within the bound.
No kernel may reach another device: no remote copies, remote signals or barrier semaphores. Data moves between devices by JAX's collectives and lax.ppermute only.
A program may use at most 64 MiB of HBM per device.

v0:
```python
import jax
import jax.numpy as jnp
from jax import lax
from jax.sharding import PartitionSpec as P


def body(features, weight, tile_cols, tile_vals, tile_counts, send_rows, bnd_adj, cotangent):
    rows_here = features.shape[0]
    row_tiles = rows_here // 128
    width = weight.shape[1]
    slots = tile_cols.shape[1]
    groups = lax.axis_size("dom")
    projected = jnp.dot(features, weight, preferred_element_type=jnp.float32).astype(jnp.bfloat16)
    live = jnp.arange(slots)[None, :] < tile_counts[:, None]
    masked = jnp.where(live[:, :, None, None], tile_vals, jnp.zeros_like(tile_vals))
    panel = lax.all_gather(projected.reshape(row_tiles, 128, width), "rep", axis=0, tiled=True)
    chosen = panel[tile_cols]
    local = jnp.einsum("tkij,tkjh->tih", masked, chosen, preferred_element_type=jnp.float32)
    index_rows = send_rows[0]
    outgoing = projected[index_rows]
    received = lax.all_to_all(outgoing, "dom", split_axis=0, concat_axis=0, tiled=True)
    boundary = jnp.dot(bnd_adj, received.reshape(-1, width), preferred_element_type=jnp.float32)
    pre = local.reshape(rows_here, width) + boundary
    output = jax.nn.silu(pre).astype(jnp.bfloat16)
    sig = jax.nn.sigmoid(pre)
    grad_pre = (cotangent.astype(jnp.float32) * sig * (1.0 + pre * (1.0 - sig))).astype(
        jnp.bfloat16
    )
    grad_tiles = grad_pre.reshape(row_tiles, 128, width)
    terms = jnp.einsum("tkji,tih->tkjh", masked, grad_tiles, preferred_element_type=jnp.float32)
    wanted = jnp.arange(row_tiles * lax.axis_size("rep"), dtype=jnp.int32)
    onehot = (tile_cols[None, :, :] == wanted[:, None, None]).astype(jnp.float32)
    grad_local = lax.psum_scatter(
        jnp.einsum("ctk,tkjh->cjh", onehot, terms), "rep", scatter_dimension=0, tiled=True
    )
    grad_received = lax.dot_general(
        bnd_adj, grad_pre, (((0,), (0,)), ((), ())), preferred_element_type=jnp.float32
    )
    grad_received = grad_received.astype(jnp.bfloat16).reshape(groups, -1, width)
    returned = lax.all_to_all(grad_received, "dom", split_axis=0, concat_axis=0, tiled=True)
    onehot_rows = (
        jnp.arange(rows_here, dtype=jnp.int32)[:, None] == index_rows.reshape(-1)[None, :]
    ).astype(jnp.bfloat16)
    grad_boundary = jnp.dot(
        onehot_rows, returned.reshape(-1, width), preferred_element_type=jnp.float32
    )
    grad_projected = (grad_local.reshape(rows_here, width) + grad_boundary).astype(jnp.bfloat16)
    grad_features = lax.dot_general(
        grad_projected, weight, (((1,), (1,)), ((), ())), preferred_element_type=jnp.float32
    ).astype(jnp.bfloat16)
    partial_weight = lax.dot_general(
        features, grad_projected, (((0,), (0,)), ((), ())), preferred_element_type=jnp.float32
    )
    grad_weight = lax.psum(partial_weight, ("dom", "rep"))
    return (output, grad_features, grad_weight)


def solution(mesh):
    placed = (
        P(("dom", "rep"), None),
        P(),
        P(("dom", "rep"), None),
        P(("dom", "rep"), None, None, None),
        P(("dom", "rep")),
        P(("dom", "rep"), None, None),
        P(("dom", "rep"), None),
        P(("dom", "rep"), None),
    )
    return jax.shard_map(
        body,
        mesh=mesh,
        in_specs=placed,
        out_specs=(P(("dom", "rep"), None), P(("dom", "rep"), None), P()),
        check_vma=False,
    )
```

profile of v0, /device:TPU:0, one launch (start us, length us, event | category | flops | bytes accessed | tf_op | source)
XLA Modules:
  0.0 205.2 jit_solution(6942525118612908183)
XLA Ops:
  7.2 0.0 copy-start
  7.2 0.8 compare_select_fusion
  8.0 0.1 reshape.95
  8.1 0.0 copy-done
  8.1 1.1 convolution_convert_fusion.1
  9.2 1.5 gather_fusion.1
  10.6 5.2 %all-to-all-start = ((bf16[8,16,256]{2,1,0:T(8,128)(2,1)}), bf16[8,16,256]{2,1,0:T(8,128)(2,1)S(1)}, u32[]{:S(2)}, u32[]{:S(2)}) async-start(bf16[8,16,256]{2,1,0:T(8,128)(2,1)} %bitcast.6), calls=%async_computation | async-start | bytes 131072 | tf_op jit(solution)/shard_map/all_to_all | solution.py:21
  15.8 0.0 reduce-scatter.2.cloned.1.call-start
  15.9 0.1 iota_compare_fusion.3
  16.0 0.1 reshape.87
  16.0 16.4 %all_gather.3 = bf16[8,128,256]{2,1,0:T(8,128)(2,1)S(1)} all-gather(bf16[2,128,256]{2,1,0:T(8,128)(2,1)S(1)} %bitcast.46), channel_id=1, replica_groups=mesh['dom'=8,'rep'=4] {'rep'}, dimensions={0}, use_global_device_ids=true | all-gather | bytes 655360 | tf_op jit(solution)/shard_map/all_gather | solution.py:16
  32.5 0.1 broadcast_select_fusion
  32.6 0.6 gather_fusion
  33.3 0.3 fusion.14
  33.6 0.5 copy-done.3
  34.1 0.1 copy-done.6
  34.2 0.9 multiply_convert_fusion
  35.1 0.6 fusion.3
  35.7 1.3 copy.15
  37.0 0.0 reduce-scatter.2.cloned.1.call-update
  37.0 0.8 convolution_convert_fusion.2
  37.9 3.9 %all-to-all-start.1 = ((bf16[8,16,256]{2,1,0:T(8,128)(2,1)}), bf16[8,16,256]{2,1,0:T(8,128)(2,1)S(1)}, u32[]{:S(2)}, u32[]{:S(2)}) async-start(bf16[8,16,256]{2,1,0:T(8,128)(2,1)} %bitcast.16), calls=%async_computation.2 | async-start | bytes 131072 | tf_op jit(solution)/shard_map/all_to_all | solution.py:40
  41.7 0.0 all-reduce.2.cloned.1.call-start
  41.8 0.1 eq.32
  41.9 4.9 %all-to-all-done.1 = bf16[8,16,256]{2,1,0:T(8,128)(2,1)S(1)} async-done(((bf16[8,16,256]{2,1,0:T(8,128)(2,1)}), bf16[8,16,256]{2,1,0:T(8,128)(2,1)S(1)}, u32[]{:S(2)}, u32[]{:S(2)}) %all-to-all-start.1) | async-done | bytes 65568 | tf_op jit(solution)/shard_map/all_to_all | solution.py:40
  46.8 19.1 %reduce-scatter.2.cloned.1.call-done = f32[2,128,256]{2,1,0:T(8,128)} async-done(((f32[8,128,256]{2,1,0:T(8,128)}), f32[2,128,256]{2,1,0:T(8,128)}) %reduce-scatter.2.cloned.1.call-update) | async-done | bytes 262160 | tf_op jit(solution)/shard_map/reduce_scatter | solution.py:33
  65.9 1.1 fusion.7
  67.0 0.9 convolution_bitcast_fusion.1
  68.0 0.0 all-reduce.2.cloned.1.call-update
  68.0 0.9 convolution_convert_fusion
  68.9 127.7 %all-reduce.2.cloned.1.call-done = f32[256,256]{0,1:T(8,128)} async-done(((f32[256,256]{0,1:T(8,128)}), f32[256,256]{0,1:T(8,128)}) %all-reduce.2.cloned.1.call-update) | async-done | bytes 262160 | tf_op jit(solution)/shard_map/psum | solution.py:54
  196.6 1.8 copy.16
  (16 shorter events, 0.1 us)
Async XLA Ops:
  7.2 0.9 copy-start
  7.2 8.7 %copy-start.7 = (s32[2]{0:T(128)S(1)}, s32[2]{0:T(128)}, u32[]{:S(2)}) copy-start(s32[2]{0:T(128)} %param.12) | copy-start | bytes 28
  7.2 8.8 %copy-start.5 = (s32[2,8]{1,0:T(2,128)S(1)}, s32[2,8]{1,0:T(2,128)}, u32[]{:S(2)}) copy-start(s32[2,8]{1,0:T(2,128)} %param.10) | copy-start | bytes 196
  7.2 25.3 %copy-start.2 = (bf16[2,8,128,128]{3,2,1,0:T(8,128)(2,1)S(1)}, bf16[2,8,128,128]{3,2,1,0:T(8,128)(2,1)}, u32[]{:S(2)}) copy-start(bf16[2,8,128,128]{3,2,1,0:T(8,128)(2,1)} %param.11) | copy-start | bytes 1572868
  10.6 22.9 %all-to-all-start = ((bf16[8,16,256]{2,1,0:T(8,128)(2,1)}), bf16[8,16,256]{2,1,0:T(8,128)(2,1)S(1)}, u32[]{:S(2)}, u32[]{:S(2)}) async-start(bf16[8,16,256]{2,1,0:T(8,128)(2,1)} %bitcast.6), calls=%async_computation | async-start | bytes 131072 | tf_op jit(solution)/shard_map/all_to_all | solution.py:21
  15.8 50.1 %reduce-scatter.2.cloned.1.call-start = ((), (), s32[]{:S(2)}) async-start(), calls=%async_computation.3 | async-start | bytes 1310720 | tf_op jit(solution)/shard_map/reduce_scatter | solution.py:33
  33.2 0.8 copy-start.3
  33.2 0.9 copy-start.6
  37.0 4.8 %copy-start.4 = (s32[1,8,16]{2,1,0:T(8,128)S(1)}, s32[1,8,16]{2,1,0:T(8,128)}, u32[]{:S(2)}) copy-start(s32[1,8,16]{2,1,0:T(8,128)} %param.13) | copy-start | bytes 1540
  37.0 31.0 %copy-start.1 = (bf16[256,256]{1,0:T(8,128)(2,1)S(1)}, bf16[256,256]{1,0:T(8,128)(2,1)}, u32[]{:S(2)}) copy-start(bf16[256,256]{1,0:T(8,128)(2,1)} %param.9) | copy-start | bytes 393220
  37.9 8.9 %all-to-all-start.1 = ((bf16[8,16,256]{2,1,0:T(8,128)(2,1)}), bf16[8,16,256]{2,1,0:T(8,128)(2,1)S(1)}, u32[]{:S(2)}, u32[]{:S(2)}) async-start(bf16[8,16,256]{2,1,0:T(8,128)(2,1)} %bitcast.16), calls=%async_computation.2 | async-start | bytes 131072 | tf_op jit(solution)/shard_map/all_to_all | solution.py:40
  41.7 154.8 %all-reduce.2.cloned.1.call-start = ((), (), s32[]{:S(2)}) async-start(), calls=%async_computation.4 | async-start | bytes 524288 | tf_op jit(solution)/shard_map/psum | solution.py:54
Sparse Core Ops, SparseCore 0:
  37.1 28.7 reduce-scatter.1
  72.9 123.6 all-reduce.1
where the time goes:
time: 206 us; the launch traced here: 205 us
  waiting for transfers between devices  152 us (74%)
  blocking collectives  16.4 us (8%)
  between operations  14.2 us (7%)
  starting transfers between devices  9.11 us (4%)
  matrix products  6.67 us (3%)
  local copies, waits for them, and re-layouts  6.06 us (3%)
    psum x1, waiting for transfers between devices, body(): grad_weight = lax.psum(partial_weight, ('dom', 'rep'))  128 us
    reduce_scatter x1, waiting for transfers between devices, body(): lax.psum_scatter(jnp.einsum('ctk,tkjh->cjh', onehot, terms), 'rep', scatt...  19.1 us
    all_gather x1, blocking collectives, body(): lax.all_gather(projected.reshape(row_tiles, 128, width), 'rep', axis=0, t...  16.4 us
    all_to_all x1, starting transfers between devices, body(): lax.all_to_all(outgoing, 'dom', split_axis=0, concat_axis=0, tiled=True)  5.17 us
    all_to_all x1, waiting for transfers between devices, body(): lax.all_to_all(grad_received, 'dom', split_axis=0, concat_axis=0, tiled=T...  4.88 us
  transfers between devices with their start and end apart: 4, of which 3 were waited for; matrix products, arithmetic and copies ran while one was open for 1% of the time, Pallas kernels for 0%

commit v1 on v0

v1 whole, which is shorter than its diff:
```python
import functools

import jax
import jax.numpy as jnp
from jax import lax
from jax.experimental import pallas as pl
from jax.experimental.pallas import tpu as pltpu
from jax.sharding import PartitionSpec as P

TILE = 128
F32 = jnp.float32
BF16 = jnp.bfloat16
VMEM = pl.BlockSpec(memory_space=pltpu.VMEM)
SMEM = pl.BlockSpec(memory_space=pltpu.SMEM)


def dot(a, b, contract_a, contract_b):
    return lax.dot_general(
        a, b, (((contract_a,), (contract_b,)), ((), ())), preferred_element_type=F32
    )


def wanted_rows(index_ref, rows):
    groups = index_ref.shape[1]
    flat = jnp.concatenate([index_ref[0, q : q + 1, :] for q in range(groups)], axis=1)
    at = lax.broadcasted_iota(jnp.int32, (rows, flat.shape[1]), 0)
    return jnp.where(at == flat, 1.0, 0.0).astype(BF16)


def pick_kernel(index_ref, features_ref, out_ref):
    onehot = wanted_rows(index_ref, features_ref.shape[0])
    picked = dot(onehot, features_ref[...], 0, 0).astype(BF16)
    each = out_ref.shape[1]
    for q in range(out_ref.shape[0]):
        out_ref[q] = picked[q * each : (q + 1) * each]


def layer_kernel(rep, cols_ref, counts_ref, vals_ref, received_ref, bnd_ref, cot_ref, weight_ref, *refs):
    blocks = refs[:rep]
    out_ref, own_ref = refs[rep], refs[rep + 1]
    sends = refs[rep + 2 : 2 * rep + 1]
    message_ref, panel, terms = refs[2 * rep + 1 :]
    me = lax.axis_index("rep")
    tiles, slots = cols_ref.shape
    width = weight_ref.shape[1]
    for shift, block in enumerate(blocks):
        owner = lax.rem(me - shift + rep, rep)
        for t in range(tiles):
            panel[owner * tiles + t] = block[t * TILE : (t + 1) * TILE, :]
    groups, each = received_ref.shape[0], received_ref.shape[1]
    received = jnp.concatenate([received_ref[q] for q in range(groups)], axis=0)
    adjacency = []
    forward = []
    backward = []
    for t in range(tiles):
        live = [
            jnp.where(k < counts_ref[t], vals_ref[t, k], jnp.zeros_like(vals_ref[t, k]))
            for k in range(slots)
        ]
        chosen = jnp.concatenate([panel[cols_ref[t, k]] for k in range(slots)], axis=0)
        stacked = jnp.concatenate(live, axis=0)
        adjacency.append(stacked)
        forward.append(dot(jnp.concatenate(live, axis=1), chosen, 1, 0))
        backward.append(dot(stacked, chosen, 0, 0))
    outside = dot(bnd_ref[...], received, 1, 0)
    mixed = jnp.concatenate(forward, axis=0) + outside
    turned = (jnp.concatenate(backward, axis=0) + outside).astype(BF16)
    high = mixed.astype(BF16)
    low = (mixed - high.astype(F32)).astype(BF16)
    weight = weight_ref[...]
    pre = dot(high, weight, 1, 0) + dot(low, weight, 1, 0)
    sig = jax.nn.sigmoid(pre)
    out_ref[...] = (pre * sig).astype(BF16)
    grad = (cot_ref[...].astype(F32) * sig * (1.0 + pre * (1.0 - sig))).astype(BF16)
    terms[...] = jnp.zeros_like(terms)
    for t in range(tiles):
        parts = dot(adjacency[t], grad[t * TILE : (t + 1) * TILE], 1, 0)
        for k in range(slots):
            terms[cols_ref[t, k]] += parts[k * TILE : (k + 1) * TILE]
    for t in range(tiles):
        own_ref[t * TILE : (t + 1) * TILE, :] = terms[me * tiles + t]
        for shift, send in enumerate(sends, 1):
            owner = lax.rem(me + shift, rep)
            send[t * TILE : (t + 1) * TILE, :] = terms[owner * tiles + t].astype(BF16)
    boundary = dot(bnd_ref[...], grad, 0, 0).astype(BF16)
    partial = dot(turned, grad, 0, 0).astype(BF16)
    share = partial.shape[0] // groups
    for q in range(groups):
        message_ref[q, :each, :] = boundary[q * each : (q + 1) * each]
        message_ref[q, each:, :] = partial[q * share : (q + 1) * share]


def final_kernel(index_ref, returned_ref, weight_ref, own_ref, *refs):
    arrived, out_ref = refs[:-1], refs[-1]
    groups, each = index_ref.shape[1], index_ref.shape[2]
    onehot = wanted_rows(index_ref, own_ref.shape[0])
    returned = jnp.concatenate([returned_ref[q, :each, :] for q in range(groups)], axis=0)
    total = own_ref[...] + dot(onehot, returned, 1, 0)
    for term in arrived:
        total = total + term[...].astype(F32)
    out_ref[...] = dot(total.astype(BF16), weight_ref[...], 1, 1).astype(BF16)


def body(features, weight, tile_cols, tile_vals, tile_counts, send_rows, bnd_adj, cotangent):
    rows, feats = features.shape
    width = weight.shape[1]
    tiles, slots = tile_cols.shape
    groups, each = send_rows.shape[1], send_rows.shape[2]
    rep = lax.axis_size("rep")
    share = feats // groups
    params = pltpu.CompilerParams(vmem_limit_bytes=40 * 1024 * 1024)

    def shifted(value, shift):
        return lax.ppermute(value, "rep", [(i, (i + shift) % rep) for i in range(rep)])

    blocks = [features] + [shifted(features, shift) for shift in range(1, rep)]
    outgoing = pl.pallas_call(
        pick_kernel,
        out_shape=jax.ShapeDtypeStruct((groups, each, feats), BF16),
        in_specs=[VMEM] * 2,
        out_specs=VMEM,
        compiler_params=params,
        name="pick_rows",
    )(send_rows, features)
    received = lax.all_to_all(outgoing, "dom", split_axis=0, concat_axis=0, tiled=True)
    results = pl.pallas_call(
        functools.partial(layer_kernel, rep),
        out_shape=[
            jax.ShapeDtypeStruct((rows, width), BF16),
            jax.ShapeDtypeStruct((rows, width), F32),
            *[jax.ShapeDtypeStruct((rows, width), BF16)] * (rep - 1),
            jax.ShapeDtypeStruct((groups, each + share, width), BF16),
        ],
        in_specs=[SMEM] * 2 + [VMEM] * (5 + rep),
        out_specs=[VMEM] * (rep + 2),
        scratch_shapes=[
            pltpu.VMEM((rep * tiles, TILE, feats), BF16),
            pltpu.VMEM((rep * tiles, TILE, width), F32),
        ],
        compiler_params=params,
        name="layer",
    )(tile_cols, tile_counts, tile_vals, received, bnd_adj, cotangent, weight, *blocks)
    output, own, sends, message = results[0], results[1], results[2:-1], results[-1]
    returned = lax.all_to_all(message, "dom", split_axis=0, concat_axis=0, tiled=True)
    arrived = [shifted(send, shift) for shift, send in enumerate(sends, 1)]
    chunk = jnp.sum(returned[:, each:].astype(F32), axis=0).astype(BF16)
    if rep == 4:
        one, two, three = [shifted(chunk, shift).astype(F32) for shift in (1, 2, 3)]
        total = (chunk.astype(F32) + two) + (one + three)
    else:
        total = jnp.sum(lax.all_gather(chunk, "rep").astype(F32), axis=0)
    spread = jnp.broadcast_to(total.astype(BF16)[None], (groups, share, width))
    grad_weight = lax.all_to_all(spread, "dom", split_axis=0, concat_axis=0, tiled=True)
    grad_weight = grad_weight.reshape(feats, width).astype(F32)
    grad_features = pl.pallas_call(
        final_kernel,
        out_shape=jax.ShapeDtypeStruct((rows, feats), BF16),
        in_specs=[VMEM] * (3 + rep),
        out_specs=VMEM,
        compiler_params=params,
        name="input_gradient",
    )(send_rows, returned, weight, own, *arrived)
    return (output, grad_features, grad_weight)


def solution(mesh):
    placed = (
        P(("dom", "rep"), None),
        P(),
        P(("dom", "rep"), None),
        P(("dom", "rep"), None, None, None),
        P(("dom", "rep")),
        P(("dom", "rep"), None, None),
        P(("dom", "rep"), None),
        P(("dom", "rep"), None),
    )
    return jax.shard_map(
        body,
        mesh=mesh,
        in_specs=placed,
        out_specs=(P(("dom", "rep"), None), P(("dom", "rep"), None), P()),
        check_vma=False,
    )
```

time: 206 us -> 53.2 us (0.26)
  waiting for transfers between devices: 152 us -> 6.76 us
  between operations: 14.2 us -> 0.75 us
  starting transfers between devices: 9.11 us -> 19.4 us
  matrix products: 6.67 us -> 0 us
  Pallas kernels: 0 us -> 3.63 us
    psum x1 -> x0, waiting for transfers between devices: 128 us -> none  [body(): grad_weight = lax.psum(partial_weight, ('dom', 'rep'))]
    reduce_scatter x1 -> x0, waiting for transfers between devices: 19.1 us -> none  [body(): lax.psum_scatter(jnp.einsum('ctk,tkjh->cjh', onehot, terms), 'rep', scatt...]
    all_to_all x0 -> x2, blocking collectives: none -> 17.3 us  [the longest x1 8.67 us: body(): lax.all_to_all(outgoing, 'dom', split_axis=0, concat_axis=0, tiled=True)]
    all_gather x1 -> x0, blocking collectives: 16.4 us -> none  [body(): lax.all_gather(projected.reshape(row_tiles, 128, width), 'rep', axis=0, t...]
    ppermute x0 -> x9, starting transfers between devices: none -> 15.9 us  [shifted(): lax.ppermute(value, 'rep', [(i, (i + shift) % rep) for i in range(rep)])]
    dot_general x8 -> x0, matrix products: 6.67 us -> none  [the longest x1 1.12 us: body(): jnp.dot(onehot_rows, returned.reshape(-1, width), preferred_element_type=...]
    all_to_all x2 -> x1, starting transfers between devices: 9.03 us -> 3.5 us  [body(): lax.all_to_all(spread, 'dom', split_axis=0, concat_axis=0, tiled=True)]
    pallas_call x0 -> x3, Pallas kernels: none -> 3.63 us  [the longest x1 2.32 us: body(): pl.pallas_call(functools.partial(layer_kernel, rep), out_shape=[jax.Shape...]
  transfers between devices with their start and end apart: 4 -> 10, of which waited for: 3 -> 3; matrix products, arithmetic and copies ran while one was open for 1% -> 1% of each run, Pallas kernels for 0% -> 2%
where the time goes in v1:
time: 53.2 us; the launch traced here: 52.8 us
  starting transfers between devices  19.4 us (36%)
  blocking collectives  17.3 us (33%)
  waiting for transfers between devices  6.76 us (13%)
  local copies, waits for them, and re-layouts  4.26 us (8%)
  Pallas kernels  3.63 us (7%)
  other arithmetic  0.76 us (1%)
  between operations  0.75 us (1%)
    ppermute x9, starting transfers between devices, shifted(): lax.ppermute(value, 'rep', [(i, (i + shift) % rep) for i in range(rep)])  15.9 us
    all_to_all x1, blocking collectives, body(): lax.all_to_all(outgoing, 'dom', split_axis=0, concat_axis=0, tiled=True)  8.67 us
    all_to_all x1, blocking collectives, body(): lax.all_to_all(message, 'dom', split_axis=0, concat_axis=0, tiled=True)  8.62 us
    all_to_all x1, waiting for transfers between devices, body(): lax.all_to_all(spread, 'dom', split_axis=0, concat_axis=0, tiled=True)  3.66 us
    unnamed x20, local copies, waits for them, and re-layouts  3.59 us
    all_to_all x1, starting transfers between devices, body(): lax.all_to_all(spread, 'dom', split_axis=0, concat_axis=0, tiled=True)  3.5 us
    ppermute x9, waiting for transfers between devices, shifted(): lax.ppermute(value, 'rep', [(i, (i + shift) % rep) for i in range(rep)])  3.1 us
    pallas_call x1, Pallas kernels, body(): pl.pallas_call(functools.partial(layer_kernel, rep), out_shape=[jax.Shape...  2.32 us
  transfers between devices with their start and end apart: 10, of which 3 were waited for; matrix products, arithmetic and copies ran while one was open for 1% of the time, Pallas kernels for 2%

profile of v1, /device:TPU:0, one launch (start us, length us, event | category | flops | bytes accessed | tf_op | source)
XLA Modules:
  0.0 52.8 jit_solution(17530426730175257903)
XLA Ops:
  0.6 4.1 %collective-permute-start.1 = (bf16[256,256]{1,0:T(8,128)(2,1)}, bf16[256,256]{1,0:T(8,128)(2,1)S(1)}, u32[]{:S(2)}, u32[]{:S(2)}) collective-permute-start(bf16[256,256]{1,0:T(8,128)(2,1)} %refs_0_.1), channel_id=1, source_target_pairs={{0,2},{1,3},{2,0},{3,1},{4,6},{5,7},{6,4},{7,5},{8,10},{9,11},{10,... | collective-permute-start | bytes 393224 | tf_op jit(solution)/shard_map/ppermute | solution.py:114
  4.7 1.6 %collective-permute-start = (bf16[256,256]{1,0:T(8,128)(2,1)}, bf16[256,256]{1,0:T(8,128)(2,1)S(1)}, u32[]{:S(2)}, u32[]{:S(2)}) collective-permute-start(bf16[256,256]{1,0:T(8,128)(2,1)} %refs_0_.1), channel_id=1, source_target_pairs={{0,1},{1,2},{2,3},{3,0},{4,5},{5,6},{6,7},{7,4},{8,9},{9,10},{10,1... | collective-permute-start | bytes 393224 | tf_op jit(solution)/shard_map/ppermute | solution.py:114
  6.3 2.2 %collective-permute-start.2 = (bf16[256,256]{1,0:T(8,128)(2,1)}, bf16[256,256]{1,0:T(8,128)(2,1)S(1)}, u32[]{:S(2)}, u32[]{:S(2)}) collective-permute-start(bf16[256,256]{1,0:T(8,128)(2,1)} %refs_0_.1), channel_id=1, source_target_pairs={{0,3},{1,0},{2,1},{3,2},{4,7},{5,4},{6,5},{7,6},{8,11},{9,8},{10,9... | collective-permute-start | bytes 393224 | tf_op jit(solution)/shard_map/ppermute | solution.py:114
  8.6 0.9 %copy-done.2 = bf16[256,256]{1,0:T(8,128)(2,1)S(1)} copy-done((bf16[256,256]{1,0:T(8,128)(2,1)S(1)}, bf16[256,256]{1,0:T(8,128)(2,1)}, u32[]{:S(2)}) %copy-start.2) | copy-done | bytes 131096
  9.5 0.7 %copy-done.6 = s32[1,8,16]{2,1,0:T(8,128)S(1)} copy-done((s32[1,8,16]{2,1,0:T(8,128)S(1)}, s32[1,8,16]{2,1,0:T(8,128)}, u32[]{:S(2)}) %copy-start.6) | copy-done | bytes 536
  10.2 0.3 pick_rows.1
  10.5 0.0 copy-start.5
  10.5 0.0 copy-start.8
  10.5 0.0 copy-start.9
  10.5 8.7 %all_to_all.15.received_ref = bf16[8,16,256]{2,1,0:T(8,128)(2,1)S(1)} all-to-all(bf16[8,16,256]{2,1,0:T(8,128)(2,1)S(1)} %pick_rows.1), channel_id=1, replica_groups=mesh['dom'=8,'rep'=4] {'dom'}, dimensions={0} | all-to-all | bytes 131072 | tf_op jit(solution)/shard_map/all_to_all | solution.py:125
  19.2 0.0 collective-permute-done.1.refs_2_
  19.2 0.0 collective-permute-done.refs_1_
  19.2 0.0 collective-permute-done.2.refs_3_
  19.2 0.0 copy-start
  19.2 1.0 %copy-done = bf16[2,8,128,128]{3,2,1,0:T(8,128)(2,1)S(1)} copy-done((bf16[2,8,128,128]{3,2,1,0:T(8,128)(2,1)S(1)}, bf16[2,8,128,128]{3,2,1,0:T(8,128)(2,1)}, u32[]{:S(2)}) %copy-start) | copy-done | bytes 524312
  20.3 0.9 %copy-done.4 = bf16[256,256]{1,0:T(8,128)(2,1)S(1)} copy-done((bf16[256,256]{1,0:T(8,128)(2,1)S(1)}, bf16[256,256]{1,0:T(8,128)(2,1)}, u32[]{:S(2)}) %copy-start.4) | copy-done | bytes 131096
  21.2 2.3 %layer.1 = (bf16[256,256]{1,0:T(8,128)(2,1)}, f32[256,256]{1,0:T(8,128)S(1)}, bf16[256,256]{1,0:T(8,128)(2,1)S(1)}, bf16[256,256]{1,0:T(8,128)(2,1)S(1)}, bf16[2...) custom-call(s32[2,8]{1,0:T(2,128)S(1)} %copy-done.8, s32[2]{0:T(128)S(1)} %copy-done.9, ...), custom_call_target="tpu_custom_call" | custom-call | tf_op jit(solution)/shard_map/layer/pallas_call | solution.py:126
  23.5 8.6 %all_to_all.16.returned_ref = bf16[8,48,256]{2,1,0:T(8,128)(2,1)S(1)} all-to-all(bf16[8,48,256]{2,1,0:T(8,128)(2,1)S(1)} %get-tuple-element.10), channel_id=1, replica_groups=mesh['dom'=8,'rep'=4] {'dom'}, dimensions={0} | all-to-all | bytes 393216 | tf_op jit(solution)/shard_map/all_to_all | solution.py:144
  32.1 0.1 collective-permute-start.8
  32.2 2.0 %collective-permute-start.7 = (bf16[32,256]{1,0:T(8,128)(2,1)S(1)}, bf16[32,256]{1,0:T(8,128)(2,1)S(1)}, u32[]{:S(2)}, u32[]{:S(2)}) collective-permute-start(bf16[32,256]{1,0:T(8,128)(2,1)S(1)} %slice_reduce_fusion), channel_id=1, source_target_pairs={{0,1},{1,2},{2,3},{3,0},{4,5},{5,6},{6,7},{7,4},{8,9},{9,10},{10,1... | collective-permute-start | bytes 49160 | tf_op jit(solution)/shard_map/ppermute | solution.py:114
  34.2 1.4 %collective-permute-start.6 = (bf16[32,256]{1,0:T(8,128)(2,1)S(1)}, bf16[32,256]{1,0:T(8,128)(2,1)S(1)}, u32[]{:S(2)}, u32[]{:S(2)}) collective-permute-start(bf16[32,256]{1,0:T(8,128)(2,1)S(1)} %slice_reduce_fusion), channel_id=1, source_target_pairs={{0,2},{1,3},{2,0},{3,1},{4,6},{5,7},{6,4},{7,5},{8,10},{9,11},{10,... | collective-permute-start | bytes 49160 | tf_op jit(solution)/shard_map/ppermute | solution.py:114
  35.7 1.0 %collective-permute-start.3 = (bf16[256,256]{1,0:T(8,128)(2,1)S(1)}, bf16[256,256]{1,0:T(8,128)(2,1)S(1)}, u32[]{:S(2)}, u32[]{:S(2)}) collective-permute-start(bf16[256,256]{1,0:T(8,128)(2,1)S(1)} %get-tuple-element.12), channel_id=1, source_target_pairs={{0,1},{1,2},{2,3},{3,0},{4,5},{5,6},{6,7},{7,4},{8,9},{9,10},{10,1... | collective-permute-start | bytes 393224 | tf_op jit(solution)/shard_map/ppermute | solution.py:114
  36.7 0.5 %collective-permute-start.4 = (bf16[256,256]{1,0:T(8,128)(2,1)S(1)}, bf16[256,256]{1,0:T(8,128)(2,1)S(1)}, u32[]{:S(2)}, u32[]{:S(2)}) collective-permute-start(bf16[256,256]{1,0:T(8,128)(2,1)S(1)} %get-tuple-element.13), channel_id=1, source_target_pairs={{0,2},{1,3},{2,0},{3,1},{4,6},{5,7},{6,4},{7,5},{8,10},{9,11},{10,... | collective-permute-start | bytes 393224 | tf_op jit(solution)/shard_map/ppermute | solution.py:114
  37.2 0.0 collective-permute-done.8
  37.2 2.9 %collective-permute-start.5 = (bf16[256,256]{1,0:T(8,128)(2,1)S(1)}, bf16[256,256]{1,0:T(8,128)(2,1)S(1)}, u32[]{:S(2)}, u32[]{:S(2)}) collective-permute-start(bf16[256,256]{1,0:T(8,128)(2,1)S(1)} %get-tuple-element.14), channel_id=1, source_target_pairs={{0,3},{1,0},{2,1},{3,2},{4,7},{5,4},{6,5},{7,6},{8,11},{9,8},{10,9... | collective-permute-start | bytes 393224 | tf_op jit(solution)/shard_map/ppermute | solution.py:114
  40.1 2.3 %collective-permute-done.6 = bf16[32,256]{1,0:T(8,128)(2,1)S(1)} collective-permute-done((bf16[32,256]{1,0:T(8,128)(2,1)S(1)}, bf16[32,256]{1,0:T(8,128)(2,1)S(1)}, u32[]{:S(2)}, u32[]{:S(2)}) %collective-permute-start.6) | collective-permute-done | bytes 16416 | tf_op jit(solution)/shard_map/ppermute | solution.py:114
  42.4 0.7 %broadcast_in_dim.2 = bf16[8,32,256]{2,1,0:T(8,128)(2,1)} broadcast(bf16[32,256]{1,0:T(8,128)(2,1)S(1)} %add_convert_fusion), dimensions={1,2} | broadcast | bytes 147456 | tf_op jit(solution)/shard_map/broadcast_in_dim | solution.py:152
  43.1 3.5 %all-to-all-start.2 = ((bf16[8,32,256]{2,1,0:T(8,128)(2,1)}), bf16[8,32,256]{2,1,0:T(8,128)(2,1)S(1)}, u32[]{:S(2)}, u32[]{:S(2)}) async-start(bf16[8,32,256]{2,1,0:T(8,128)(2,1)} %broadcast_in_dim.2), calls=%async_computation.2 | async-start | bytes 262144 | tf_op jit(solution)/shard_map/all_to_all | solution.py:153
  46.6 0.7 %collective-permute-done.4.refs_1_ = bf16[256,256]{1,0:T(8,128)(2,1)S(1)} collective-permute-done((bf16[256,256]{1,0:T(8,128)(2,1)S(1)}, bf16[256,256]{1,0:T(8,128)(2,1)S(1)}, u32[]{:S(2)}, u32[]{:S(2)}) %collective-permute-start.4) | collective-permute-done | bytes 131104 | tf_op jit(solution)/shard_map/ppermute | solution.py:114
  47.4 1.0 %input_gradient.1 = bf16[256,256]{1,0:T(8,128)(2,1)} custom-call(s32[1,8,16]{2,1,0:T(8,128)S(1)} %copy-done.7, bf16[8,48,256]{2,1,0:T(8,128)(2,1)S(1)} %all_to_all.16.returned_ref, bf16[256,256]{1,0:T(8,128)(2,1)S(1)} %copy-done.1, f32[256,256]{1,0:T(8,128)S(1)} %get-tuple-element.11.own_ref, bf16[256,256]{1,0:T(8,128)(2,1)S(1)} %collective-permute-done.3.refs_0_, ...), custom_call_target="tpu_custom_call" | custom-call | tf_op jit(solution)/shard_map/input_gradient/pallas_call | solution.py:155
  48.4 3.7 %all-to-all-done.2 = bf16[8,32,256]{2,1,0:T(8,128)(2,1)S(1)} async-done(((bf16[8,32,256]{2,1,0:T(8,128)(2,1)}), bf16[8,32,256]{2,1,0:T(8,128)(2,1)S(1)}, u32[]{:S(2)}, u32[]{:S(2)}) %all-to-all-start.2) | async-done | bytes 131104 | tf_op jit(solution)/shard_map/all_to_all | solution.py:153
  52.1 0.7 %bitcast_convert_fusion = f32[256,256]{1,0:T(8,128)} fusion(bf16[8,32,256]{2,1,0:T(8,128)(2,1)S(1)} %all-to-all-done.2), kind=kLoop, calls=%fused_computation.1 | loop fusion | flops 65536 | bytes 393216 | tf_op jit(solution)/shard_map/convert_element_type | solution.py:154
  (17 shorter events, 0.1 us)
Async XLA Ops:
  0.6 18.6 %copy-start.1 = (bf16[256,256]{1,0:T(8,128)(2,1)S(1)}, bf16[256,256]{1,0:T(8,128)(2,1)}, u32[]{:S(2)}) copy-start(bf16[256,256]{1,0:T(8,128)(2,1)} %weight_ref.3) | copy-start | bytes 393220
  0.6 18.5 %collective-permute-start.1 = (bf16[256,256]{1,0:T(8,128)(2,1)}, bf16[256,256]{1,0:T(8,128)(2,1)S(1)}, u32[]{:S(2)}, u32[]{:S(2)}) collective-permute-start(bf16[256,256]{1,0:T(8,128)(2,1)} %refs_0_.1), channel_id=1, source_target_pairs={{0,2},{1,3},{2,0},{3,1},{4,6},{5,7},{6,4},{7,5},{8,10},{9,11},{10,... | collective-permute-start | bytes 393224 | tf_op jit(solution)/shard_map/ppermute | solution.py:114
  4.7 14.4 %collective-permute-start = (bf16[256,256]{1,0:T(8,128)(2,1)}, bf16[256,256]{1,0:T(8,128)(2,1)S(1)}, u32[]{:S(2)}, u32[]{:S(2)}) collective-permute-start(bf16[256,256]{1,0:T(8,128)(2,1)} %refs_0_.1), channel_id=1, source_target_pairs={{0,1},{1,2},{2,3},{3,0},{4,5},{5,6},{6,7},{7,4},{8,9},{9,10},{10,1... | collective-permute-start | bytes 393224 | tf_op jit(solution)/shard_map/ppermute | solution.py:114
  6.3 12.9 %collective-permute-start.2 = (bf16[256,256]{1,0:T(8,128)(2,1)}, bf16[256,256]{1,0:T(8,128)(2,1)S(1)}, u32[]{:S(2)}, u32[]{:S(2)}) collective-permute-start(bf16[256,256]{1,0:T(8,128)(2,1)} %refs_0_.1), channel_id=1, source_target_pairs={{0,3},{1,0},{2,1},{3,2},{4,7},{5,4},{6,5},{7,6},{8,11},{9,8},{10,9... | collective-permute-start | bytes 393224 | tf_op jit(solution)/shard_map/ppermute | solution.py:114
  8.6 0.9 %copy-start.2 = (bf16[256,256]{1,0:T(8,128)(2,1)S(1)}, bf16[256,256]{1,0:T(8,128)(2,1)}, u32[]{:S(2)}) copy-start(bf16[256,256]{1,0:T(8,128)(2,1)} %refs_0_.1) | copy-start | bytes 393220
  9.5 0.7 %copy-start.6 = (s32[1,8,16]{2,1,0:T(8,128)S(1)}, s32[1,8,16]{2,1,0:T(8,128)}, u32[]{:S(2)}) copy-start(s32[1,8,16]{2,1,0:T(8,128)} %index_ref.3) | copy-start | bytes 1540
  10.2 9.0 %copy-start.3 = (bf16[256,256]{1,0:T(8,128)(2,1)S(1)}, bf16[256,256]{1,0:T(8,128)(2,1)}, u32[]{:S(2)}) copy-start(bf16[256,256]{1,0:T(8,128)(2,1)} %refs_0_.1) | copy-start | bytes 393220
  10.5 8.7 %copy-start.5 = (bf16[256,128]{1,0:T(8,128)(2,1)S(1)}, bf16[256,128]{1,0:T(8,128)(2,1)}, u32[]{:S(2)}) copy-start(bf16[256,128]{1,0:T(8,128)(2,1)} %bnd_ref.1) | copy-start | bytes 196612
  10.5 8.7 %copy-start.8 = (s32[2,8]{1,0:T(2,128)S(1)}, s32[2,8]{1,0:T(2,128)}, u32[]{:S(2)}) copy-start(s32[2,8]{1,0:T(2,128)} %cols_ref.1) | copy-start | bytes 196
  10.5 8.7 %copy-start.9 = (s32[2]{0:T(128)S(1)}, s32[2]{0:T(128)}, u32[]{:S(2)}) copy-start(s32[2]{0:T(128)} %counts_ref.1) | copy-start | bytes 28
  19.2 1.0 %copy-start = (bf16[2,8,128,128]{3,2,1,0:T(8,128)(2,1)S(1)}, bf16[2,8,128,128]{3,2,1,0:T(8,128)(2,1)}, u32[]{:S(2)}) copy-start(bf16[2,8,128,128]{3,2,1,0:T(8,128)(2,1)} %vals_ref.1) | copy-start | bytes 1572868
  20.3 0.9 %copy-start.4 = (bf16[256,256]{1,0:T(8,128)(2,1)S(1)}, bf16[256,256]{1,0:T(8,128)(2,1)}, u32[]{:S(2)}) copy-start(bf16[256,256]{1,0:T(8,128)(2,1)} %cot_ref.1) | copy-start | bytes 393220
  32.1 5.0 %collective-permute-start.8 = (bf16[32,256]{1,0:T(8,128)(2,1)S(1)}, bf16[32,256]{1,0:T(8,128)(2,1)S(1)}, u32[]{:S(2)}, u32[]{:S(2)}) collective-permute-start(bf16[32,256]{1,0:T(8,128)(2,1)S(1)} %slice_reduce_fusion), channel_id=1, source_target_pairs={{0,3},{1,0},{2,1},{3,2},{4,7},{5,4},{6,5},{7,6},{8,11},{9,8},{10,9... | collective-permute-start | bytes 49160 | tf_op jit(solution)/shard_map/ppermute | solution.py:114
  32.2 7.9 %collective-permute-start.7 = (bf16[32,256]{1,0:T(8,128)(2,1)S(1)}, bf16[32,256]{1,0:T(8,128)(2,1)S(1)}, u32[]{:S(2)}, u32[]{:S(2)}) collective-permute-start(bf16[32,256]{1,0:T(8,128)(2,1)S(1)} %slice_reduce_fusion), channel_id=1, source_target_pairs={{0,1},{1,2},{2,3},{3,0},{4,5},{5,6},{6,7},{7,4},{8,9},{9,10},{10,1... | collective-permute-start | bytes 49160 | tf_op jit(solution)/shard_map/ppermute | solution.py:114
  34.2 8.2 %collective-permute-start.6 = (bf16[32,256]{1,0:T(8,128)(2,1)S(1)}, bf16[32,256]{1,0:T(8,128)(2,1)S(1)}, u32[]{:S(2)}, u32[]{:S(2)}) collective-permute-start(bf16[32,256]{1,0:T(8,128)(2,1)S(1)} %slice_reduce_fusion), channel_id=1, source_target_pairs={{0,2},{1,3},{2,0},{3,1},{4,6},{5,7},{6,4},{7,5},{8,10},{9,11},{10,... | collective-permute-start | bytes 49160 | tf_op jit(solution)/shard_map/ppermute | solution.py:114
  35.7 11.0 %collective-permute-start.3 = (bf16[256,256]{1,0:T(8,128)(2,1)S(1)}, bf16[256,256]{1,0:T(8,128)(2,1)S(1)}, u32[]{:S(2)}, u32[]{:S(2)}) collective-permute-start(bf16[256,256]{1,0:T(8,128)(2,1)S(1)} %get-tuple-element.12), channel_id=1, source_target_pairs={{0,1},{1,2},{2,3},{3,0},{4,5},{5,6},{6,7},{7,4},{8,9},{9,10},{10,1... | collective-permute-start | bytes 393224 | tf_op jit(solution)/shard_map/ppermute | solution.py:114
  36.7 10.7 %collective-permute-start.4 = (bf16[256,256]{1,0:T(8,128)(2,1)S(1)}, bf16[256,256]{1,0:T(8,128)(2,1)S(1)}, u32[]{:S(2)}, u32[]{:S(2)}) collective-permute-start(bf16[256,256]{1,0:T(8,128)(2,1)S(1)} %get-tuple-element.13), channel_id=1, source_target_pairs={{0,2},{1,3},{2,0},{3,1},{4,6},{5,7},{6,4},{7,5},{8,10},{9,11},{10,... | collective-permute-start | bytes 393224 | tf_op jit(solution)/shard_map/ppermute | solution.py:114
  37.2 10.2 %collective-permute-start.5 = (bf16[256,256]{1,0:T(8,128)(2,1)S(1)}, bf16[256,256]{1,0:T(8,128)(2,1)S(1)}, u32[]{:S(2)}, u32[]{:S(2)}) collective-permute-start(bf16[256,256]{1,0:T(8,128)(2,1)S(1)} %get-tuple-element.14), channel_id=1, source_target_pairs={{0,3},{1,0},{2,1},{3,2},{4,7},{5,4},{6,5},{7,6},{8,11},{9,8},{10,9... | collective-permute-start | bytes 393224 | tf_op jit(solution)/shard_map/ppermute | solution.py:114
  43.1 4.3 %copy-start.7 = (s32[1,8,16]{2,1,0:T(8,128)S(1)}, s32[1,8,16]{2,1,0:T(8,128)}, u32[]{:S(2)}) copy-start(s32[1,8,16]{2,1,0:T(8,128)} %index_ref.3) | copy-start | bytes 1540
  43.1 9.0 %all-to-all-start.2 = ((bf16[8,32,256]{2,1,0:T(8,128)(2,1)}), bf16[8,32,256]{2,1,0:T(8,128)(2,1)S(1)}, u32[]{:S(2)}, u32[]{:S(2)}) async-start(bf16[8,32,256]{2,1,0:T(8,128)(2,1)} %broadcast_in_dim.2), calls=%async_computation.2 | async-start | bytes 262144 | tf_op jit(solution)/shard_map/all_to_all | solution.py:153

commit v2 on v1

--- a/solution.py
+++ b/solution.py
@@ -11,6 +11,7 @@
 F32 = jnp.float32
 BF16 = jnp.bfloat16
 VMEM = pl.BlockSpec(memory_space=pltpu.VMEM)
+HBM = pl.BlockSpec(memory_space=pltpu.HBM)
 SMEM = pl.BlockSpec(memory_space=pltpu.SMEM)
 
 
@@ -18,6 +19,14 @@
     return lax.dot_general(
         a, b, (((contract_a,), (contract_b,)), ((), ())), preferred_element_type=F32
     )
+
+
+def target(me, shift, count):
+    return me ^ shift if count & (count - 1) == 0 else (me + shift) % count
+
+
+def source(me, shift, count):
+    return me ^ shift if count & (count - 1) == 0 else (me - shift + count) % count
 
 
 def wanted_rows(index_ref, rows):
@@ -27,12 +36,24 @@
     return jnp.where(at == flat, 1.0, 0.0).astype(BF16)
 
 
-def pick_kernel(index_ref, features_ref, out_ref):
-    onehot = wanted_rows(index_ref, features_ref.shape[0])
-    picked = dot(onehot, features_ref[...], 0, 0).astype(BF16)
+def pick_kernel(index_ref, features_ref, vals_ref, cot_ref, out_ref, vals_out, cot_out, index, features, sems):
+    copies = [
+        pltpu.make_async_copy(index_ref, index, sems.at[0]),
+        pltpu.make_async_copy(features_ref, features, sems.at[1]),
+        pltpu.make_async_copy(cot_ref, cot_out, sems.at[2]),
+        pltpu.make_async_copy(vals_ref, vals_out, sems.at[3]),
+    ]
+    for copy in copies:
+        copy.start()
+    copies[0].wait()
+    onehot = wanted_rows(index, features_ref.shape[0])
+    copies[1].wait()
+    picked = dot(onehot, features[...], 0, 0).astype(BF16)
     each = out_ref.shape[1]
     for q in range(out_ref.shape[0]):
         out_ref[q] = picked[q * each : (q + 1) * each]
+    for copy in copies[2:]:
+        copy.wait()
 
 
 def layer_kernel(rep, cols_ref, counts_ref, vals_ref, received_ref, bnd_ref, cot_ref, weight_ref, *refs):
@@ -44,7 +65,7 @@
     tiles, slots = cols_ref.shape
     width = weight_ref.shape[1]
     for shift, block in enumerate(blocks):
-        owner = lax.rem(me - shift + rep, rep)
+        owner = source(me, shift, rep)
         for t in range(tiles):
             panel[owner * tiles + t] = block[t * TILE : (t + 1) * TILE, :]
     groups, each = received_ref.shape[0], received_ref.shape[1]
@@ -80,7 +101,7 @@
     for t in range(tiles):
         own_ref[t * TILE : (t + 1) * TILE, :] = terms[me * tiles + t]
         for shift, send in enumerate(sends, 1):
-            owner = lax.rem(me + shift, rep)
+            owner = target(me, shift, rep)
             send[t * TILE : (t + 1) * TILE, :] = terms[owner * tiles + t].astype(BF16)
     boundary = dot(bnd_ref[...], grad, 0, 0).astype(BF16)
     partial = dot(turned, grad, 0, 0).astype(BF16)
@@ -111,17 +132,26 @@
     params = pltpu.CompilerParams(vmem_limit_bytes=40 * 1024 * 1024)
 
     def shifted(value, shift):
-        return lax.ppermute(value, "rep", [(i, (i + shift) % rep) for i in range(rep)])
+        return lax.ppermute(value, "rep", [(i, target(i, shift, rep)) for i in range(rep)])
 
     blocks = [features] + [shifted(features, shift) for shift in range(1, rep)]
-    outgoing = pl.pallas_call(
+    outgoing, tile_vals, cotangent = pl.pallas_call(
         pick_kernel,
-        out_shape=jax.ShapeDtypeStruct((groups, each, feats), BF16),
-        in_specs=[VMEM] * 2,
-        out_specs=VMEM,
+        out_shape=[
+            jax.ShapeDtypeStruct((groups, each, feats), BF16),
+            jax.ShapeDtypeStruct(tile_vals.shape, BF16),
+            jax.ShapeDtypeStruct(cotangent.shape, BF16),
+        ],
+        in_specs=[HBM] * 4,
+        out_specs=[VMEM] * 3,
+        scratch_shapes=[
+            pltpu.VMEM(send_rows.shape, jnp.int32),
+            pltpu.VMEM((rows, feats), BF16),
+            pltpu.SemaphoreType.DMA((4,)),
+        ],
         compiler_params=params,
         name="pick_rows",
-    )(send_rows, features)
+    )(send_rows, features, tile_vals, cotangent)
     received = lax.all_to_all(outgoing, "dom", split_axis=0, concat_axis=0, tiled=True)
     results = pl.pallas_call(
         functools.partial(layer_kernel, rep),
@@ -144,14 +174,8 @@
     returned = lax.all_to_all(message, "dom", split_axis=0, concat_axis=0, tiled=True)
     arrived = [shifted(send, shift) for shift, send in enumerate(sends, 1)]
     chunk = jnp.sum(returned[:, each:].astype(F32), axis=0).astype(BF16)
-    if rep == 4:
-        one, two, three = [shifted(chunk, shift).astype(F32) for shift in (1, 2, 3)]
-        total = (chunk.astype(F32) + two) + (one + three)
-    else:
-        total = jnp.sum(lax.all_gather(chunk, "rep").astype(F32), axis=0)
-    spread = jnp.broadcast_to(total.astype(BF16)[None], (groups, share, width))
-    grad_weight = lax.all_to_all(spread, "dom", split_axis=0, concat_axis=0, tiled=True)
-    grad_weight = grad_weight.reshape(feats, width).astype(F32)
+    chunks = lax.all_gather(chunk, ("dom", "rep"), axis=0).reshape(groups, rep, share, width)
+    grad_weight = jnp.sum(chunks.astype(F32), axis=1).reshape(feats, width)
     grad_features = pl.pallas_call(
         final_kernel,
         out_shape=jax.ShapeDtypeStruct((rows, feats), BF16),

time: 53.2 us -> 107 us (2.01)
  blocking collectives: 17.3 us -> 81.2 us
  starting transfers between devices: 19.4 us -> 13.5 us
  waiting for transfers between devices: 6.76 us -> 1.73 us
    all_gather x0 -> x1, blocking collectives: none -> 72.3 us  [body(): lax.all_gather(chunk, ('dom', 'rep'), axis=0)]
    all_to_all x1 -> x0, blocking collectives: 8.62 us -> none  [body(): lax.all_to_all(message, 'dom', split_axis=0, concat_axis=0, tiled=True)]
    ppermute x9 -> x6, starting transfers between devices: 15.9 us -> 10.1 us  [shifted(): lax.ppermute(value, 'rep', [(i, target(i, shift, rep)) for i in range(rep)])]
    ppermute x9 -> x6, waiting for transfers between devices: 3.1 us -> 0.02 us  [shifted(): lax.ppermute(value, 'rep', [(i, target(i, shift, rep)) for i in range(rep)])]
    all_to_all x1, waiting for transfers between devices: 3.66 us -> 1.71 us  [body(): lax.all_to_all(message, 'dom', split_axis=0, concat_axis=0, tiled=True)]
    unnamed x20 -> x18, local copies, waits for them, and re-layouts: 3.59 us -> 4.2 us
  transfers between devices with their start and end apart: 10 -> 7, of which waited for: 3 -> 1; matrix products, arithmetic and copies ran while one was open for 1% -> 1% of each run, Pallas kernels for 2% -> 1%
where the time goes in v2:
time: 107 us; the launch traced here: 106 us
  blocking collectives  81.2 us (76%)
  starting transfers between devices  13.5 us (13%)
  Pallas kernels  4.28 us (4%)
  local copies, waits for them, and re-layouts  4.2 us (4%)
  waiting for transfers between devices  1.73 us (2%)
    all_gather x1, blocking collectives, body(): lax.all_gather(chunk, ('dom', 'rep'), axis=0)  72.3 us
    ppermute x6, starting transfers between devices, shifted(): lax.ppermute(value, 'rep', [(i, target(i, shift, rep)) for i in range(rep)])  10.1 us
    all_to_all x1, blocking collectives, body(): lax.all_to_all(outgoing, 'dom', split_axis=0, concat_axis=0, tiled=True)  8.89 us
    unnamed x18, local copies, waits for them, and re-layouts  4.2 us
    all_to_all x1, starting transfers between devices, body(): lax.all_to_all(message, 'dom', split_axis=0, concat_axis=0, tiled=True)  3.39 us
    pallas_call x1, Pallas kernels, body(): pl.pallas_call(functools.partial(layer_kernel, rep), out_shape=[jax.Shape...  2.55 us
  transfers between devices with their start and end apart: 7, of which 1 were waited for; matrix products, arithmetic and copies ran while one was open for 1% of the time, Pallas kernels for 1%

profile of v2, /device:TPU:0, one launch (start us, length us, event | category | flops | bytes accessed | tf_op | source)
XLA Modules:
  0.0 106.4 jit_solution(1321137259743884313)
XLA Ops:
  0.6 4.1 %collective-permute-start.1 = (bf16[256,256]{1,0:T(8,128)(2,1)}, bf16[256,256]{1,0:T(8,128)(2,1)S(1)}, u32[]{:S(2)}, u32[]{:S(2)}) collective-permute-start(bf16[256,256]{1,0:T(8,128)(2,1)} %refs_0_.1), channel_id=1, source_target_pairs={{0,2},{1,3},{2,0},{3,1},{4,6},{5,7},{6,4},{7,5},{8,10},{9,11},{10,... | collective-permute-start | bytes 393224 | tf_op jit(solution)/shard_map/ppermute | solution.py:135
  4.7 1.6 %collective-permute-start = (bf16[256,256]{1,0:T(8,128)(2,1)}, bf16[256,256]{1,0:T(8,128)(2,1)S(1)}, u32[]{:S(2)}, u32[]{:S(2)}) collective-permute-start(bf16[256,256]{1,0:T(8,128)(2,1)} %refs_0_.1), channel_id=1, source_target_pairs={{0,1},{1,0},{2,3},{3,2},{4,5},{5,4},{6,7},{7,6},{8,9},{9,8},{10,11... | collective-permute-start | bytes 393224 | tf_op jit(solution)/shard_map/ppermute | solution.py:135
  6.3 0.0 collective-permute-start.2
  6.3 1.0 copy-done.1
  7.4 0.9 copy-done.2
  8.3 0.9 copy-done.3
  9.2 0.7 copy-done.5
  9.9 0.7 pick_rows.1
  10.5 0.0 copy-start
  10.6 8.9 %all_to_all.10.received_ref = bf16[8,16,256]{2,1,0:T(8,128)(2,1)S(1)} all-to-all(bf16[8,16,256]{2,1,0:T(8,128)(2,1)S(1)} %get-tuple-element.13), channel_id=1, replica_groups=mesh['dom'=8,'rep'=4] {'dom'}, dimensions={0} | all-to-all | bytes 131072 | tf_op jit(solution)/shard_map/all_to_all | solution.py:155
  19.4 0.0 collective-permute-done.1.refs_2_
  19.5 0.0 collective-permute-done.refs_1_
  19.5 0.0 collective-permute-done.2.refs_3_
  19.5 0.0 copy-start.7
  19.5 0.0 copy-start.8
  19.5 0.0 copy-done.4
  19.5 0.0 copy-done
  19.5 0.6 copy-done.7
  20.1 0.0 copy-done.8
  20.1 2.6 %layer.1 = (bf16[256,256]{1,0:T(8,128)(2,1)}, f32[256,256]{1,0:T(8,128)S(1)}, bf16[256,256]{1,0:T(8,128)(2,1)S(1)}, bf16[256,256]{1,0:T(8,128)(2,1)S(1)}, bf16[2...) custom-call(s32[2,8]{1,0:T(2,128)S(1)} %copy-done.7, s32[2]{0:T(128)S(1)} %copy-done.8, ...), custom_call_target="tpu_custom_call" | custom-call | tf_op jit(solution)/shard_map/layer/pallas_call | solution.py:156
  22.7 3.4 %all-to-all-start.1 = ((bf16[8,48,256]{2,1,0:T(8,128)(2,1)}), bf16[8,48,256]{2,1,0:T(8,128)(2,1)S(1)}, u32[]{:S(2)}, u32[]{:S(2)}) async-start(bf16[8,48,256]{2,1,0:T(8,128)(2,1)} %get-tuple-element.16), calls=%async_computation.1 | async-start | bytes 393216 | tf_op jit(solution)/shard_map/all_to_all | solution.py:174
  26.1 0.7 collective-permute-start.3
  26.8 3.5 %collective-permute-start.4 = (bf16[256,256]{1,0:T(8,128)(2,1)S(1)}, bf16[256,256]{1,0:T(8,128)(2,1)S(1)}, u32[]{:S(2)}, u32[]{:S(2)}) collective-permute-start(bf16[256,256]{1,0:T(8,128)(2,1)S(1)} %get-tuple-element.19), channel_id=1, source_target_pairs={{0,2},{1,3},{2,0},{3,1},{4,6},{5,7},{6,4},{7,5},{8,10},{9,11},{10,... | collective-permute-start | bytes 393224 | tf_op jit(solution)/shard_map/ppermute | solution.py:135
  30.3 0.2 collective-permute-start.5
  30.6 1.7 %all-to-all-done.1.returned_ref = bf16[8,48,256]{2,1,0:T(8,128)(2,1)S(1)} async-done(((bf16[8,48,256]{2,1,0:T(8,128)(2,1)}), bf16[8,48,256]{2,1,0:T(8,128)(2,1)S(1)}, u32[]{:S(2)}, u32[]{:S(2)}) %all-to-all-start.1) | async-done | bytes 196640 | tf_op jit(solution)/shard_map/all_to_all | solution.py:174
  32.3 72.3 %all-gather = bf16[1024,256]{1,0:T(8,128)(2,1)S(1)} all-gather(bf16[32,256]{1,0:T(8,128)(2,1)S(1)} %slice_reduce_fusion), channel_id=2, replica_groups=mesh['dom'=8,'rep'=4] {'dom','rep'}, dimensions={0}, use_global_device_ids=true | all-gather | bytes 540672 | tf_op jit(solution)/shard_map/all_gather | solution.py:177
  104.6 0.8 convert_reduce_fusion
  105.4 0.0 collective-permute-done.3.refs_0_
  105.4 0.0 collective-permute-done.4.refs_1_
  105.4 0.0 collective-permute-done.5.refs_2_
  105.4 0.0 copy-done.6
  105.4 1.0 input_gradient.1
  (7 shorter events, 0.0 us)
Async XLA Ops:
  0.6 18.8 %collective-permute-start.1 = (bf16[256,256]{1,0:T(8,128)(2,1)}, bf16[256,256]{1,0:T(8,128)(2,1)S(1)}, u32[]{:S(2)}, u32[]{:S(2)}) collective-permute-start(bf16[256,256]{1,0:T(8,128)(2,1)} %refs_0_.1), channel_id=1, source_target_pairs={{0,2},{1,3},{2,0},{3,1},{4,6},{5,7},{6,4},{7,5},{8,10},{9,11},{10,... | collective-permute-start | bytes 393224 | tf_op jit(solution)/shard_map/ppermute | solution.py:135
  4.7 14.7 %collective-permute-start = (bf16[256,256]{1,0:T(8,128)(2,1)}, bf16[256,256]{1,0:T(8,128)(2,1)S(1)}, u32[]{:S(2)}, u32[]{:S(2)}) collective-permute-start(bf16[256,256]{1,0:T(8,128)(2,1)} %refs_0_.1), channel_id=1, source_target_pairs={{0,1},{1,0},{2,3},{3,2},{4,5},{5,4},{6,7},{7,6},{8,9},{9,8},{10,11... | collective-permute-start | bytes 393224 | tf_op jit(solution)/shard_map/ppermute | solution.py:135
  6.3 13.1 %collective-permute-start.2 = (bf16[256,256]{1,0:T(8,128)(2,1)}, bf16[256,256]{1,0:T(8,128)(2,1)S(1)}, u32[]{:S(2)}, u32[]{:S(2)}) collective-permute-start(bf16[256,256]{1,0:T(8,128)(2,1)} %refs_0_.1), channel_id=1, source_target_pairs={{0,3},{1,2},{2,1},{3,0},{4,7},{5,6},{6,5},{7,4},{8,11},{9,10},{10,... | collective-permute-start | bytes 393224 | tf_op jit(solution)/shard_map/ppermute | solution.py:135
  6.3 1.0 copy-start.1
  7.4 0.9 copy-start.2
  8.3 0.9 copy-start.3
  9.2 0.7 copy-start.5
  9.9 9.6 %copy-start.4 = (bf16[256,128]{1,0:T(8,128)(2,1)S(1)}, bf16[256,128]{1,0:T(8,128)(2,1)}, u32[]{:S(2)}) copy-start(bf16[256,128]{1,0:T(8,128)(2,1)} %bnd_ref.1) | copy-start | bytes 196612
  10.5 8.9 %copy-start = (bf16[256,256]{1,0:T(8,128)(2,1)S(1)}, bf16[256,256]{1,0:T(8,128)(2,1)}, u32[]{:S(2)}) copy-start(bf16[256,256]{1,0:T(8,128)(2,1)} %weight_ref.3) | copy-start | bytes 393220
  19.5 0.7 copy-start.7
  19.5 0.7 copy-start.8
  22.7 9.6 %all-to-all-start.1 = ((bf16[8,48,256]{2,1,0:T(8,128)(2,1)}), bf16[8,48,256]{2,1,0:T(8,128)(2,1)S(1)}, u32[]{:S(2)}, u32[]{:S(2)}) async-start(bf16[8,48,256]{2,1,0:T(8,128)(2,1)} %get-tuple-element.16), calls=%async_computation.1 | async-start | bytes 393216 | tf_op jit(solution)/shard_map/all_to_all | solution.py:174
  26.1 79.3 %collective-permute-start.3 = (bf16[256,256]{1,0:T(8,128)(2,1)S(1)}, bf16[256,256]{1,0:T(8,128)(2,1)S(1)}, u32[]{:S(2)}, u32[]{:S(2)}) collective-permute-start(bf16[256,256]{1,0:T(8,128)(2,1)S(1)} %get-tuple-element.18), channel_id=1, source_target_pairs={{0,1},{1,0},{2,3},{3,2},{4,5},{5,4},{6,7},{7,6},{8,9},{9,8},{10,11... | collective-permute-start | bytes 393224 | tf_op jit(solution)/shard_map/ppermute | solution.py:135
  26.8 78.5 %collective-permute-start.4 = (bf16[256,256]{1,0:T(8,128)(2,1)S(1)}, bf16[256,256]{1,0:T(8,128)(2,1)S(1)}, u32[]{:S(2)}, u32[]{:S(2)}) collective-permute-start(bf16[256,256]{1,0:T(8,128)(2,1)S(1)} %get-tuple-element.19), channel_id=1, source_target_pairs={{0,2},{1,3},{2,0},{3,1},{4,6},{5,7},{6,4},{7,5},{8,10},{9,11},{10,... | collective-permute-start | bytes 393224 | tf_op jit(solution)/shard_map/ppermute | solution.py:135
  30.3 75.1 %collective-permute-start.5 = (bf16[256,256]{1,0:T(8,128)(2,1)S(1)}, bf16[256,256]{1,0:T(8,128)(2,1)S(1)}, u32[]{:S(2)}, u32[]{:S(2)}) collective-permute-start(bf16[256,256]{1,0:T(8,128)(2,1)S(1)} %get-tuple-element.20), channel_id=1, source_target_pairs={{0,3},{1,2},{2,1},{3,0},{4,7},{5,6},{6,5},{7,4},{8,11},{9,10},{10,... | collective-permute-start | bytes 393224 | tf_op jit(solution)/shard_map/ppermute | solution.py:135
  104.6 0.8 copy-start.6

commit v3 on v2

--- a/solution.py
+++ b/solution.py
@@ -27,6 +27,13 @@
 
 def source(me, shift, count):
     return me ^ shift if count & (count - 1) == 0 else (me - shift + count) % count
+
+
+def share_order(q, groups):
+    order = 0
+    for b in range(groups.bit_length() - 1):
+        order = 2 * order + (q >> b & 1)
+    return order
 
 
 def wanted_rows(index_ref, rows):
@@ -108,7 +115,16 @@
     share = partial.shape[0] // groups
     for q in range(groups):
         message_ref[q, :each, :] = boundary[q * each : (q + 1) * each]
-        message_ref[q, each:, :] = partial[q * share : (q + 1) * share]
+        at = share_order(q, groups) * share
+        message_ref[q, each:, :] = partial[at : at + share]
+
+
+def join_kernel(bit, own_ref, got_ref, out_ref):
+    own, got = own_ref[...], got_ref[...]
+    half = own.shape[0]
+    upper = lax.rem(lax.axis_index("dom") // bit, 2) == 1
+    out_ref[:half, :] = jnp.where(upper, got, own).astype(out_ref.dtype)
+    out_ref[half:, :] = jnp.where(upper, own, got).astype(out_ref.dtype)
 
 
 def final_kernel(index_ref, returned_ref, weight_ref, own_ref, *refs):
@@ -129,6 +145,7 @@
     groups, each = send_rows.shape[1], send_rows.shape[2]
     rep = lax.axis_size("rep")
     share = feats // groups
+    bits = [1 << b for b in range(groups.bit_length() - 1)]
     params = pltpu.CompilerParams(vmem_limit_bytes=40 * 1024 * 1024)
 
     def shifted(value, shift):
@@ -151,7 +168,7 @@
         ],
         compiler_params=params,
         name="pick_rows",
-    )(send_rows, features, tile_vals, cotangent)
+    )(*[pltpu.with_memory_space_constraint(x, pltpu.HBM) for x in (send_rows, features, tile_vals, cotangent)])
     received = lax.all_to_all(outgoing, "dom", split_axis=0, concat_axis=0, tiled=True)
     results = pl.pallas_call(
         functools.partial(layer_kernel, rep),
@@ -174,8 +191,24 @@
     returned = lax.all_to_all(message, "dom", split_axis=0, concat_axis=0, tiled=True)
     arrived = [shifted(send, shift) for shift, send in enumerate(sends, 1)]
     chunk = jnp.sum(returned[:, each:].astype(F32), axis=0).astype(BF16)
-    chunks = lax.all_gather(chunk, ("dom", "rep"), axis=0).reshape(groups, rep, share, width)
-    grad_weight = jnp.sum(chunks.astype(F32), axis=1).reshape(feats, width)
+    if rep == 4:
+        one, two, three = [shifted(chunk, shift).astype(F32) for shift in (1, 2, 3)]
+        total = (chunk.astype(F32) + two) + (one + three)
+    else:
+        total = jnp.sum(lax.all_gather(chunk, "rep").astype(F32), axis=0)
+    piece = total.astype(BF16)
+    for bit in reversed(bits):
+        got = lax.ppermute(piece, "dom", [(i, i ^ bit) for i in range(groups)])
+        piece = pl.pallas_call(
+            functools.partial(join_kernel, bit),
+            out_shape=jax.ShapeDtypeStruct((2 * piece.shape[0], width), F32 if bit == 1 else BF16),
+            in_specs=[VMEM] * 2,
+            out_specs=VMEM,
+            compiler_params=params,
+            cost_estimate=pl.CostEstimate(flops=1, bytes_accessed=1, transcendentals=0),
+            name="join",
+        )(piece, got)
+    grad_weight = piece
     grad_features = pl.pallas_call(
         final_kernel,
         out_shape=jax.ShapeDtypeStruct((rows, feats), BF16),

time: 107 us -> 48.8 us (0.46)
  blocking collectives: 81.2 us -> 17.5 us
  waiting for transfers between devices: 1.73 us -> 8.09 us
  local copies, waits for them, and re-layouts: 4.2 us -> 0.66 us
  starting transfers between devices: 13.5 us -> 16.1 us
  Pallas kernels: 4.28 us -> 5.46 us
    all_gather x1 -> x0, blocking collectives: 72.3 us -> none  [body(): lax.all_gather(chunk, ('dom', 'rep'), axis=0)]
    all_to_all x0 -> x1, blocking collectives: none -> 8.62 us  [body(): lax.all_to_all(message, 'dom', split_axis=0, concat_axis=0, tiled=True)]
    ppermute x0 -> x3, waiting for transfers between devices: none -> 6.55 us  [body(): got = lax.ppermute(piece, 'dom', [(i, i ^ bit) for i in range(groups)])]
    ppermute x6 -> x9, starting transfers between devices: 10.1 us -> 14.9 us  [shifted(): lax.ppermute(value, 'rep', [(i, target(i, shift, rep)) for i in range(rep)])]
    unnamed x18 -> x12, local copies, waits for them, and re-layouts: 4.2 us -> 0.66 us
    all_to_all x1 -> x0, starting transfers between devices: 3.39 us -> none  [body(): lax.all_to_all(message, 'dom', split_axis=0, concat_axis=0, tiled=True)]
    all_to_all x1 -> x0, waiting for transfers between devices: 1.71 us -> none  [body(): lax.all_to_all(message, 'dom', split_axis=0, concat_axis=0, tiled=True)]
    ppermute x6 -> x9, waiting for transfers between devices: 0.02 us -> 1.54 us  [shifted(): lax.ppermute(value, 'rep', [(i, target(i, shift, rep)) for i in range(rep)])]
  transfers between devices with their start and end apart: 7 -> 12, of which waited for: 1 -> 4; matrix products, arithmetic and copies ran while one was open for 1% -> 0% of each run, Pallas kernels for 1% -> 5%
where the time goes in v3:
time: 48.8 us; the launch traced here: 48.6 us
  blocking collectives  17.5 us (36%)
  starting transfers between devices  16.1 us (33%)
  waiting for transfers between devices  8.09 us (17%)
  Pallas kernels  5.46 us (11%)
  between operations  0.73 us (1%)
  local copies, waits for them, and re-layouts  0.66 us (1%)
    ppermute x9, starting transfers between devices, shifted(): lax.ppermute(value, 'rep', [(i, target(i, shift, rep)) for i in range(rep)])  14.9 us
    all_to_all x1, blocking collectives, body(): lax.all_to_all(outgoing, 'dom', split_axis=0, concat_axis=0, tiled=True)  8.87 us
    all_to_all x1, blocking collectives, body(): lax.all_to_all(message, 'dom', split_axis=0, concat_axis=0, tiled=True)  8.62 us
    ppermute x3, waiting for transfers between devices, body(): got = lax.ppermute(piece, 'dom', [(i, i ^ bit) for i in range(groups)])  6.55 us
    pallas_call x1, Pallas kernels, body(): pl.pallas_call(functools.partial(layer_kernel, rep), out_shape=[jax.Shape...  2.4 us
    ppermute x9, waiting for transfers between devices, shifted(): lax.ppermute(value, 'rep', [(i, target(i, shift, rep)) for i in range(rep)])  1.54 us
    pallas_call x1, Pallas kernels, body(): pl.pallas_call(pick_kernel, out_shape=[jax.ShapeDtypeStruct((groups, each...  1.28 us
    ppermute x3, starting transfers between devices, body(): got = lax.ppermute(piece, 'dom', [(i, i ^ bit) for i in range(groups)])  1.24 us
  transfers between devices with their start and end apart: 12, of which 4 were waited for; matrix products, arithmetic and copies ran while one was open for 0% of the time, Pallas kernels for 5%

profile of v3, /device:TPU:0, one launch (start us, length us, event | category | flops | bytes accessed | tf_op | source)
XLA Modules:
  0.0 48.6 jit_solution(7639137828254736469)
XLA Ops:
  0.6 4.1 %collective-permute-start.1 = (bf16[256,256]{1,0:T(8,128)(2,1)}, bf16[256,256]{1,0:T(8,128)(2,1)S(1)}, u32[]{:S(2)}, u32[]{:S(2)}) collective-permute-start(bf16[256,256]{1,0:T(8,128)(2,1)} %refs_0_.1), channel_id=1, source_target_pairs={{0,2},{1,3},{2,0},{3,1},{4,6},{5,7},{6,4},{7,5},{8,10},{9,11},{10,... | collective-permute-start | bytes 393224 | tf_op jit(solution)/shard_map/ppermute | solution.py:152
  4.7 1.6 %collective-permute-start = (bf16[256,256]{1,0:T(8,128)(2,1)}, bf16[256,256]{1,0:T(8,128)(2,1)S(1)}, u32[]{:S(2)}, u32[]{:S(2)}) collective-permute-start(bf16[256,256]{1,0:T(8,128)(2,1)} %refs_0_.1), channel_id=1, source_target_pairs={{0,1},{1,0},{2,3},{3,2},{4,5},{5,4},{6,7},{7,6},{8,9},{9,8},{10,11... | collective-permute-start | bytes 393224 | tf_op jit(solution)/shard_map/ppermute | solution.py:152
  6.3 0.0 collective-permute-start.2
  6.3 1.3 %pick_rows.1 = (bf16[8,16,256]{2,1,0:T(8,128)(2,1)S(1)}, bf16[2,8,128,128]{3,2,1,0:T(8,128)(2,1)S(1)}, bf16[256,256]{1,0:T(8,128)(2,1)S(1)}) custom-call(s32[1,8,16]{2,1,0:T(8,128)} %index_ref.3, bf16[256,256]{1,0:T(8,128)(2,1)} %refs_0_.1, bf16[2,8,128,128]{3,2,1,0:T(8,128)(2,1)} %vals_ref.1, bf16[256,256]{1,0:T(8,128)(2,1)} %cot_ref.1), custom_call_target="tpu_custom_call" | custom-call | tf_op jit(solution)/shard_map/pick_rows/pallas_call | solution.py:155
  7.6 0.0 copy-start
  7.6 8.9 %all_to_all.10.received_ref = bf16[8,16,256]{2,1,0:T(8,128)(2,1)S(1)} all-to-all(bf16[8,16,256]{2,1,0:T(8,128)(2,1)S(1)} %get-tuple-element.13), channel_id=1, replica_groups=mesh['dom'=8,'rep'=4] {'dom'}, dimensions={0} | all-to-all | bytes 131072 | tf_op jit(solution)/shard_map/all_to_all | solution.py:172
  16.5 0.0 collective-permute-done.1.refs_2_
  16.5 0.0 collective-permute-done.refs_1_
  16.5 0.0 collective-permute-done.2.refs_3_
  16.5 0.0 copy-start.4
  16.5 0.0 copy-start.5
  16.6 0.6 %copy-done.4 = s32[2,8]{1,0:T(2,128)S(1)} copy-done((s32[2,8]{1,0:T(2,128)S(1)}, s32[2,8]{1,0:T(2,128)}, u32[]{:S(2)}) %copy-start.4) | copy-done | bytes 88
  17.2 2.4 %layer.1 = (bf16[256,256]{1,0:T(8,128)(2,1)}, f32[256,256]{1,0:T(8,128)S(1)}, bf16[256,256]{1,0:T(8,128)(2,1)S(1)}, bf16[256,256]{1,0:T(8,128)(2,1)S(1)}, bf16[2...) custom-call(s32[2,8]{1,0:T(2,128)S(1)} %copy-done.4, s32[2]{0:T(128)S(1)} %copy-done.5, ...), custom_call_target="tpu_custom_call" | custom-call | tf_op jit(solution)/shard_map/layer/pallas_call | solution.py:173
  19.6 8.6 %all_to_all.11.returned_ref = bf16[8,48,256]{2,1,0:T(8,128)(2,1)S(1)} all-to-all(bf16[8,48,256]{2,1,0:T(8,128)(2,1)S(1)} %get-tuple-element.16), channel_id=1, replica_groups=mesh['dom'=8,'rep'=4] {'dom'}, dimensions={0} | all-to-all | bytes 393216 | tf_op jit(solution)/shard_map/all_to_all | solution.py:191
  28.2 3.7 %collective-permute-start.8 = (bf16[32,256]{1,0:T(8,128)(2,1)S(1)}, bf16[32,256]{1,0:T(8,128)(2,1)S(1)}, u32[]{:S(2)}, u32[]{:S(2)}) collective-permute-start(bf16[32,256]{1,0:T(8,128)(2,1)S(1)} %slice_reduce_fusion), channel_id=1, source_target_pairs={{0,3},{1,2},{2,1},{3,0},{4,7},{5,6},{6,5},{7,4},{8,11},{9,10},{10,... | collective-permute-start | bytes 49160 | tf_op jit(solution)/shard_map/ppermute | solution.py:152
  31.9 1.1 %collective-permute-start.7 = (bf16[32,256]{1,0:T(8,128)(2,1)S(1)}, bf16[32,256]{1,0:T(8,128)(2,1)S(1)}, u32[]{:S(2)}, u32[]{:S(2)}) collective-permute-start(bf16[32,256]{1,0:T(8,128)(2,1)S(1)} %slice_reduce_fusion), channel_id=1, source_target_pairs={{0,1},{1,0},{2,3},{3,2},{4,5},{5,4},{6,7},{7,6},{8,9},{9,8},{10,11... | collective-permute-start | bytes 49160 | tf_op jit(solution)/shard_map/ppermute | solution.py:152
  33.0 0.0 collective-permute-start.6
  33.0 1.5 %collective-permute-start.3 = (bf16[256,256]{1,0:T(8,128)(2,1)S(1)}, bf16[256,256]{1,0:T(8,128)(2,1)S(1)}, u32[]{:S(2)}, u32[]{:S(2)}) collective-permute-start(bf16[256,256]{1,0:T(8,128)(2,1)S(1)} %get-tuple-element.18), channel_id=1, source_target_pairs={{0,1},{1,0},{2,3},{3,2},{4,5},{5,4},{6,7},{7,6},{8,9},{9,8},{10,11... | collective-permute-start | bytes 393224 | tf_op jit(solution)/shard_map/ppermute | solution.py:152
  34.5 2.3 %collective-permute-start.4 = (bf16[256,256]{1,0:T(8,128)(2,1)S(1)}, bf16[256,256]{1,0:T(8,128)(2,1)S(1)}, u32[]{:S(2)}, u32[]{:S(2)}) collective-permute-start(bf16[256,256]{1,0:T(8,128)(2,1)S(1)} %get-tuple-element.19), channel_id=1, source_target_pairs={{0,2},{1,3},{2,0},{3,1},{4,6},{5,7},{6,4},{7,5},{8,10},{9,11},{10,... | collective-permute-start | bytes 393224 | tf_op jit(solution)/shard_map/ppermute | solution.py:152
  36.9 0.0 collective-permute-done.8
  36.9 0.6 %collective-permute-start.5 = (bf16[256,256]{1,0:T(8,128)(2,1)S(1)}, bf16[256,256]{1,0:T(8,128)(2,1)S(1)}, u32[]{:S(2)}, u32[]{:S(2)}) collective-permute-start(bf16[256,256]{1,0:T(8,128)(2,1)S(1)} %get-tuple-element.20), channel_id=1, source_target_pairs={{0,3},{1,2},{2,1},{3,0},{4,7},{5,6},{6,5},{7,4},{8,11},{9,10},{10,... | collective-permute-start | bytes 393224 | tf_op jit(solution)/shard_map/ppermute | solution.py:152
  37.4 0.4 collective-permute-done.6
  37.9 0.6 %collective-permute-start.9 = (bf16[32,256]{1,0:T(8,128)(2,1)S(1)}, bf16[32,256]{1,0:T(8,128)(2,1)S(1)}, u32[]{:S(2)}, u32[]{:S(2)}) collective-permute-start(bf16[32,256]{1,0:T(8,128)(2,1)S(1)} %add_convert_fusion.own_ref), channel_id=1, source_target_pairs={{0,16},{4,20},{8,24},{12,28},{16,0},{20,4},{24,8},{28,12},{1,17},{... | collective-permute-start | bytes 49160 | tf_op jit(solution)/shard_map/ppermute | solution.py:201
  38.5 3.2 %collective-permute-done.9.got_ref = bf16[32,256]{1,0:T(8,128)(2,1)S(1)} collective-permute-done((bf16[32,256]{1,0:T(8,128)(2,1)S(1)}, bf16[32,256]{1,0:T(8,128)(2,1)S(1)}, u32[]{:S(2)}, u32[]{:S(2)}) %collective-permute-start.9) | collective-permute-done | bytes 16416 | tf_op jit(solution)/shard_map/ppermute | solution.py:201
  41.7 0.5 %collective-permute-start.10 = (bf16[64,256]{1,0:T(8,128)(2,1)S(1)}, bf16[64,256]{1,0:T(8,128)(2,1)S(1)}, u32[]{:S(2)}, u32[]{:S(2)}) collective-permute-start(bf16[64,256]{1,0:T(8,128)(2,1)S(1)} %join.3.own_ref), channel_id=1, source_target_pairs={{0,8},{4,12},{8,0},{12,4},{16,24},{20,28},{24,16},{28,20},{1,9},{5... | collective-permute-start | bytes 98312 | tf_op jit(solution)/shard_map/ppermute | solution.py:201
  42.2 3.4 %collective-permute-done.10.got_ref = bf16[64,256]{1,0:T(8,128)(2,1)S(1)} collective-permute-done((bf16[64,256]{1,0:T(8,128)(2,1)S(1)}, bf16[64,256]{1,0:T(8,128)(2,1)S(1)}, u32[]{:S(2)}, u32[]{:S(2)}) %collective-permute-start.10) | collective-permute-done | bytes 32800 | tf_op jit(solution)/shard_map/ppermute | solution.py:201
  45.6 0.1 collective-permute-start.11
  45.7 1.1 %collective-permute-done.4.refs_1_ = bf16[256,256]{1,0:T(8,128)(2,1)S(1)} collective-permute-done((bf16[256,256]{1,0:T(8,128)(2,1)S(1)}, bf16[256,256]{1,0:T(8,128)(2,1)S(1)}, u32[]{:S(2)}, u32[]{:S(2)}) %collective-permute-start.4) | collective-permute-done | bytes 131104 | tf_op jit(solution)/shard_map/ppermute | solution.py:152
  46.8 0.0 collective-permute-done.5.refs_2_
  46.8 1.0 %input_gradient.1 = bf16[256,256]{1,0:T(8,128)(2,1)} custom-call(s32[1,8,16]{2,1,0:T(8,128)S(1)} %copy-done.3, bf16[8,48,256]{2,1,0:T(8,128)(2,1)S(1)} %all_to_all.11.returned_ref, bf16[256,256]{1,0:T(8,128)(2,1)S(1)} %copy-done, f32[256,256]{1,0:T(8,128)S(1)} %get-tuple-element.17.own_ref, bf16[256,256]{1,0:T(8,128)(2,1)S(1)} %collective-permute-done.3.refs_0_, ...), custom_call_target="tpu_custom_call" | custom-call | tf_op jit(solution)/shard_map/input_gradient/pallas_call | solution.py:212
  47.9 0.0 collective-permute-done.11.got_ref
  47.9 0.7 %join.5 = f32[256,256]{1,0:T(8,128)} custom-call(bf16[128,256]{1,0:T(8,128)(2,1)S(1)} %join.4.own_ref, bf16[128,256]{1,0:T(8,128)(2,1)S(1)} %collective-permute-done.11.got_ref), custom_call_target="tpu_custom_call" | custom-call | flops 1 | bytes 1 | tf_op jit(solution)/shard_map/join/pallas_call | solution.py:202
  (14 shorter events, 0.1 us)
Async XLA Ops:
  0.6 15.9 %collective-permute-start.1 = (bf16[256,256]{1,0:T(8,128)(2,1)}, bf16[256,256]{1,0:T(8,128)(2,1)S(1)}, u32[]{:S(2)}, u32[]{:S(2)}) collective-permute-start(bf16[256,256]{1,0:T(8,128)(2,1)} %refs_0_.1), channel_id=1, source_target_pairs={{0,2},{1,3},{2,0},{3,1},{4,6},{5,7},{6,4},{7,5},{8,10},{9,11},{10,... | collective-permute-start | bytes 393224 | tf_op jit(solution)/shard_map/ppermute | solution.py:152
  4.7 11.8 %collective-permute-start = (bf16[256,256]{1,0:T(8,128)(2,1)}, bf16[256,256]{1,0:T(8,128)(2,1)S(1)}, u32[]{:S(2)}, u32[]{:S(2)}) collective-permute-start(bf16[256,256]{1,0:T(8,128)(2,1)} %refs_0_.1), channel_id=1, source_target_pairs={{0,1},{1,0},{2,3},{3,2},{4,5},{5,4},{6,7},{7,6},{8,9},{9,8},{10,11... | collective-permute-start | bytes 393224 | tf_op jit(solution)/shard_map/ppermute | solution.py:152
  6.3 10.2 %collective-permute-start.2 = (bf16[256,256]{1,0:T(8,128)(2,1)}, bf16[256,256]{1,0:T(8,128)(2,1)S(1)}, u32[]{:S(2)}, u32[]{:S(2)}) collective-permute-start(bf16[256,256]{1,0:T(8,128)(2,1)} %refs_0_.1), channel_id=1, source_target_pairs={{0,3},{1,2},{2,1},{3,0},{4,7},{5,6},{6,5},{7,4},{8,11},{9,10},{10,... | collective-permute-start | bytes 393224 | tf_op jit(solution)/shard_map/ppermute | solution.py:152
  6.3 10.2 %copy-start.1 = (bf16[256,256]{1,0:T(8,128)(2,1)S(1)}, bf16[256,256]{1,0:T(8,128)(2,1)}, u32[]{:S(2)}) copy-start(bf16[256,256]{1,0:T(8,128)(2,1)} %refs_0_.1) | copy-start | bytes 393220
  6.3 10.2 %copy-start.2 = (bf16[256,128]{1,0:T(8,128)(2,1)S(1)}, bf16[256,128]{1,0:T(8,128)(2,1)}, u32[]{:S(2)}) copy-start(bf16[256,128]{1,0:T(8,128)(2,1)} %bnd_ref.1) | copy-start | bytes 196612
  7.6 8.9 %copy-start = (bf16[256,256]{1,0:T(8,128)(2,1)S(1)}, bf16[256,256]{1,0:T(8,128)(2,1)}, u32[]{:S(2)}) copy-start(bf16[256,256]{1,0:T(8,128)(2,1)} %weight_ref.3) | copy-start | bytes 393220
  16.5 0.7 %copy-start.4 = (s32[2,8]{1,0:T(2,128)S(1)}, s32[2,8]{1,0:T(2,128)}, u32[]{:S(2)}) copy-start(s32[2,8]{1,0:T(2,128)} %cols_ref.1) | copy-start | bytes 196
  16.5 0.7 %copy-start.5 = (s32[2]{0:T(128)S(1)}, s32[2]{0:T(128)}, u32[]{:S(2)}) copy-start(s32[2]{0:T(128)} %counts_ref.1) | copy-start | bytes 28
  28.2 8.6 %collective-permute-start.8 = (bf16[32,256]{1,0:T(8,128)(2,1)S(1)}, bf16[32,256]{1,0:T(8,128)(2,1)S(1)}, u32[]{:S(2)}, u32[]{:S(2)}) collective-permute-start(bf16[32,256]{1,0:T(8,128)(2,1)S(1)} %slice_reduce_fusion), channel_id=1, source_target_pairs={{0,3},{1,2},{2,1},{3,0},{4,7},{5,6},{6,5},{7,4},{8,11},{9,10},{10,... | collective-permute-start | bytes 49160 | tf_op jit(solution)/shard_map/ppermute | solution.py:152
  31.9 5.5 %collective-permute-start.7 = (bf16[32,256]{1,0:T(8,128)(2,1)S(1)}, bf16[32,256]{1,0:T(8,128)(2,1)S(1)}, u32[]{:S(2)}, u32[]{:S(2)}) collective-permute-start(bf16[32,256]{1,0:T(8,128)(2,1)S(1)} %slice_reduce_fusion), channel_id=1, source_target_pairs={{0,1},{1,0},{2,3},{3,2},{4,5},{5,4},{6,7},{7,6},{8,9},{9,8},{10,11... | collective-permute-start | bytes 49160 | tf_op jit(solution)/shard_map/ppermute | solution.py:152
  33.0 4.9 %collective-permute-start.6 = (bf16[32,256]{1,0:T(8,128)(2,1)S(1)}, bf16[32,256]{1,0:T(8,128)(2,1)S(1)}, u32[]{:S(2)}, u32[]{:S(2)}) collective-permute-start(bf16[32,256]{1,0:T(8,128)(2,1)S(1)} %slice_reduce_fusion), channel_id=1, source_target_pairs={{0,2},{1,3},{2,0},{3,1},{4,6},{5,7},{6,4},{7,5},{8,10},{9,11},{10,... | collective-permute-start | bytes 49160 | tf_op jit(solution)/shard_map/ppermute | solution.py:152
  33.0 12.7 %collective-permute-start.3 = (bf16[256,256]{1,0:T(8,128)(2,1)S(1)}, bf16[256,256]{1,0:T(8,128)(2,1)S(1)}, u32[]{:S(2)}, u32[]{:S(2)}) collective-permute-start(bf16[256,256]{1,0:T(8,128)(2,1)S(1)} %get-tuple-element.18), channel_id=1, source_target_pairs={{0,1},{1,0},{2,3},{3,2},{4,5},{5,4},{6,7},{7,6},{8,9},{9,8},{10,11... | collective-permute-start | bytes 393224 | tf_op jit(solution)/shard_map/ppermute | solution.py:152
  34.5 12.3 %collective-permute-start.4 = (bf16[256,256]{1,0:T(8,128)(2,1)S(1)}, bf16[256,256]{1,0:T(8,128)(2,1)S(1)}, u32[]{:S(2)}, u32[]{:S(2)}) collective-permute-start(bf16[256,256]{1,0:T(8,128)(2,1)S(1)} %get-tuple-element.19), channel_id=1, source_target_pairs={{0,2},{1,3},{2,0},{3,1},{4,6},{5,7},{6,4},{7,5},{8,10},{9,11},{10,... | collective-permute-start | bytes 393224 | tf_op jit(solution)/shard_map/ppermute | solution.py:152
  36.9 10.0 %collective-permute-start.5 = (bf16[256,256]{1,0:T(8,128)(2,1)S(1)}, bf16[256,256]{1,0:T(8,128)(2,1)S(1)}, u32[]{:S(2)}, u32[]{:S(2)}) collective-permute-start(bf16[256,256]{1,0:T(8,128)(2,1)S(1)} %get-tuple-element.20), channel_id=1, source_target_pairs={{0,3},{1,2},{2,1},{3,0},{4,7},{5,6},{6,5},{7,4},{8,11},{9,10},{10,... | collective-permute-start | bytes 393224 | tf_op jit(solution)/shard_map/ppermute | solution.py:152
  37.9 3.8 %collective-permute-start.9 = (bf16[32,256]{1,0:T(8,128)(2,1)S(1)}, bf16[32,256]{1,0:T(8,128)(2,1)S(1)}, u32[]{:S(2)}, u32[]{:S(2)}) collective-permute-start(bf16[32,256]{1,0:T(8,128)(2,1)S(1)} %add_convert_fusion.own_ref), channel_id=1, source_target_pairs={{0,16},{4,20},{8,24},{12,28},{16,0},{20,4},{24,8},{28,12},{1,17},{... | collective-permute-start | bytes 49160 | tf_op jit(solution)/shard_map/ppermute | solution.py:201
  41.7 3.9 %collective-permute-start.10 = (bf16[64,256]{1,0:T(8,128)(2,1)S(1)}, bf16[64,256]{1,0:T(8,128)(2,1)S(1)}, u32[]{:S(2)}, u32[]{:S(2)}) collective-permute-start(bf16[64,256]{1,0:T(8,128)(2,1)S(1)} %join.3.own_ref), channel_id=1, source_target_pairs={{0,8},{4,12},{8,0},{12,4},{16,24},{20,28},{24,16},{28,20},{1,9},{5... | collective-permute-start | bytes 98312 | tf_op jit(solution)/shard_map/ppermute | solution.py:201
  45.6 1.2 %copy-start.3 = (s32[1,8,16]{2,1,0:T(8,128)S(1)}, s32[1,8,16]{2,1,0:T(8,128)}, u32[]{:S(2)}) copy-start(s32[1,8,16]{2,1,0:T(8,128)} %index_ref.3) | copy-start | bytes 1540
  45.6 2.2 %collective-permute-start.11 = (bf16[128,256]{1,0:T(8,128)(2,1)S(1)}, bf16[128,256]{1,0:T(8,128)(2,1)S(1)}, u32[]{:S(2)}, u32[]{:S(2)}) collective-permute-start(bf16[128,256]{1,0:T(8,128)(2,1)S(1)} %join.4.own_ref), channel_id=1, source_target_pairs={{0,4},{4,0},{8,12},{12,8},{16,20},{20,16},{24,28},{28,24},{1,5},{5... | collective-permute-start | bytes 196616 | tf_op jit(solution)/shard_map/ppermute | solution.py:201

commit v4 on v3

--- a/solution.py
+++ b/solution.py
@@ -119,6 +119,11 @@
         message_ref[q, each:, :] = partial[at : at + share]
 
 
+def rep_sum_kernel(*refs):
+    chunk, one, two, three = [ref[...].astype(F32) for ref in refs[:4]]
+    refs[-1][...] = ((chunk + two) + (one + three)).astype(BF16)
+
+
 def join_kernel(bit, own_ref, got_ref, out_ref):
     own, got = own_ref[...], got_ref[...]
     half = own.shape[0]
@@ -192,11 +197,17 @@
     arrived = [shifted(send, shift) for shift, send in enumerate(sends, 1)]
     chunk = jnp.sum(returned[:, each:].astype(F32), axis=0).astype(BF16)
     if rep == 4:
-        one, two, three = [shifted(chunk, shift).astype(F32) for shift in (1, 2, 3)]
-        total = (chunk.astype(F32) + two) + (one + three)
+        piece = pl.pallas_call(
+            rep_sum_kernel,
+            out_shape=jax.ShapeDtypeStruct(chunk.shape, BF16),
+            in_specs=[VMEM] * (3 + rep),
+            out_specs=VMEM,
+            compiler_params=params,
+            cost_estimate=pl.CostEstimate(flops=1, bytes_accessed=1, transcendentals=0),
+            name="rep_sum",
+        )(chunk, *[shifted(chunk, shift) for shift in (1, 2, 3)], *arrived)
     else:
-        total = jnp.sum(lax.all_gather(chunk, "rep").astype(F32), axis=0)
-    piece = total.astype(BF16)
+        piece = jnp.sum(lax.all_gather(chunk, "rep").astype(F32), axis=0).astype(BF16)
     for bit in reversed(bits):
         got = lax.ppermute(piece, "dom", [(i, i ^ bit) for i in range(groups)])
         piece = pl.pallas_call(

time: 48.8 us -> 51.6 us (1.057)
  blocking collectives: 17.5 us -> 8.87 us
  starting transfers between devices: 16.1 us -> 21.9 us
  waiting for transfers between devices: 8.09 us -> 12.9 us
  local copies, waits for them, and re-layouts: 0.66 us -> 1.25 us
    all_to_all x1 -> x0, blocking collectives: 8.62 us -> none  [body(): lax.all_to_all(message, 'dom', split_axis=0, concat_axis=0, tiled=True)]
    ppermute x9, waiting for transfers between devices: 1.54 us -> 7.29 us  [shifted(): lax.ppermute(value, 'rep', [(i, target(i, shift, rep)) for i in range(rep)])]
    all_to_all x0 -> x1, starting transfers between devices: none -> 3.39 us  [body(): lax.all_to_all(message, 'dom', split_axis=0, concat_axis=0, tiled=True)]
    ppermute x3, waiting for transfers between devices: 6.55 us -> 4.24 us  [body(): got = lax.ppermute(piece, 'dom', [(i, i ^ bit) for i in range(groups)])]
    ppermute x3, starting transfers between devices: 1.24 us -> 3.55 us  [body(): got = lax.ppermute(piece, 'dom', [(i, i ^ bit) for i in range(groups)])]
    all_to_all x0 -> x1, waiting for transfers between devices: none -> 1.37 us  [body(): lax.all_to_all(message, 'dom', split_axis=0, concat_axis=0, tiled=True)]
    unnamed x12, local copies, waits for them, and re-layouts: 0.66 us -> 1.25 us
  transfers between devices with their start and end apart: 12 -> 13, of which waited for: 4 -> 6; matrix products, arithmetic and copies ran while one was open for 0% -> 0% of each run, Pallas kernels for 5% -> 5%
where the time goes in v4:
time: 51.6 us; the launch traced here: 51.3 us
  starting transfers between devices  21.9 us (42%)
  waiting for transfers between devices  12.9 us (25%)
  blocking collectives  8.87 us (17%)
  Pallas kernels  5.62 us (11%)
  local copies, waits for them, and re-layouts  1.25 us (2%)
  between operations  0.73 us (1%)
    ppermute x9, starting transfers between devices, shifted(): lax.ppermute(value, 'rep', [(i, target(i, shift, rep)) for i in range(rep)])  14.9 us
    all_to_all x1, blocking collectives, body(): lax.all_to_all(outgoing, 'dom', split_axis=0, concat_axis=0, tiled=True)  8.87 us
    ppermute x9, waiting for transfers between devices, shifted(): lax.ppermute(value, 'rep', [(i, target(i, shift, rep)) for i in range(rep)])  7.29 us
    ppermute x3, waiting for transfers between devices, body(): got = lax.ppermute(piece, 'dom', [(i, i ^ bit) for i in range(groups)])  4.24 us
    ppermute x3, starting transfers between devices, body(): got = lax.ppermute(piece, 'dom', [(i, i ^ bit) for i in range(groups)])  3.55 us
    all_to_all x1, starting transfers between devices, body(): lax.all_to_all(message, 'dom', split_axis=0, concat_axis=0, tiled=True)  3.39 us
    pallas_call x1, Pallas kernels, body(): pl.pallas_call(functools.partial(layer_kernel, rep), out_shape=[jax.Shape...  2.55 us
    all_to_all x1, waiting for transfers between devices, body(): lax.all_to_all(message, 'dom', split_axis=0, concat_axis=0, tiled=True)  1.37 us
  transfers between devices with their start and end apart: 13, of which 6 were waited for; matrix products, arithmetic and copies ran while one was open for 0% of the time, Pallas kernels for 5%

profile of v4, /device:TPU:0, one launch (start us, length us, event | category | flops | bytes accessed | tf_op | source)
XLA Modules:
  0.0 51.3 jit_solution(894896321985581738)
XLA Ops:
  0.6 4.1 %collective-permute-start.1 = (bf16[256,256]{1,0:T(8,128)(2,1)}, bf16[256,256]{1,0:T(8,128)(2,1)S(1)}, u32[]{:S(2)}, u32[]{:S(2)}) collective-permute-start(bf16[256,256]{1,0:T(8,128)(2,1)} %refs_0_.1), channel_id=1, source_target_pairs={{0,2},{1,3},{2,0},{3,1},{4,6},{5,7},{6,4},{7,5},{8,10},{9,11},{10,... | collective-permute-start | bytes 393224 | tf_op jit(solution)/shard_map/ppermute | solution.py:157
  4.7 1.6 %collective-permute-start = (bf16[256,256]{1,0:T(8,128)(2,1)}, bf16[256,256]{1,0:T(8,128)(2,1)S(1)}, u32[]{:S(2)}, u32[]{:S(2)}) collective-permute-start(bf16[256,256]{1,0:T(8,128)(2,1)} %refs_0_.1), channel_id=1, source_target_pairs={{0,1},{1,0},{2,3},{3,2},{4,5},{5,4},{6,7},{7,6},{8,9},{9,8},{10,11... | collective-permute-start | bytes 393224 | tf_op jit(solution)/shard_map/ppermute | solution.py:157
  6.3 0.0 collective-permute-start.2
  6.3 1.3 %pick_rows.1 = (bf16[8,16,256]{2,1,0:T(8,128)(2,1)S(1)}, bf16[2,8,128,128]{3,2,1,0:T(8,128)(2,1)S(1)}, bf16[256,256]{1,0:T(8,128)(2,1)S(1)}) custom-call(s32[1,8,16]{2,1,0:T(8,128)} %index_ref.3, bf16[256,256]{1,0:T(8,128)(2,1)} %refs_0_.1, bf16[2,8,128,128]{3,2,1,0:T(8,128)(2,1)} %vals_ref.1, bf16[256,256]{1,0:T(8,128)(2,1)} %cot_ref.1), custom_call_target="tpu_custom_call" | custom-call | tf_op jit(solution)/shard_map/pick_rows/pallas_call | solution.py:160
  7.6 0.0 copy-start
  7.6 8.9 %all_to_all.10.received_ref = bf16[8,16,256]{2,1,0:T(8,128)(2,1)S(1)} all-to-all(bf16[8,16,256]{2,1,0:T(8,128)(2,1)S(1)} %get-tuple-element.13), channel_id=1, replica_groups=mesh['dom'=8,'rep'=4] {'dom'}, dimensions={0} | all-to-all | bytes 131072 | tf_op jit(solution)/shard_map/all_to_all | solution.py:177
  16.5 0.0 collective-permute-done.1.refs_2_
  16.5 0.0 collective-permute-done.refs_1_
  16.5 0.0 copy-start.4
  16.5 0.0 copy-start.5
  16.6 0.6 %copy-done.4 = s32[2,8]{1,0:T(2,128)S(1)} copy-done((s32[2,8]{1,0:T(2,128)S(1)}, s32[2,8]{1,0:T(2,128)}, u32[]{:S(2)}) %copy-start.4) | copy-done | bytes 88
  17.2 2.6 %layer.1 = (bf16[256,256]{1,0:T(8,128)(2,1)}, f32[256,256]{1,0:T(8,128)S(1)}, bf16[256,256]{1,0:T(8,128)(2,1)S(1)}, bf16[256,256]{1,0:T(8,128)(2,1)S(1)}, bf16[2...) custom-call(s32[2,8]{1,0:T(2,128)S(1)} %copy-done.4, s32[2]{0:T(128)S(1)} %copy-done.5, ...), custom_call_target="tpu_custom_call" | custom-call | tf_op jit(solution)/shard_map/layer/pallas_call | solution.py:178
  19.7 3.4 %all-to-all-start.1 = ((bf16[8,48,256]{2,1,0:T(8,128)(2,1)}), bf16[8,48,256]{2,1,0:T(8,128)(2,1)S(1)}, u32[]{:S(2)}, u32[]{:S(2)}) async-start(bf16[8,48,256]{2,1,0:T(8,128)(2,1)} %get-tuple-element.16), calls=%async_computation.1 | async-start | bytes 393216 | tf_op jit(solution)/shard_map/all_to_all | solution.py:196
  23.1 1.5 %collective-permute-start.3 = (bf16[256,256]{1,0:T(8,128)(2,1)S(1)}, bf16[256,256]{1,0:T(8,128)(2,1)S(1)}, u32[]{:S(2)}, u32[]{:S(2)}) collective-permute-start(bf16[256,256]{1,0:T(8,128)(2,1)S(1)} %get-tuple-element.18), channel_id=1, source_target_pairs={{0,1},{1,0},{2,3},{3,2},{4,5},{5,4},{6,7},{7,6},{8,9},{9,8},{10,11... | collective-permute-start | bytes 393224 | tf_op jit(solution)/shard_map/ppermute | solution.py:157
  24.7 2.7 %collective-permute-start.4 = (bf16[256,256]{1,0:T(8,128)(2,1)S(1)}, bf16[256,256]{1,0:T(8,128)(2,1)S(1)}, u32[]{:S(2)}, u32[]{:S(2)}) collective-permute-start(bf16[256,256]{1,0:T(8,128)(2,1)S(1)} %get-tuple-element.19), channel_id=1, source_target_pairs={{0,2},{1,3},{2,0},{3,1},{4,6},{5,7},{6,4},{7,5},{8,10},{9,11},{10,... | collective-permute-start | bytes 393224 | tf_op jit(solution)/shard_map/ppermute | solution.py:157
  27.4 0.6 %collective-permute-start.5 = (bf16[256,256]{1,0:T(8,128)(2,1)S(1)}, bf16[256,256]{1,0:T(8,128)(2,1)S(1)}, u32[]{:S(2)}, u32[]{:S(2)}) collective-permute-start(bf16[256,256]{1,0:T(8,128)(2,1)S(1)} %get-tuple-element.20), channel_id=1, source_target_pairs={{0,3},{1,2},{2,1},{3,0},{4,7},{5,6},{6,5},{7,4},{8,11},{9,10},{10,... | collective-permute-start | bytes 393224 | tf_op jit(solution)/shard_map/ppermute | solution.py:157
  27.9 1.4 %all-to-all-done.1.returned_ref = bf16[8,48,256]{2,1,0:T(8,128)(2,1)S(1)} async-done(((bf16[8,48,256]{2,1,0:T(8,128)(2,1)}), bf16[8,48,256]{2,1,0:T(8,128)(2,1)S(1)}, u32[]{:S(2)}, u32[]{:S(2)}) %all-to-all-start.1) | async-done | bytes 196640 | tf_op jit(solution)/shard_map/all_to_all | solution.py:196
  29.3 3.7 %collective-permute-start.8 = (bf16[32,256]{1,0:T(8,128)(2,1)S(1)}, bf16[32,256]{1,0:T(8,128)(2,1)S(1)}, u32[]{:S(2)}, u32[]{:S(2)}) collective-permute-start(bf16[32,256]{1,0:T(8,128)(2,1)S(1)} %slice_reduce_fusion.refs_0_), channel_id=1, source_target_pairs={{0,3},{1,2},{2,1},{3,0},{4,7},{5,6},{6,5},{7,4},{8,11},{9,10},{10,... | collective-permute-start | bytes 49160 | tf_op jit(solution)/shard_map/ppermute | solution.py:157
  33.0 0.0 collective-permute-done.3.refs_0_.refs_4_
  33.0 0.8 %collective-permute-start.6 = (bf16[32,256]{1,0:T(8,128)(2,1)S(1)}, bf16[32,256]{1,0:T(8,128)(2,1)S(1)}, u32[]{:S(2)}, u32[]{:S(2)}) collective-permute-start(bf16[32,256]{1,0:T(8,128)(2,1)S(1)} %slice_reduce_fusion.refs_0_), channel_id=1, source_target_pairs={{0,1},{1,0},{2,3},{3,2},{4,5},{5,4},{6,7},{7,6},{8,9},{9,8},{10,11... | collective-permute-start | bytes 49160 | tf_op jit(solution)/shard_map/ppermute | solution.py:157
  33.8 4.2 %collective-permute-done.4.refs_1_.refs_5_ = bf16[256,256]{1,0:T(8,128)(2,1)S(1)} collective-permute-done((bf16[256,256]{1,0:T(8,128)(2,1)S(1)}, bf16[256,256]{1,0:T(8,128)(2,1)S(1)}, u32[]{:S(2)}, u32[]{:S(2)}) %collective-permute-start.4) | collective-permute-done | bytes 131104 | tf_op jit(solution)/shard_map/ppermute | solution.py:157
  37.9 0.2 collective-permute-done.8.refs_3_
  38.2 2.9 %collective-permute-done.7.refs_2_ = bf16[32,256]{1,0:T(8,128)(2,1)S(1)} collective-permute-done((bf16[32,256]{1,0:T(8,128)(2,1)S(1)}, bf16[32,256]{1,0:T(8,128)(2,1)S(1)}, u32[]{:S(2)}, u32[]{:S(2)}) %collective-permute-start.7) | collective-permute-done | bytes 16416 | tf_op jit(solution)/shard_map/ppermute | solution.py:157
  41.1 0.0 collective-permute-done.6.refs_1_
  41.1 1.8 %collective-permute-start.9 = (bf16[32,256]{1,0:T(8,128)(2,1)S(1)}, bf16[32,256]{1,0:T(8,128)(2,1)S(1)}, u32[]{:S(2)}, u32[]{:S(2)}) collective-permute-start(bf16[32,256]{1,0:T(8,128)(2,1)S(1)} %rep_sum.1.own_ref), channel_id=1, source_target_pairs={{0,16},{4,20},{8,24},{12,28},{16,0},{20,4},{24,8},{28,12},{1,17},{... | collective-permute-start | bytes 49160 | tf_op jit(solution)/shard_map/ppermute | solution.py:212
  42.8 2.0 %collective-permute-done.9.got_ref = bf16[32,256]{1,0:T(8,128)(2,1)S(1)} collective-permute-done((bf16[32,256]{1,0:T(8,128)(2,1)S(1)}, bf16[32,256]{1,0:T(8,128)(2,1)S(1)}, u32[]{:S(2)}, u32[]{:S(2)}) %collective-permute-start.9) | collective-permute-done | bytes 16416 | tf_op jit(solution)/shard_map/ppermute | solution.py:212
  44.9 1.7 %collective-permute-start.10 = (bf16[64,256]{1,0:T(8,128)(2,1)S(1)}, bf16[64,256]{1,0:T(8,128)(2,1)S(1)}, u32[]{:S(2)}, u32[]{:S(2)}) collective-permute-start(bf16[64,256]{1,0:T(8,128)(2,1)S(1)} %join.3.own_ref), channel_id=1, source_target_pairs={{0,8},{4,12},{8,0},{12,4},{16,24},{20,28},{24,16},{28,20},{1,9},{5... | collective-permute-start | bytes 98312 | tf_op jit(solution)/shard_map/ppermute | solution.py:212
  46.6 2.2 %collective-permute-done.10.got_ref = bf16[64,256]{1,0:T(8,128)(2,1)S(1)} collective-permute-done((bf16[64,256]{1,0:T(8,128)(2,1)S(1)}, bf16[64,256]{1,0:T(8,128)(2,1)S(1)}, u32[]{:S(2)}, u32[]{:S(2)}) %collective-permute-start.10) | collective-permute-done | bytes 32800 | tf_op jit(solution)/shard_map/ppermute | solution.py:212
  48.8 0.1 collective-permute-start.11
  48.9 0.6 %copy-done.3 = s32[1,8,16]{2,1,0:T(8,128)S(1)} copy-done((s32[1,8,16]{2,1,0:T(8,128)S(1)}, s32[1,8,16]{2,1,0:T(8,128)}, u32[]{:S(2)}) %copy-start.3) | copy-done | bytes 536
  49.5 1.0 %input_gradient.1 = bf16[256,256]{1,0:T(8,128)(2,1)} custom-call(s32[1,8,16]{2,1,0:T(8,128)S(1)} %copy-done.3, bf16[8,48,256]{2,1,0:T(8,128)(2,1)S(1)} %all-to-all-done.1.returned_ref, bf16[256,256]{1,0:T(8,128)(2,1)S(1)} %copy-done, f32[256,256]{1,0:T(8,128)S(1)} %get-tuple-element.17.own_ref, bf16[256,256]{1,0:T(8,128)(2,1)S(1)} %collective-permute-done.3.refs_0_.refs_4_, ...), custom_call_target="tpu_custom_call" | custom-call | tf_op jit(solution)/shard_map/input_gradient/pallas_call | solution.py:223
  50.5 0.7 %join.5 = f32[256,256]{1,0:T(8,128)} custom-call(bf16[128,256]{1,0:T(8,128)(2,1)S(1)} %join.4.own_ref, bf16[128,256]{1,0:T(8,128)(2,1)S(1)} %collective-permute-done.11.got_ref), custom_call_target="tpu_custom_call" | custom-call | flops 1 | bytes 1 | tf_op jit(solution)/shard_map/join/pallas_call | solution.py:213
  (15 shorter events, 0.1 us)
Async XLA Ops:
  0.6 15.9 %collective-permute-start.1 = (bf16[256,256]{1,0:T(8,128)(2,1)}, bf16[256,256]{1,0:T(8,128)(2,1)S(1)}, u32[]{:S(2)}, u32[]{:S(2)}) collective-permute-start(bf16[256,256]{1,0:T(8,128)(2,1)} %refs_0_.1), channel_id=1, source_target_pairs={{0,2},{1,3},{2,0},{3,1},{4,6},{5,7},{6,4},{7,5},{8,10},{9,11},{10,... | collective-permute-start | bytes 393224 | tf_op jit(solution)/shard_map/ppermute | solution.py:157
  4.7 11.8 %collective-permute-start = (bf16[256,256]{1,0:T(8,128)(2,1)}, bf16[256,256]{1,0:T(8,128)(2,1)S(1)}, u32[]{:S(2)}, u32[]{:S(2)}) collective-permute-start(bf16[256,256]{1,0:T(8,128)(2,1)} %refs_0_.1), channel_id=1, source_target_pairs={{0,1},{1,0},{2,3},{3,2},{4,5},{5,4},{6,7},{7,6},{8,9},{9,8},{10,11... | collective-permute-start | bytes 393224 | tf_op jit(solution)/shard_map/ppermute | solution.py:157
  6.3 10.2 %collective-permute-start.2 = (bf16[256,256]{1,0:T(8,128)(2,1)}, bf16[256,256]{1,0:T(8,128)(2,1)S(1)}, u32[]{:S(2)}, u32[]{:S(2)}) collective-permute-start(bf16[256,256]{1,0:T(8,128)(2,1)} %refs_0_.1), channel_id=1, source_target_pairs={{0,3},{1,2},{2,1},{3,0},{4,7},{5,6},{6,5},{7,4},{8,11},{9,10},{10,... | collective-permute-start | bytes 393224 | tf_op jit(solution)/shard_map/ppermute | solution.py:157
  6.3 10.2 %copy-start.1 = (bf16[256,256]{1,0:T(8,128)(2,1)S(1)}, bf16[256,256]{1,0:T(8,128)(2,1)}, u32[]{:S(2)}) copy-start(bf16[256,256]{1,0:T(8,128)(2,1)} %refs_0_.1) | copy-start | bytes 393220
  6.3 10.2 %copy-start.2 = (bf16[256,128]{1,0:T(8,128)(2,1)S(1)}, bf16[256,128]{1,0:T(8,128)(2,1)}, u32[]{:S(2)}) copy-start(bf16[256,128]{1,0:T(8,128)(2,1)} %bnd_ref.1) | copy-start | bytes 196612
  7.6 8.9 %copy-start = (bf16[256,256]{1,0:T(8,128)(2,1)S(1)}, bf16[256,256]{1,0:T(8,128)(2,1)}, u32[]{:S(2)}) copy-start(bf16[256,256]{1,0:T(8,128)(2,1)} %weight_ref.3) | copy-start | bytes 393220
  16.5 0.7 %copy-start.4 = (s32[2,8]{1,0:T(2,128)S(1)}, s32[2,8]{1,0:T(2,128)}, u32[]{:S(2)}) copy-start(s32[2,8]{1,0:T(2,128)} %cols_ref.1) | copy-start | bytes 196
  16.5 0.7 %copy-start.5 = (s32[2]{0:T(128)S(1)}, s32[2]{0:T(128)}, u32[]{:S(2)}) copy-start(s32[2]{0:T(128)} %counts_ref.1) | copy-start | bytes 28
  19.7 9.6 %all-to-all-start.1 = ((bf16[8,48,256]{2,1,0:T(8,128)(2,1)}), bf16[8,48,256]{2,1,0:T(8,128)(2,1)S(1)}, u32[]{:S(2)}, u32[]{:S(2)}) async-start(bf16[8,48,256]{2,1,0:T(8,128)(2,1)} %get-tuple-element.16), calls=%async_computation.1 | async-start | bytes 393216 | tf_op jit(solution)/shard_map/all_to_all | solution.py:196
  23.1 9.9 %collective-permute-start.3 = (bf16[256,256]{1,0:T(8,128)(2,1)S(1)}, bf16[256,256]{1,0:T(8,128)(2,1)S(1)}, u32[]{:S(2)}, u32[]{:S(2)}) collective-permute-start(bf16[256,256]{1,0:T(8,128)(2,1)S(1)} %get-tuple-element.18), channel_id=1, source_target_pairs={{0,1},{1,0},{2,3},{3,2},{4,5},{5,4},{6,7},{7,6},{8,9},{9,8},{10,11... | collective-permute-start | bytes 393224 | tf_op jit(solution)/shard_map/ppermute | solution.py:157
  24.7 13.3 %collective-permute-start.4 = (bf16[256,256]{1,0:T(8,128)(2,1)S(1)}, bf16[256,256]{1,0:T(8,128)(2,1)S(1)}, u32[]{:S(2)}, u32[]{:S(2)}) collective-permute-start(bf16[256,256]{1,0:T(8,128)(2,1)S(1)} %get-tuple-element.19), channel_id=1, source_target_pairs={{0,2},{1,3},{2,0},{3,1},{4,6},{5,7},{6,4},{7,5},{8,10},{9,11},{10,... | collective-permute-start | bytes 393224 | tf_op jit(solution)/shard_map/ppermute | solution.py:157
  27.4 10.6 %collective-permute-start.5 = (bf16[256,256]{1,0:T(8,128)(2,1)S(1)}, bf16[256,256]{1,0:T(8,128)(2,1)S(1)}, u32[]{:S(2)}, u32[]{:S(2)}) collective-permute-start(bf16[256,256]{1,0:T(8,128)(2,1)S(1)} %get-tuple-element.20), channel_id=1, source_target_pairs={{0,3},{1,2},{2,1},{3,0},{4,7},{5,6},{6,5},{7,4},{8,11},{9,10},{10,... | collective-permute-start | bytes 393224 | tf_op jit(solution)/shard_map/ppermute | solution.py:157
  29.3 8.9 %collective-permute-start.8 = (bf16[32,256]{1,0:T(8,128)(2,1)S(1)}, bf16[32,256]{1,0:T(8,128)(2,1)S(1)}, u32[]{:S(2)}, u32[]{:S(2)}) collective-permute-start(bf16[32,256]{1,0:T(8,128)(2,1)S(1)} %slice_reduce_fusion.refs_0_), channel_id=1, source_target_pairs={{0,3},{1,2},{2,1},{3,0},{4,7},{5,6},{6,5},{7,4},{8,11},{9,10},{10,... | collective-permute-start | bytes 49160 | tf_op jit(solution)/shard_map/ppermute | solution.py:157
  33.0 8.1 %collective-permute-start.7 = (bf16[32,256]{1,0:T(8,128)(2,1)S(1)}, bf16[32,256]{1,0:T(8,128)(2,1)S(1)}, u32[]{:S(2)}, u32[]{:S(2)}) collective-permute-start(bf16[32,256]{1,0:T(8,128)(2,1)S(1)} %slice_reduce_fusion.refs_0_), channel_id=1, source_target_pairs={{0,2},{1,3},{2,0},{3,1},{4,6},{5,7},{6,4},{7,5},{8,10},{9,11},{10,... | collective-permute-start | bytes 49160 | tf_op jit(solution)/shard_map/ppermute | solution.py:157
  33.0 8.1 %collective-permute-start.6 = (bf16[32,256]{1,0:T(8,128)(2,1)S(1)}, bf16[32,256]{1,0:T(8,128)(2,1)S(1)}, u32[]{:S(2)}, u32[]{:S(2)}) collective-permute-start(bf16[32,256]{1,0:T(8,128)(2,1)S(1)} %slice_reduce_fusion.refs_0_), channel_id=1, source_target_pairs={{0,1},{1,0},{2,3},{3,2},{4,5},{5,4},{6,7},{7,6},{8,9},{9,8},{10,11... | collective-permute-start | bytes 49160 | tf_op jit(solution)/shard_map/ppermute | solution.py:157
  41.1 3.8 %collective-permute-start.9 = (bf16[32,256]{1,0:T(8,128)(2,1)S(1)}, bf16[32,256]{1,0:T(8,128)(2,1)S(1)}, u32[]{:S(2)}, u32[]{:S(2)}) collective-permute-start(bf16[32,256]{1,0:T(8,128)(2,1)S(1)} %rep_sum.1.own_ref), channel_id=1, source_target_pairs={{0,16},{4,20},{8,24},{12,28},{16,0},{20,4},{24,8},{28,12},{1,17},{... | collective-permute-start | bytes 49160 | tf_op jit(solution)/shard_map/ppermute | solution.py:212
  44.9 3.9 %collective-permute-start.10 = (bf16[64,256]{1,0:T(8,128)(2,1)S(1)}, bf16[64,256]{1,0:T(8,128)(2,1)S(1)}, u32[]{:S(2)}, u32[]{:S(2)}) collective-permute-start(bf16[64,256]{1,0:T(8,128)(2,1)S(1)} %join.3.own_ref), channel_id=1, source_target_pairs={{0,8},{4,12},{8,0},{12,4},{16,24},{20,28},{24,16},{28,20},{1,9},{5... | collective-permute-start | bytes 98312 | tf_op jit(solution)/shard_map/ppermute | solution.py:212
  48.8 0.7 %copy-start.3 = (s32[1,8,16]{2,1,0:T(8,128)S(1)}, s32[1,8,16]{2,1,0:T(8,128)}, u32[]{:S(2)}) copy-start(s32[1,8,16]{2,1,0:T(8,128)} %index_ref.3) | copy-start | bytes 1540
  48.8 1.7 %collective-permute-start.11 = (bf16[128,256]{1,0:T(8,128)(2,1)S(1)}, bf16[128,256]{1,0:T(8,128)(2,1)S(1)}, u32[]{:S(2)}, u32[]{:S(2)}) collective-permute-start(bf16[128,256]{1,0:T(8,128)(2,1)S(1)} %join.4.own_ref), channel_id=1, source_target_pairs={{0,4},{4,0},{8,12},{12,8},{16,20},{20,16},{24,28},{28,24},{1,5},{5... | collective-permute-start | bytes 196616 | tf_op jit(solution)/shard_map/ppermute | solution.py:212

commit v5 on v2

--- a/solution.py
+++ b/solution.py
@@ -60,7 +60,7 @@
     blocks = refs[:rep]
     out_ref, own_ref = refs[rep], refs[rep + 1]
     sends = refs[rep + 2 : 2 * rep + 1]
-    message_ref, panel, terms = refs[2 * rep + 1 :]
+    message_ref, partial_ref, panel, terms = refs[2 * rep + 1 :]
     me = lax.axis_index("rep")
     tiles, slots = cols_ref.shape
     width = weight_ref.shape[1]
@@ -104,18 +104,37 @@
             owner = target(me, shift, rep)
             send[t * TILE : (t + 1) * TILE, :] = terms[owner * tiles + t].astype(BF16)
     boundary = dot(bnd_ref[...], grad, 0, 0).astype(BF16)
-    partial = dot(turned, grad, 0, 0).astype(BF16)
-    share = partial.shape[0] // groups
     for q in range(groups):
-        message_ref[q, :each, :] = boundary[q * each : (q + 1) * each]
-        message_ref[q, each:, :] = partial[q * share : (q + 1) * share]
+        message_ref[q] = boundary[q * each : (q + 1) * each]
+    partial = dot(turned, grad, 0, 0)
+    if partial_ref.shape == partial.shape:
+        partial_ref[...] = partial
+    else:
+        count, high, wide = partial_ref.shape
+        across = width // wide
+        for j in range(count):
+            row, column = j // across * high, j % across * wide
+            partial_ref[j] = partial[row : row + high, column : column + wide].astype(BF16)
+
+
+def sum_kernel(parts_ref, returned_ref, out_ref):
+    total = jnp.sum(parts_ref[...].astype(F32), axis=0).astype(BF16)
+    out_ref[...] = jnp.broadcast_to(total[None], out_ref.shape)
+
+
+def spread_kernel(chunks_ref, out_ref):
+    count, high, wide = chunks_ref.shape
+    across = out_ref.shape[1] // wide
+    for j in range(count):
+        row, column = j // across * high, j % across * wide
+        out_ref[row : row + high, column : column + wide] = chunks_ref[j].astype(F32)
 
 
 def final_kernel(index_ref, returned_ref, weight_ref, own_ref, *refs):
     arrived, out_ref = refs[:-1], refs[-1]
     groups, each = index_ref.shape[1], index_ref.shape[2]
     onehot = wanted_rows(index_ref, own_ref.shape[0])
-    returned = jnp.concatenate([returned_ref[q, :each, :] for q in range(groups)], axis=0)
+    returned = jnp.concatenate([returned_ref[q] for q in range(groups)], axis=0)
     total = own_ref[...] + dot(onehot, returned, 1, 0)
     for term in arrived:
         total = total + term[...].astype(F32)
@@ -128,7 +147,13 @@
     tiles, slots = tile_cols.shape
     groups, each = send_rows.shape[1], send_rows.shape[2]
     rep = lax.axis_size("rep")
-    share = feats // groups
+    devices = groups * rep
+    wide = feats * width // (16 * devices)
+    chunked = wide >= TILE and width % wide == 0 and feats % 16 == 0
+    if chunked:
+        partial_shape = jax.ShapeDtypeStruct((devices, 16, wide), BF16)
+    else:
+        partial_shape = jax.ShapeDtypeStruct((feats, width), F32)
     params = pltpu.CompilerParams(vmem_limit_bytes=40 * 1024 * 1024)
 
     def shifted(value, shift):
@@ -151,7 +176,7 @@
         ],
         compiler_params=params,
         name="pick_rows",
-    )(send_rows, features, tile_vals, cotangent)
+    )(*[pltpu.with_memory_space_constraint(x, pltpu.HBM) for x in (send_rows, features, tile_vals, cotangent)])
     received = lax.all_to_all(outgoing, "dom", split_axis=0, concat_axis=0, tiled=True)
     results = pl.pallas_call(
         functools.partial(layer_kernel, rep),
@@ -159,10 +184,11 @@
             jax.ShapeDtypeStruct((rows, width), BF16),
             jax.ShapeDtypeStruct((rows, width), F32),
             *[jax.ShapeDtypeStruct((rows, width), BF16)] * (rep - 1),
-            jax.ShapeDtypeStruct((groups, each + share, width), BF16),
+            jax.ShapeDtypeStruct((groups, each, width), BF16),
+            partial_shape,
         ],
         in_specs=[SMEM] * 2 + [VMEM] * (5 + rep),
-        out_specs=[VMEM] * (rep + 2),
+        out_specs=[VMEM] * (rep + 3),
         scratch_shapes=[
             pltpu.VMEM((rep * tiles, TILE, feats), BF16),
             pltpu.VMEM((rep * tiles, TILE, width), F32),
@@ -170,12 +196,31 @@
         compiler_params=params,
         name="layer",
     )(tile_cols, tile_counts, tile_vals, received, bnd_adj, cotangent, weight, *blocks)
-    output, own, sends, message = results[0], results[1], results[2:-1], results[-1]
+    output, own, sends, message, partial = *results[:2], results[2:-2], *results[-2:]
+    arrived = [shifted(send, shift) for shift, send in enumerate(sends, 1)]
     returned = lax.all_to_all(message, "dom", split_axis=0, concat_axis=0, tiled=True)
-    arrived = [shifted(send, shift) for shift, send in enumerate(sends, 1)]
-    chunk = jnp.sum(returned[:, each:].astype(F32), axis=0).astype(BF16)
-    chunks = lax.all_gather(chunk, ("dom", "rep"), axis=0).reshape(groups, rep, share, width)
-    grad_weight = jnp.sum(chunks.astype(F32), axis=1).reshape(feats, width)
+    if chunked:
+        everyone = ("dom", "rep")
+        parts = lax.all_to_all(partial, everyone, split_axis=0, concat_axis=0, tiled=True)
+        total = pl.pallas_call(
+            sum_kernel,
+            out_shape=partial_shape,
+            in_specs=[VMEM] * 2,
+            out_specs=VMEM,
+            compiler_params=params,
+            name="sum_parts",
+        )(parts, returned)
+        chunks = lax.all_to_all(total, everyone, split_axis=0, concat_axis=0, tiled=True)
+        grad_weight = pl.pallas_call(
+            spread_kernel,
+            out_shape=jax.ShapeDtypeStruct((feats, width), F32),
+            in_specs=[VMEM],
+            out_specs=VMEM,
+            compiler_params=params,
+            name="weight_gradient",
+        )(chunks)
+    else:
+        grad_weight = lax.psum(partial, ("dom", "rep"))
     grad_features = pl.pallas_call(
         final_kernel,
         out_shape=jax.ShapeDtypeStruct((rows, feats), BF16),

time: 107 us -> 60.4 us (0.56)
  blocking collectives: 81.2 us -> 29 us
  waiting for transfers between devices: 1.73 us -> 10.9 us
  local copies, waits for them, and re-layouts: 4.2 us -> 0.66 us
  Pallas kernels: 4.28 us -> 6.15 us
    all_gather x1 -> x0, blocking collectives: 72.3 us -> none  [body(): lax.all_gather(chunk, ('dom', 'rep'), axis=0)]
    all_to_all x0 -> x2, blocking collectives: none -> 20.1 us  [the longest x1 12.7 us: body(): lax.all_to_all(partial, everyone, split_axis=0, concat_axis=0, tiled=True)]
    ppermute x6, waiting for transfers between devices: 0.02 us -> 10.9 us  [shifted(): lax.ppermute(value, 'rep', [(i, target(i, shift, rep)) for i in range(rep)])]
    unnamed x18 -> x12, local copies, waits for them, and re-layouts: 4.2 us -> 0.66 us
    all_to_all x1, waiting for transfers between devices: 1.71 us -> 0.01 us  [body(): lax.all_to_all(total, everyone, split_axis=0, concat_axis=0, tiled=True)]
    pallas_call x0 -> x2, Pallas kernels: none -> 1.42 us  [the longest x1 0.72 us: body(): pl.pallas_call(spread_kernel, out_shape=jax.ShapeDtypeStruct((feats, widt...]
  transfers between devices with their start and end apart: 7 -> 7, of which waited for: 1 -> 2; matrix products, arithmetic and copies ran while one was open for 1% -> 0% of each run, Pallas kernels for 1% -> 4%
where the time goes in v5:
time: 60.4 us; the launch traced here: 60.1 us
  blocking collectives  29 us (48%)
  starting transfers between devices  12.7 us (21%)
  waiting for transfers between devices  10.9 us (18%)
  Pallas kernels  6.15 us (10%)
  between operations  0.72 us (1%)
  local copies, waits for them, and re-layouts  0.66 us (1%)
    all_to_all x1, blocking collectives, body(): lax.all_to_all(partial, everyone, split_axis=0, concat_axis=0, tiled=True)  12.7 us
    ppermute x6, waiting for transfers between devices, shifted(): lax.ppermute(value, 'rep', [(i, target(i, shift, rep)) for i in range(rep)])  10.9 us
    ppermute x6, starting transfers between devices, shifted(): lax.ppermute(value, 'rep', [(i, target(i, shift, rep)) for i in range(rep)])  10.1 us
    all_to_all x1, blocking collectives, body(): lax.all_to_all(outgoing, 'dom', split_axis=0, concat_axis=0, tiled=True)  8.87 us
    all_to_all x1, blocking collectives, body(): lax.all_to_all(message, 'dom', split_axis=0, concat_axis=0, tiled=True)  7.39 us
    all_to_all x1, starting transfers between devices, body(): lax.all_to_all(total, everyone, split_axis=0, concat_axis=0, tiled=True)  2.58 us
    pallas_call x1, Pallas kernels, body(): pl.pallas_call(functools.partial(layer_kernel, rep), out_shape=[jax.Shape...  2.41 us
    pallas_call x1, Pallas kernels, body(): pl.pallas_call(pick_kernel, out_shape=[jax.ShapeDtypeStruct((groups, each...  1.28 us
  transfers between devices with their start and end apart: 7, of which 2 were waited for; matrix products, arithmetic and copies ran while one was open for 0% of the time, Pallas kernels for 4%

profile of v5, /device:TPU:0, one launch (start us, length us, event | category | flops | bytes accessed | tf_op | source)
XLA Modules:
  0.0 60.1 jit_solution(8087834166923215605)
XLA Ops:
  0.6 4.1 %collective-permute-start.1 = (bf16[256,256]{1,0:T(8,128)(2,1)}, bf16[256,256]{1,0:T(8,128)(2,1)S(1)}, u32[]{:S(2)}, u32[]{:S(2)}) collective-permute-start(bf16[256,256]{1,0:T(8,128)(2,1)} %refs_0_.1), channel_id=1, source_target_pairs={{0,2},{1,3},{2,0},{3,1},{4,6},{5,7},{6,4},{7,5},{8,10},{9,11},{10,... | collective-permute-start | bytes 393224 | tf_op jit(solution)/shard_map/ppermute | solution.py:160
  4.7 1.6 %collective-permute-start = (bf16[256,256]{1,0:T(8,128)(2,1)}, bf16[256,256]{1,0:T(8,128)(2,1)S(1)}, u32[]{:S(2)}, u32[]{:S(2)}) collective-permute-start(bf16[256,256]{1,0:T(8,128)(2,1)} %refs_0_.1), channel_id=1, source_target_pairs={{0,1},{1,0},{2,3},{3,2},{4,5},{5,4},{6,7},{7,6},{8,9},{9,8},{10,11... | collective-permute-start | bytes 393224 | tf_op jit(solution)/shard_map/ppermute | solution.py:160
  6.3 0.0 collective-permute-start.2
  6.3 1.3 %pick_rows.1 = (bf16[8,16,256]{2,1,0:T(8,128)(2,1)S(1)}, bf16[2,8,128,128]{3,2,1,0:T(8,128)(2,1)S(1)}, bf16[256,256]{1,0:T(8,128)(2,1)S(1)}) custom-call(s32[1,8,16]{2,1,0:T(8,128)} %index_ref.3, bf16[256,256]{1,0:T(8,128)(2,1)} %refs_0_.1, bf16[2,8,128,128]{3,2,1,0:T(8,128)(2,1)} %vals_ref.1, bf16[256,256]{1,0:T(8,128)(2,1)} %cot_ref.1), custom_call_target="tpu_custom_call" | custom-call | tf_op jit(solution)/shard_map/pick_rows/pallas_call | solution.py:163
  7.6 0.0 copy-start
  7.6 8.9 %all_to_all.20.received_ref = bf16[8,16,256]{2,1,0:T(8,128)(2,1)S(1)} all-to-all(bf16[8,16,256]{2,1,0:T(8,128)(2,1)S(1)} %get-tuple-element.14), channel_id=1, replica_groups=mesh['dom'=8,'rep'=4] {'dom'}, dimensions={0} | all-to-all | bytes 131072 | tf_op jit(solution)/shard_map/all_to_all | solution.py:180
  16.5 0.0 collective-permute-done.1.refs_2_
  16.5 0.0 collective-permute-done.refs_1_
  16.5 0.0 collective-permute-done.2.refs_3_
  16.5 0.0 copy-start.4
  16.5 0.0 copy-start.5
  16.5 0.0 copy-done.1
  16.5 0.0 copy-done.2
  16.5 0.0 copy-done
  16.6 0.6 %copy-done.4 = s32[2,8]{1,0:T(2,128)S(1)} copy-done((s32[2,8]{1,0:T(2,128)S(1)}, s32[2,8]{1,0:T(2,128)}, u32[]{:S(2)}) %copy-start.4) | copy-done | bytes 88
  17.2 0.0 copy-done.5
  17.2 2.4 %layer.1 = (bf16[256,256]{1,0:T(8,128)(2,1)}, f32[256,256]{1,0:T(8,128)S(1)}, bf16[256,256]{1,0:T(8,128)(2,1)S(1)}, bf16[256,256]{1,0:T(8,128)(2,1)S(1)}, bf16[2...) custom-call(s32[2,8]{1,0:T(2,128)S(1)} %copy-done.4, s32[2]{0:T(128)S(1)} %copy-done.5, ...), custom_call_target="tpu_custom_call" | custom-call | tf_op jit(solution)/shard_map/layer/pallas_call | solution.py:181
  19.6 7.4 %all_to_all.21.returned_ref = bf16[8,16,256]{2,1,0:T(8,128)(2,1)S(1)} all-to-all(bf16[8,16,256]{2,1,0:T(8,128)(2,1)S(1)} %get-tuple-element.17), channel_id=1, replica_groups=mesh['dom'=8,'rep'=4] {'dom'}, dimensions={0} | all-to-all | bytes 131072 | tf_op jit(solution)/shard_map/all_to_all | solution.py:201
  27.0 12.7 %all_to_all.22.parts_ref = bf16[32,16,128]{2,1,0:T(8,128)(2,1)S(1)} all-to-all(bf16[32,16,128]{2,1,0:T(8,128)(2,1)S(1)} %get-tuple-element.22), channel_id=1, replica_groups=mesh['dom'=8,'rep'=4] {'dom','rep'}, dimensions={0} | all-to-all | bytes 262144 | tf_op jit(solution)/shard_map/all_to_all | solution.py:204
  39.7 0.7 %sum_parts.1 = bf16[32,16,128]{2,1,0:T(8,128)(2,1)} custom-call(bf16[32,16,128]{2,1,0:T(8,128)(2,1)S(1)} %all_to_all.22.parts_ref, bf16[8,16,256]{2,1,0:T(8,128)(2,1)S(1)} %all_to_all.21.returned_ref), custom_call_target="tpu_custom_call" | custom-call | tf_op jit(solution)/shard_map/sum_parts/pallas_call | solution.py:205
  40.4 2.6 %all-to-all-start.3 = ((bf16[32,16,128]{2,1,0:T(8,128)(2,1)}), bf16[32,16,128]{2,1,0:T(8,128)(2,1)S(1)}, u32[]{:S(2)}, u32[]{:S(2)}) async-start(bf16[32,16,128]{2,1,0:T(8,128)(2,1)} %sum_parts.1), calls=%async_computation.3 | async-start | bytes 262144 | tf_op jit(solution)/shard_map/all_to_all | solution.py:213
  43.0 0.0 copy-start.3
  43.0 1.8 %collective-permute-start.3 = (bf16[256,256]{1,0:T(8,128)(2,1)S(1)}, bf16[256,256]{1,0:T(8,128)(2,1)S(1)}, u32[]{:S(2)}, u32[]{:S(2)}) collective-permute-start(bf16[256,256]{1,0:T(8,128)(2,1)S(1)} %get-tuple-element.19), channel_id=1, source_target_pairs={{0,1},{1,0},{2,3},{3,2},{4,5},{5,4},{6,7},{7,6},{8,9},{9,8},{10,11... | collective-permute-start | bytes 393224 | tf_op jit(solution)/shard_map/ppermute | solution.py:160
  44.7 2.5 %collective-permute-start.4 = (bf16[256,256]{1,0:T(8,128)(2,1)S(1)}, bf16[256,256]{1,0:T(8,128)(2,1)S(1)}, u32[]{:S(2)}, u32[]{:S(2)}) collective-permute-start(bf16[256,256]{1,0:T(8,128)(2,1)S(1)} %get-tuple-element.20), channel_id=1, source_target_pairs={{0,2},{1,3},{2,0},{3,1},{4,6},{5,7},{6,4},{7,5},{8,10},{9,11},{10,... | collective-permute-start | bytes 393224 | tf_op jit(solution)/shard_map/ppermute | solution.py:160
  47.2 0.2 collective-permute-start.5
  47.4 6.0 %collective-permute-done.3.refs_0_ = bf16[256,256]{1,0:T(8,128)(2,1)S(1)} collective-permute-done((bf16[256,256]{1,0:T(8,128)(2,1)S(1)}, bf16[256,256]{1,0:T(8,128)(2,1)S(1)}, u32[]{:S(2)}, u32[]{:S(2)}) %collective-permute-start.3) | collective-permute-done | bytes 131104 | tf_op jit(solution)/shard_map/ppermute | solution.py:160
  53.5 0.0 collective-permute-done.4.refs_1_
  53.5 4.8 %collective-permute-done.5.refs_2_ = bf16[256,256]{1,0:T(8,128)(2,1)S(1)} collective-permute-done((bf16[256,256]{1,0:T(8,128)(2,1)S(1)}, bf16[256,256]{1,0:T(8,128)(2,1)S(1)}, u32[]{:S(2)}, u32[]{:S(2)}) %collective-permute-start.5) | collective-permute-done | bytes 131104 | tf_op jit(solution)/shard_map/ppermute | solution.py:160
  58.3 0.0 copy-done.3
  58.3 1.0 %input_gradient.1 = bf16[256,256]{1,0:T(8,128)(2,1)} custom-call(s32[1,8,16]{2,1,0:T(8,128)S(1)} %copy-done.3, bf16[8,16,256]{2,1,0:T(8,128)(2,1)S(1)} %all_to_all.21.returned_ref, bf16[256,256]{1,0:T(8,128)(2,1)S(1)} %copy-done, f32[256,256]{1,0:T(8,128)S(1)} %get-tuple-element.18.own_ref, bf16[256,256]{1,0:T(8,128)(2,1)S(1)} %collective-permute-done.3.refs_0_, ...), custom_call_target="tpu_custom_call" | custom-call | tf_op jit(solution)/shard_map/input_gradient/pallas_call | solution.py:224
  59.4 0.0 all-to-all-done.3.chunks_ref
  59.4 0.7 %weight_gradient.1 = f32[256,256]{1,0:T(8,128)} custom-call(bf16[32,16,128]{2,1,0:T(8,128)(2,1)S(1)} %all-to-all-done.3.chunks_ref), custom_call_target="tpu_custom_call" | custom-call | tf_op jit(solution)/shard_map/weight_gradient/pallas_call | solution.py:214
  (2 shorter events, 0.0 us)
Async XLA Ops:
  0.6 15.9 %collective-permute-start.1 = (bf16[256,256]{1,0:T(8,128)(2,1)}, bf16[256,256]{1,0:T(8,128)(2,1)S(1)}, u32[]{:S(2)}, u32[]{:S(2)}) collective-permute-start(bf16[256,256]{1,0:T(8,128)(2,1)} %refs_0_.1), channel_id=1, source_target_pairs={{0,2},{1,3},{2,0},{3,1},{4,6},{5,7},{6,4},{7,5},{8,10},{9,11},{10,... | collective-permute-start | bytes 393224 | tf_op jit(solution)/shard_map/ppermute | solution.py:160
  4.7 11.8 %collective-permute-start = (bf16[256,256]{1,0:T(8,128)(2,1)}, bf16[256,256]{1,0:T(8,128)(2,1)S(1)}, u32[]{:S(2)}, u32[]{:S(2)}) collective-permute-start(bf16[256,256]{1,0:T(8,128)(2,1)} %refs_0_.1), channel_id=1, source_target_pairs={{0,1},{1,0},{2,3},{3,2},{4,5},{5,4},{6,7},{7,6},{8,9},{9,8},{10,11... | collective-permute-start | bytes 393224 | tf_op jit(solution)/shard_map/ppermute | solution.py:160
  6.3 10.2 %collective-permute-start.2 = (bf16[256,256]{1,0:T(8,128)(2,1)}, bf16[256,256]{1,0:T(8,128)(2,1)S(1)}, u32[]{:S(2)}, u32[]{:S(2)}) collective-permute-start(bf16[256,256]{1,0:T(8,128)(2,1)} %refs_0_.1), channel_id=1, source_target_pairs={{0,3},{1,2},{2,1},{3,0},{4,7},{5,6},{6,5},{7,4},{8,11},{9,10},{10,... | collective-permute-start | bytes 393224 | tf_op jit(solution)/shard_map/ppermute | solution.py:160
  6.3 10.2 %copy-start.1 = (bf16[256,256]{1,0:T(8,128)(2,1)S(1)}, bf16[256,256]{1,0:T(8,128)(2,1)}, u32[]{:S(2)}) copy-start(bf16[256,256]{1,0:T(8,128)(2,1)} %refs_0_.1) | copy-start | bytes 393220
  6.3 10.2 %copy-start.2 = (bf16[256,128]{1,0:T(8,128)(2,1)S(1)}, bf16[256,128]{1,0:T(8,128)(2,1)}, u32[]{:S(2)}) copy-start(bf16[256,128]{1,0:T(8,128)(2,1)} %bnd_ref.1) | copy-start | bytes 196612
  7.6 8.9 %copy-start = (bf16[256,256]{1,0:T(8,128)(2,1)S(1)}, bf16[256,256]{1,0:T(8,128)(2,1)}, u32[]{:S(2)}) copy-start(bf16[256,256]{1,0:T(8,128)(2,1)} %weight_ref.3) | copy-start | bytes 393220
  16.5 0.7 %copy-start.4 = (s32[2,8]{1,0:T(2,128)S(1)}, s32[2,8]{1,0:T(2,128)}, u32[]{:S(2)}) copy-start(s32[2,8]{1,0:T(2,128)} %cols_ref.1) | copy-start | bytes 196
  16.5 0.7 %copy-start.5 = (s32[2]{0:T(128)S(1)}, s32[2]{0:T(128)}, u32[]{:S(2)}) copy-start(s32[2]{0:T(128)} %counts_ref.1) | copy-start | bytes 28
  40.4 19.0 %all-to-all-start.3 = ((bf16[32,16,128]{2,1,0:T(8,128)(2,1)}), bf16[32,16,128]{2,1,0:T(8,128)(2,1)S(1)}, u32[]{:S(2)}, u32[]{:S(2)}) async-start(bf16[32,16,128]{2,1,0:T(8,128)(2,1)} %sum_parts.1), calls=%async_computation.3 | async-start | bytes 262144 | tf_op jit(solution)/shard_map/all_to_all | solution.py:213
  43.0 15.4 %copy-start.3 = (s32[1,8,16]{2,1,0:T(8,128)S(1)}, s32[1,8,16]{2,1,0:T(8,128)}, u32[]{:S(2)}) copy-start(s32[1,8,16]{2,1,0:T(8,128)} %index_ref.3) | copy-start | bytes 1540
  43.0 10.5 %collective-permute-start.3 = (bf16[256,256]{1,0:T(8,128)(2,1)S(1)}, bf16[256,256]{1,0:T(8,128)(2,1)S(1)}, u32[]{:S(2)}, u32[]{:S(2)}) collective-permute-start(bf16[256,256]{1,0:T(8,128)(2,1)S(1)} %get-tuple-element.19), channel_id=1, source_target_pairs={{0,1},{1,0},{2,3},{3,2},{4,5},{5,4},{6,7},{7,6},{8,9},{9,8},{10,11... | collective-permute-start | bytes 393224 | tf_op jit(solution)/shard_map/ppermute | solution.py:160
  44.7 8.7 %collective-permute-start.4 = (bf16[256,256]{1,0:T(8,128)(2,1)S(1)}, bf16[256,256]{1,0:T(8,128)(2,1)S(1)}, u32[]{:S(2)}, u32[]{:S(2)}) collective-permute-start(bf16[256,256]{1,0:T(8,128)(2,1)S(1)} %get-tuple-element.20), channel_id=1, source_target_pairs={{0,2},{1,3},{2,0},{3,1},{4,6},{5,7},{6,4},{7,5},{8,10},{9,11},{10,... | collective-permute-start | bytes 393224 | tf_op jit(solution)/shard_map/ppermute | solution.py:160
  47.2 11.1 %collective-permute-start.5 = (bf16[256,256]{1,0:T(8,128)(2,1)S(1)}, bf16[256,256]{1,0:T(8,128)(2,1)S(1)}, u32[]{:S(2)}, u32[]{:S(2)}) collective-permute-start(bf16[256,256]{1,0:T(8,128)(2,1)S(1)} %get-tuple-element.21), channel_id=1, source_target_pairs={{0,3},{1,2},{2,1},{3,0},{4,7},{5,6},{6,5},{7,4},{8,11},{9,10},{10,... | collective-permute-start | bytes 393224 | tf_op jit(solution)/shard_map/ppermute | solution.py:160

commit v6 on v5

--- a/solution.py
+++ b/solution.py
@@ -29,14 +29,13 @@
     return me ^ shift if count & (count - 1) == 0 else (me - shift + count) % count
 
 
-def wanted_rows(index_ref, rows):
-    groups = index_ref.shape[1]
-    flat = jnp.concatenate([index_ref[0, q : q + 1, :] for q in range(groups)], axis=1)
+def wanted_rows(index_ref, rows, order):
+    flat = jnp.concatenate([index_ref[0, pl.ds(q, 1), :] for q in order], axis=1)
     at = lax.broadcasted_iota(jnp.int32, (rows, flat.shape[1]), 0)
     return jnp.where(at == flat, 1.0, 0.0).astype(BF16)
 
 
-def pick_kernel(index_ref, features_ref, vals_ref, cot_ref, out_ref, vals_out, cot_out, index, features, sems):
+def pick_kernel(index_ref, features_ref, vals_ref, cot_ref, send_ref, keep_ref, vals_out, cot_out, index, features, sems):
     copies = [
         pltpu.make_async_copy(index_ref, index, sems.at[0]),
         pltpu.make_async_copy(features_ref, features, sems.at[1]),
@@ -46,21 +45,33 @@
     for copy in copies:
         copy.start()
     copies[0].wait()
-    onehot = wanted_rows(index, features_ref.shape[0])
+    me = lax.axis_index("dom")
+    groups = index_ref.shape[1]
+    onehot = wanted_rows(index, features_ref.shape[0], [me ^ s for s in range(groups)])
     copies[1].wait()
     picked = dot(onehot, features[...], 0, 0).astype(BF16)
-    each = out_ref.shape[1]
-    for q in range(out_ref.shape[0]):
-        out_ref[q] = picked[q * each : (q + 1) * each]
+    each = keep_ref.shape[1]
+    for s in range(groups):
+        (send_ref if s % 2 else keep_ref)[s // 2] = picked[s * each : (s + 1) * each]
     for copy in copies[2:]:
         copy.wait()
 
 
-def layer_kernel(rep, cols_ref, counts_ref, vals_ref, received_ref, bnd_ref, cot_ref, weight_ref, *refs):
+def stage_kernel(keep_ref, got_ref, *refs):
+    next_send_ref, next_keep_ref = refs[-2:]
+    rows = keep_ref.shape[1]
+    for j in range(keep_ref.shape[0]):
+        to_ref = (next_send_ref if j % 2 else next_keep_ref).at[j // 2]
+        to_ref[:rows, :] = keep_ref[j]
+        to_ref[rows:, :] = got_ref[j]
+
+
+def layer_kernel(rep, cols_ref, counts_ref, vals_ref, kept_ref, came_ref, bnd_ref, cot_ref, weight_ref, *refs):
     blocks = refs[:rep]
     out_ref, own_ref = refs[rep], refs[rep + 1]
     sends = refs[rep + 2 : 2 * rep + 1]
-    message_ref, partial_ref, panel, terms = refs[2 * rep + 1 :]
+    bnd_send_ref, bnd_keep_ref, partial_ref, panel, terms, received, boundary = refs[2 * rep + 1 :]
+    here = lax.axis_index("dom")
     me = lax.axis_index("rep")
     tiles, slots = cols_ref.shape
     width = weight_ref.shape[1]
@@ -68,8 +79,11 @@
         owner = source(me, shift, rep)
         for t in range(tiles):
             panel[owner * tiles + t] = block[t * TILE : (t + 1) * TILE, :]
-    groups, each = received_ref.shape[0], received_ref.shape[1]
-    received = jnp.concatenate([received_ref[q] for q in range(groups)], axis=0)
+    each = bnd_keep_ref.shape[1]
+    groups = received.shape[0] // each
+    for o in range(groups):
+        side, at = (kept_ref, o) if o < groups // 2 else (came_ref, o - groups // 2)
+        received[pl.ds(pl.multiple_of((here ^ o) * each, each), each), :] = side[0, at * each : (at + 1) * each, :]
     adjacency = []
     forward = []
     backward = []
@@ -83,7 +97,7 @@
         adjacency.append(stacked)
         forward.append(dot(jnp.concatenate(live, axis=1), chosen, 1, 0))
         backward.append(dot(stacked, chosen, 0, 0))
-    outside = dot(bnd_ref[...], received, 1, 0)
+    outside = dot(bnd_ref[...], received[...], 1, 0)
     mixed = jnp.concatenate(forward, axis=0) + outside
     turned = (jnp.concatenate(backward, axis=0) + outside).astype(BF16)
     high = mixed.astype(BF16)
@@ -103,9 +117,10 @@
         for shift, send in enumerate(sends, 1):
             owner = target(me, shift, rep)
             send[t * TILE : (t + 1) * TILE, :] = terms[owner * tiles + t].astype(BF16)
-    boundary = dot(bnd_ref[...], grad, 0, 0).astype(BF16)
-    for q in range(groups):
-        message_ref[q] = boundary[q * each : (q + 1) * each]
+    boundary[...] = dot(bnd_ref[...], grad, 0, 0).astype(BF16)
+    for s in range(groups):
+        at = pl.multiple_of((here ^ s) * each, each)
+        (bnd_send_ref if s % 2 else bnd_keep_ref)[s // 2] = boundary[pl.ds(at, each), :]
     partial = dot(turned, grad, 0, 0)
     if partial_ref.shape == partial.shape:
         partial_ref[...] = partial
@@ -117,7 +132,7 @@
             partial_ref[j] = partial[row : row + high, column : column + wide].astype(BF16)
 
 
-def sum_kernel(parts_ref, returned_ref, out_ref):
+def sum_kernel(parts_ref, out_ref):
     total = jnp.sum(parts_ref[...].astype(F32), axis=0).astype(BF16)
     out_ref[...] = jnp.broadcast_to(total[None], out_ref.shape)
 
@@ -130,11 +145,11 @@
         out_ref[row : row + high, column : column + wide] = chunks_ref[j].astype(F32)
 
 
-def final_kernel(index_ref, returned_ref, weight_ref, own_ref, *refs):
+def final_kernel(index_ref, kept_ref, came_ref, weight_ref, own_ref, *refs):
     arrived, out_ref = refs[:-1], refs[-1]
-    groups, each = index_ref.shape[1], index_ref.shape[2]
-    onehot = wanted_rows(index_ref, own_ref.shape[0])
-    returned = jnp.concatenate([returned_ref[q] for q in range(groups)], axis=0)
+    here = lax.axis_index("dom")
+    onehot = wanted_rows(index_ref, own_ref.shape[0], [here ^ o for o in range(index_ref.shape[1])])
+    returned = jnp.concatenate([kept_ref[0], came_ref[0]], axis=0)
     total = own_ref[...] + dot(onehot, returned, 1, 0)
     for term in arrived:
         total = total + term[...].astype(F32)
@@ -159,16 +174,33 @@
     def shifted(value, shift):
         return lax.ppermute(value, "rep", [(i, target(i, shift, rep)) for i in range(rep)])
 
+    def exchange(send, keep, after=(), flops=1):
+        for b in range(groups.bit_length() - 1):
+            came = lax.ppermute(send, "dom", [(i, i ^ 1 << b) for i in range(groups)])
+            parts, high = keep.shape[0], keep.shape[1]
+            if parts == 1:
+                return keep, came
+            send, keep = pl.pallas_call(
+                stage_kernel,
+                out_shape=[jax.ShapeDtypeStruct((parts // 2, 2 * high, keep.shape[2]), BF16)] * 2,
+                in_specs=[VMEM] * (2 + len(after)),
+                out_specs=[VMEM] * 2,
+                compiler_params=params,
+                cost_estimate=pl.CostEstimate(flops=flops, bytes_accessed=1, transcendentals=0),
+                name="exchange_step",
+            )(keep, came, *after)
+            after = ()
+
     blocks = [features] + [shifted(features, shift) for shift in range(1, rep)]
-    outgoing, tile_vals, cotangent = pl.pallas_call(
+    send, keep, tile_vals, cotangent = pl.pallas_call(
         pick_kernel,
         out_shape=[
-            jax.ShapeDtypeStruct((groups, each, feats), BF16),
+            *[jax.ShapeDtypeStruct((groups // 2, each, feats), BF16)] * 2,
             jax.ShapeDtypeStruct(tile_vals.shape, BF16),
             jax.ShapeDtypeStruct(cotangent.shape, BF16),
         ],
         in_specs=[HBM] * 4,
-        out_specs=[VMEM] * 3,
+        out_specs=[VMEM] * 4,
         scratch_shapes=[
             pltpu.VMEM(send_rows.shape, jnp.int32),
             pltpu.VMEM((rows, feats), BF16),
@@ -177,39 +209,40 @@
         compiler_params=params,
         name="pick_rows",
     )(*[pltpu.with_memory_space_constraint(x, pltpu.HBM) for x in (send_rows, features, tile_vals, cotangent)])
-    received = lax.all_to_all(outgoing, "dom", split_axis=0, concat_axis=0, tiled=True)
+    received = exchange(send, keep)
     results = pl.pallas_call(
         functools.partial(layer_kernel, rep),
         out_shape=[
             jax.ShapeDtypeStruct((rows, width), BF16),
             jax.ShapeDtypeStruct((rows, width), F32),
             *[jax.ShapeDtypeStruct((rows, width), BF16)] * (rep - 1),
-            jax.ShapeDtypeStruct((groups, each, width), BF16),
+            *[jax.ShapeDtypeStruct((groups // 2, each, width), BF16)] * 2,
             partial_shape,
         ],
-        in_specs=[SMEM] * 2 + [VMEM] * (5 + rep),
-        out_specs=[VMEM] * (rep + 3),
+        in_specs=[SMEM] * 2 + [VMEM] * (6 + rep),
+        out_specs=[VMEM] * (rep + 4),
         scratch_shapes=[
             pltpu.VMEM((rep * tiles, TILE, feats), BF16),
             pltpu.VMEM((rep * tiles, TILE, width), F32),
+            pltpu.VMEM((groups * each, feats), BF16),
+            pltpu.VMEM((groups * each, width), BF16),
         ],
         compiler_params=params,
         name="layer",
-    )(tile_cols, tile_counts, tile_vals, received, bnd_adj, cotangent, weight, *blocks)
-    output, own, sends, message, partial = *results[:2], results[2:-2], *results[-2:]
+    )(tile_cols, tile_counts, tile_vals, *received, bnd_adj, cotangent, weight, *blocks)
+    output, own, sends, send, keep, partial = *results[:2], results[2:-3], *results[-3:]
     arrived = [shifted(send, shift) for shift, send in enumerate(sends, 1)]
-    returned = lax.all_to_all(message, "dom", split_axis=0, concat_axis=0, tiled=True)
     if chunked:
         everyone = ("dom", "rep")
         parts = lax.all_to_all(partial, everyone, split_axis=0, concat_axis=0, tiled=True)
         total = pl.pallas_call(
             sum_kernel,
             out_shape=partial_shape,
-            in_specs=[VMEM] * 2,
+            in_specs=[VMEM],
             out_specs=VMEM,
             compiler_params=params,
             name="sum_parts",
-        )(parts, returned)
+        )(parts)
         chunks = lax.all_to_all(total, everyone, split_axis=0, concat_axis=0, tiled=True)
         grad_weight = pl.pallas_call(
             spread_kernel,
@@ -220,15 +253,18 @@
             name="weight_gradient",
         )(chunks)
     else:
+        total = None
         grad_weight = lax.psum(partial, ("dom", "rep"))
+    returned = exchange(send, keep, () if total is None else (total,))
     grad_features = pl.pallas_call(
         final_kernel,
         out_shape=jax.ShapeDtypeStruct((rows, feats), BF16),
-        in_specs=[VMEM] * (3 + rep),
+        in_specs=[VMEM] * (4 + rep),
         out_specs=VMEM,
         compiler_params=params,
+        cost_estimate=pl.CostEstimate(flops=1_800_000_000, bytes_accessed=1, transcendentals=0),
         name="input_gradient",
-    )(send_rows, returned, weight, own, *arrived)
+    )(send_rows, *returned, weight, own, *arrived)
     return (output, grad_features, grad_weight)
 
 

time: 60.4 us -> 49.2 us (0.81)
  blocking collectives: 29 us -> 0 us
  starting transfers between devices: 12.7 us -> 25.6 us
  waiting for transfers between devices: 10.9 us -> 14.8 us
  Pallas kernels: 6.15 us -> 7.22 us
    all_to_all x3 -> x0, blocking collectives: 29 us -> none  [the longest x1 12.7 us: body(): lax.all_to_all(partial, everyone, split_axis=0, concat_axis=0, tiled=True)]
    ppermute x6, waiting for transfers between devices: 10.9 us -> 0.02 us  [shifted(): lax.ppermute(value, 'rep', [(i, target(i, shift, rep)) for i in range(rep)])]
    ppermute x0 -> x6, waiting for transfers between devices: none -> 10.6 us  [exchange(): came = lax.ppermute(send, 'dom', [(i, i ^ 1 << b) for i in range(groups)])]
    ppermute x0 -> x6, starting transfers between devices: none -> 6.78 us  [exchange(): came = lax.ppermute(send, 'dom', [(i, i ^ 1 << b) for i in range(groups)])]
    all_to_all x0 -> x1, starting transfers between devices: none -> 6.07 us  [body(): lax.all_to_all(partial, everyone, split_axis=0, concat_axis=0, tiled=True)]
    all_to_all x0 -> x1, waiting for transfers between devices: none -> 4.17 us  [body(): lax.all_to_all(partial, everyone, split_axis=0, concat_axis=0, tiled=True)]
    pallas_call x2 -> x6, Pallas kernels: 1.97 us -> 2.92 us  [the longest x1 1.26 us: body(): pl.pallas_call(pick_kernel, out_shape=[*[jax.ShapeDtypeStruct((groups //...]
  transfers between devices with their start and end apart: 7 -> 14, of which waited for: 2 -> 6; matrix products, arithmetic and copies ran while one was open for 0% -> 0% of each run, Pallas kernels for 4% -> 8%
where the time goes in v6:
time: 49.2 us; the launch traced here: 49 us
  starting transfers between devices  25.6 us (52%)
  waiting for transfers between devices  14.8 us (30%)
  Pallas kernels  7.22 us (15%)
  between operations  0.75 us (2%)
  local copies, waits for them, and re-layouts  0.66 us (1%)
    ppermute x6, waiting for transfers between devices, exchange(): came = lax.ppermute(send, 'dom', [(i, i ^ 1 << b) for i in range(groups)])  10.6 us
    ppermute x6, starting transfers between devices, shifted(): lax.ppermute(value, 'rep', [(i, target(i, shift, rep)) for i in range(rep)])  10.1 us
    ppermute x6, starting transfers between devices, exchange(): came = lax.ppermute(send, 'dom', [(i, i ^ 1 << b) for i in range(groups)])  6.78 us
    all_to_all x1, starting transfers between devices, body(): lax.all_to_all(partial, everyone, split_axis=0, concat_axis=0, tiled=True)  6.07 us
    all_to_all x1, waiting for transfers between devices, body(): lax.all_to_all(partial, everyone, split_axis=0, concat_axis=0, tiled=True)  4.17 us
    all_to_all x1, starting transfers between devices, body(): lax.all_to_all(total, everyone, split_axis=0, concat_axis=0, tiled=True)  2.58 us
    pallas_call x1, Pallas kernels, body(): pl.pallas_call(functools.partial(layer_kernel, rep), out_shape=[jax.Shape...  2.54 us
    pallas_call x1, Pallas kernels, body(): pl.pallas_call(pick_kernel, out_shape=[*[jax.ShapeDtypeStruct((groups //...  1.26 us
  transfers between devices with their start and end apart: 14, of which 6 were waited for; matrix products, arithmetic and copies ran while one was open for 0% of the time, Pallas kernels for 8%

profile of v6, /device:TPU:0, one launch (start us, length us, event | category | flops | bytes accessed | tf_op | source)
XLA Modules:
  0.0 49.0 jit_solution(16909226317871866334)
XLA Ops:
  0.6 4.1 %collective-permute-start.4 = (bf16[256,256]{1,0:T(8,128)(2,1)}, bf16[256,256]{1,0:T(8,128)(2,1)S(1)}, u32[]{:S(2)}, u32[]{:S(2)}) collective-permute-start(bf16[256,256]{1,0:T(8,128)(2,1)} %refs_0_.1), channel_id=1, source_target_pairs={{0,2},{1,3},{2,0},{3,1},{4,6},{5,7},{6,4},{7,5},{8,10},{9,11},{10,... | collective-permute-start | bytes 393224 | tf_op jit(solution)/shard_map/ppermute | solution.py:175
  4.7 1.6 %collective-permute-start.3 = (bf16[256,256]{1,0:T(8,128)(2,1)}, bf16[256,256]{1,0:T(8,128)(2,1)S(1)}, u32[]{:S(2)}, u32[]{:S(2)}) collective-permute-start(bf16[256,256]{1,0:T(8,128)(2,1)} %refs_0_.1), channel_id=1, source_target_pairs={{0,1},{1,0},{2,3},{3,2},{4,5},{5,4},{6,7},{7,6},{8,9},{9,8},{10,11... | collective-permute-start | bytes 393224 | tf_op jit(solution)/shard_map/ppermute | solution.py:175
  6.3 0.0 collective-permute-start.5
  6.3 1.3 %pick_rows.1 = (bf16[4,16,256]{2,1,0:T(8,128)(2,1)S(1)}, bf16[4,16,256]{2,1,0:T(8,128)(2,1)S(1)}, bf16[2,8,128,128]{3,2,1,0:T(8,128)(2,1)S(1)}, bf16[256,256]{1,0:T(8,128)(2,1)S(1)}) custom-call(s32[1,8,16]{2,1,0:T(8,128)} %index_ref.3, bf16[256,256]{1,0:T(8,128)(2,1)} %refs_0_.1, bf16[2,8,128,128]{3,2,1,0:T(8,128)(2,1)} %vals_ref.1, bf16[256,256]{1,0:T(8,128)(2,1)} %cot_ref.1), custom_call_target="tpu_custom_call" | custom-call | tf_op jit(solution)/shard_map/pick_rows/pallas_call | solution.py:195
  7.6 0.0 copy-start
  7.6 0.1 collective-permute-start
  7.7 1.2 %collective-permute-done.got_ref = bf16[4,16,256]{2,1,0:T(8,128)(2,1)S(1)} collective-permute-done((bf16[4,16,256]{2,1,0:T(8,128)(2,1)S(1)}, bf16[4,16,256]{2,1,0:T(8,128)(2,1)S(1)}, u32[]{:S(2)}, u32[]{:S(2)}) %collective-permute-start) | collective-permute-done | bytes 32800 | tf_op jit(solution)/shard_map/ppermute | solution.py:179
  8.9 1.7 %collective-permute-start.1 = (bf16[2,32,256]{2,1,0:T(8,128)(2,1)S(1)}, bf16[2,32,256]{2,1,0:T(8,128)(2,1)S(1)}, u32[]{:S(2)}, u32[]{:S(2)}) collective-permute-start(bf16[2,32,256]{2,1,0:T(8,128)(2,1)S(1)} %get-tuple-element.27), channel_id=1, source_target_pairs={{0,8},{4,12},{8,0},{12,4},{16,24},{20,28},{24,16},{28,20},{1,9},{5... | collective-permute-start | bytes 98312 | tf_op jit(solution)/shard_map/ppermute | solution.py:179
  10.6 2.2 %collective-permute-done.1.got_ref = bf16[2,32,256]{2,1,0:T(8,128)(2,1)S(1)} collective-permute-done((bf16[2,32,256]{2,1,0:T(8,128)(2,1)S(1)}, bf16[2,32,256]{2,1,0:T(8,128)(2,1)S(1)}, u32[]{:S(2)}, u32[]{:S(2)}) %collective-permute-start.1) | collective-permute-done | bytes 32800 | tf_op jit(solution)/shard_map/ppermute | solution.py:179
  12.8 1.7 %collective-permute-start.2 = (bf16[1,64,256]{2,1,0:T(8,128)(2,1)S(1)}, bf16[1,64,256]{2,1,0:T(8,128)(2,1)S(1)}, u32[]{:S(2)}, u32[]{:S(2)}) collective-permute-start(bf16[1,64,256]{2,1,0:T(8,128)(2,1)S(1)} %get-tuple-element.29), channel_id=1, source_target_pairs={{0,16},{4,20},{8,24},{12,28},{16,0},{20,4},{24,8},{28,12},{1,17},{... | collective-permute-start | bytes 98312 | tf_op jit(solution)/shard_map/ppermute | solution.py:179
  14.5 2.2 %collective-permute-done.2.came_ref = bf16[1,64,256]{2,1,0:T(8,128)(2,1)S(1)} collective-permute-done((bf16[1,64,256]{2,1,0:T(8,128)(2,1)S(1)}, bf16[1,64,256]{2,1,0:T(8,128)(2,1)S(1)}, u32[]{:S(2)}, u32[]{:S(2)}) %collective-permute-start.2) | collective-permute-done | bytes 32800 | tf_op jit(solution)/shard_map/ppermute | solution.py:179
  16.7 0.0 collective-permute-done.4.refs_2_
  16.7 0.0 collective-permute-done.3.refs_1_
  16.7 0.0 collective-permute-done.5.refs_3_
  16.7 0.0 copy-start.4
  16.7 0.0 copy-start.5
  16.8 0.6 %copy-done.4 = s32[2,8]{1,0:T(2,128)S(1)} copy-done((s32[2,8]{1,0:T(2,128)S(1)}, s32[2,8]{1,0:T(2,128)}, u32[]{:S(2)}) %copy-start.4) | copy-done | bytes 88
  17.4 2.5 %layer.1 = (bf16[256,256]{1,0:T(8,128)(2,1)}, f32[256,256]{1,0:T(8,128)S(1)}, bf16[256,256]{1,0:T(8,128)(2,1)S(1)}, bf16[256,256]{1,0:T(8,128)(2,1)S(1)}, bf16[2...) custom-call(s32[2,8]{1,0:T(2,128)S(1)} %copy-done.4, ...), custom_call_target="tpu_custom_call" | custom-call | tf_op jit(solution)/shard_map/layer/pallas_call | solution.py:213
  19.9 6.1 %all-to-all-start = ((bf16[32,16,128]{2,1,0:T(8,128)(2,1)}), bf16[32,16,128]{2,1,0:T(8,128)(2,1)S(1)}, u32[]{:S(2)}, u32[]{:S(2)}) async-start(bf16[32,16,128]{2,1,0:T(8,128)(2,1)} %get-tuple-element.34), calls=%async_computation | async-start | bytes 262144 | tf_op jit(solution)/shard_map/all_to_all | solution.py:237
  26.0 1.8 %collective-permute-start.9 = (bf16[256,256]{1,0:T(8,128)(2,1)S(1)}, bf16[256,256]{1,0:T(8,128)(2,1)S(1)}, u32[]{:S(2)}, u32[]{:S(2)}) collective-permute-start(bf16[256,256]{1,0:T(8,128)(2,1)S(1)} %get-tuple-element.40), channel_id=1, source_target_pairs={{0,1},{1,0},{2,3},{3,2},{4,5},{5,4},{6,7},{7,6},{8,9},{9,8},{10,11... | collective-permute-start | bytes 393224 | tf_op jit(solution)/shard_map/ppermute | solution.py:175
  27.9 2.4 %collective-permute-start.10 = (bf16[256,256]{1,0:T(8,128)(2,1)S(1)}, bf16[256,256]{1,0:T(8,128)(2,1)S(1)}, u32[]{:S(2)}, u32[]{:S(2)}) collective-permute-start(bf16[256,256]{1,0:T(8,128)(2,1)S(1)} %get-tuple-element.41), channel_id=1, source_target_pairs={{0,2},{1,3},{2,0},{3,1},{4,6},{5,7},{6,4},{7,5},{8,10},{9,11},{10,... | collective-permute-start | bytes 393224 | tf_op jit(solution)/shard_map/ppermute | solution.py:175
  30.3 0.2 collective-permute-start.11
  30.5 4.2 %all-to-all-done.parts_ref = bf16[32,16,128]{2,1,0:T(8,128)(2,1)S(1)} async-done(((bf16[32,16,128]{2,1,0:T(8,128)(2,1)}), bf16[32,16,128]{2,1,0:T(8,128)(2,1)S(1)}, u32[]{:S(2)}, u32[]{:S(2)}) %all-to-all-start) | async-done | bytes 131104 | tf_op jit(solution)/shard_map/all_to_all | solution.py:237
  34.7 0.7 %sum_parts.1.refs_0_ = bf16[32,16,128]{2,1,0:T(8,128)(2,1)} custom-call(bf16[32,16,128]{2,1,0:T(8,128)(2,1)S(1)} %all-to-all-done.parts_ref), custom_call_target="tpu_custom_call" | custom-call | tf_op jit(solution)/shard_map/sum_parts/pallas_call | solution.py:238
  35.4 2.6 %all-to-all-start.1 = ((bf16[32,16,128]{2,1,0:T(8,128)(2,1)}), bf16[32,16,128]{2,1,0:T(8,128)(2,1)S(1)}, u32[]{:S(2)}, u32[]{:S(2)}) async-start(bf16[32,16,128]{2,1,0:T(8,128)(2,1)} %sum_parts.1.refs_0_), calls=%async_computation.1 | async-start | bytes 262144 | tf_op jit(solution)/shard_map/all_to_all | solution.py:246
  37.9 0.9 %exchange_step.6 = (bf16[2,32,256]{2,1,0:T(8,128)(2,1)S(1)}, bf16[2,32,256]{2,1,0:T(8,128)(2,1)S(1)}) custom-call(bf16[4,16,256]{2,1,0:T(8,128)(2,1)S(1)} %get-tuple-element.32.keep_ref, bf16[4,16,256]{2,1,0:T(8,128)(2,1)S(1)} %collective-permute-done.6.got_ref, bf16[32,16,128]{2,1,0:T(8,128)(2,1)} %sum_parts.1.refs_0_), custom_call_target="tpu_custom_call" | custom-call | flops 1 | bytes 1 | tf_op jit(solution)/shard_map/exchange_step/pallas_call | solution.py:183
  38.9 1.6 %collective-permute-start.7 = (bf16[2,32,256]{2,1,0:T(8,128)(2,1)S(1)}, bf16[2,32,256]{2,1,0:T(8,128)(2,1)S(1)}, u32[]{:S(2)}, u32[]{:S(2)}) collective-permute-start(bf16[2,32,256]{2,1,0:T(8,128)(2,1)S(1)} %get-tuple-element.36), channel_id=1, source_target_pairs={{0,8},{4,12},{8,0},{12,4},{16,24},{20,28},{24,16},{28,20},{1,9},{5... | collective-permute-start | bytes 98312 | tf_op jit(solution)/shard_map/ppermute | solution.py:179
  40.5 2.5 %collective-permute-done.7.got_ref = bf16[2,32,256]{2,1,0:T(8,128)(2,1)S(1)} collective-permute-done((bf16[2,32,256]{2,1,0:T(8,128)(2,1)S(1)}, bf16[2,32,256]{2,1,0:T(8,128)(2,1)S(1)}, u32[]{:S(2)}, u32[]{:S(2)}) %collective-permute-start.7) | collective-permute-done | bytes 32800 | tf_op jit(solution)/shard_map/ppermute | solution.py:179
  43.1 1.6 %collective-permute-start.8 = (bf16[1,64,256]{2,1,0:T(8,128)(2,1)S(1)}, bf16[1,64,256]{2,1,0:T(8,128)(2,1)S(1)}, u32[]{:S(2)}, u32[]{:S(2)}) collective-permute-start(bf16[1,64,256]{2,1,0:T(8,128)(2,1)S(1)} %get-tuple-element.38), channel_id=1, source_target_pairs={{0,16},{4,20},{8,24},{12,28},{16,0},{20,4},{24,8},{28,12},{1,17},{... | collective-permute-start | bytes 98312 | tf_op jit(solution)/shard_map/ppermute | solution.py:179
  44.7 2.5 %collective-permute-done.8.came_ref = bf16[1,64,256]{2,1,0:T(8,128)(2,1)S(1)} collective-permute-done((bf16[1,64,256]{2,1,0:T(8,128)(2,1)S(1)}, bf16[1,64,256]{2,1,0:T(8,128)(2,1)S(1)}, u32[]{:S(2)}, u32[]{:S(2)}) %collective-permute-start.8) | collective-permute-done | bytes 32800 | tf_op jit(solution)/shard_map/ppermute | solution.py:179
  47.2 1.0 %input_gradient.1 = bf16[256,256]{1,0:T(8,128)(2,1)} custom-call(s32[1,8,16]{2,1,0:T(8,128)S(1)} %copy-done.3, bf16[1,64,256]{2,1,0:T(8,128)(2,1)S(1)} %get-tuple-element.37.kept_ref, bf16[1,64,256]{2,1,0:T(8,128)(2,1)S(1)} %collective-permute-done.8.came_ref, bf16[256,256]{1,0:T(8,128)(2,1)S(1)} %copy-done.1, f32[256,256]{1,0:T(8,128)S(1)} %get-tuple-element.39.own_ref, ...), custom_call_target="tpu_custom_call" | custom-call | flops 1800000000 | bytes 1 | tf_op jit(solution)/shard_map/input_gradient/pallas_call | solution.py:259
  48.2 0.7 %weight_gradient.1 = f32[256,256]{1,0:T(8,128)} custom-call(bf16[32,16,128]{2,1,0:T(8,128)(2,1)S(1)} %all-to-all-done.1.chunks_ref), custom_call_target="tpu_custom_call" | custom-call | tf_op jit(solution)/shard_map/weight_gradient/pallas_call | solution.py:247
  (17 shorter events, 0.0 us)
Async XLA Ops:
  0.6 16.1 %collective-permute-start.4 = (bf16[256,256]{1,0:T(8,128)(2,1)}, bf16[256,256]{1,0:T(8,128)(2,1)S(1)}, u32[]{:S(2)}, u32[]{:S(2)}) collective-permute-start(bf16[256,256]{1,0:T(8,128)(2,1)} %refs_0_.1), channel_id=1, source_target_pairs={{0,2},{1,3},{2,0},{3,1},{4,6},{5,7},{6,4},{7,5},{8,10},{9,11},{10,... | collective-permute-start | bytes 393224 | tf_op jit(solution)/shard_map/ppermute | solution.py:175
  4.7 12.0 %collective-permute-start.3 = (bf16[256,256]{1,0:T(8,128)(2,1)}, bf16[256,256]{1,0:T(8,128)(2,1)S(1)}, u32[]{:S(2)}, u32[]{:S(2)}) collective-permute-start(bf16[256,256]{1,0:T(8,128)(2,1)} %refs_0_.1), channel_id=1, source_target_pairs={{0,1},{1,0},{2,3},{3,2},{4,5},{5,4},{6,7},{7,6},{8,9},{9,8},{10,11... | collective-permute-start | bytes 393224 | tf_op jit(solution)/shard_map/ppermute | solution.py:175
  6.3 10.4 %collective-permute-start.5 = (bf16[256,256]{1,0:T(8,128)(2,1)}, bf16[256,256]{1,0:T(8,128)(2,1)S(1)}, u32[]{:S(2)}, u32[]{:S(2)}) collective-permute-start(bf16[256,256]{1,0:T(8,128)(2,1)} %refs_0_.1), channel_id=1, source_target_pairs={{0,3},{1,2},{2,1},{3,0},{4,7},{5,6},{6,5},{7,4},{8,11},{9,10},{10,... | collective-permute-start | bytes 393224 | tf_op jit(solution)/shard_map/ppermute | solution.py:175
  6.3 10.4 %copy-start.1 = (bf16[256,256]{1,0:T(8,128)(2,1)S(1)}, bf16[256,256]{1,0:T(8,128)(2,1)}, u32[]{:S(2)}) copy-start(bf16[256,256]{1,0:T(8,128)(2,1)} %weight_ref.3) | copy-start | bytes 393220
  6.3 10.4 %copy-start.2 = (bf16[256,128]{1,0:T(8,128)(2,1)S(1)}, bf16[256,128]{1,0:T(8,128)(2,1)}, u32[]{:S(2)}) copy-start(bf16[256,128]{1,0:T(8,128)(2,1)} %bnd_ref.1) | copy-start | bytes 196612
  7.6 9.2 %copy-start = (bf16[256,256]{1,0:T(8,128)(2,1)S(1)}, bf16[256,256]{1,0:T(8,128)(2,1)}, u32[]{:S(2)}) copy-start(bf16[256,256]{1,0:T(8,128)(2,1)} %refs_0_.1) | copy-start | bytes 393220
  7.6 1.3 %collective-permute-start = (bf16[4,16,256]{2,1,0:T(8,128)(2,1)S(1)}, bf16[4,16,256]{2,1,0:T(8,128)(2,1)S(1)}, u32[]{:S(2)}, u32[]{:S(2)}) collective-permute-start(bf16[4,16,256]{2,1,0:T(8,128)(2,1)S(1)} %get-tuple-element.25), channel_id=1, source_target_pairs={{0,4},{4,0},{8,12},{12,8},{16,20},{20,16},{24,28},{28,24},{1,5},{5... | collective-permute-start | bytes 98312 | tf_op jit(solution)/shard_map/ppermute | solution.py:179
  8.9 3.9 %collective-permute-start.1 = (bf16[2,32,256]{2,1,0:T(8,128)(2,1)S(1)}, bf16[2,32,256]{2,1,0:T(8,128)(2,1)S(1)}, u32[]{:S(2)}, u32[]{:S(2)}) collective-permute-start(bf16[2,32,256]{2,1,0:T(8,128)(2,1)S(1)} %get-tuple-element.27), channel_id=1, source_target_pairs={{0,8},{4,12},{8,0},{12,4},{16,24},{20,28},{24,16},{28,20},{1,9},{5... | collective-permute-start | bytes 98312 | tf_op jit(solution)/shard_map/ppermute | solution.py:179
  12.8 3.9 %collective-permute-start.2 = (bf16[1,64,256]{2,1,0:T(8,128)(2,1)S(1)}, bf16[1,64,256]{2,1,0:T(8,128)(2,1)S(1)}, u32[]{:S(2)}, u32[]{:S(2)}) collective-permute-start(bf16[1,64,256]{2,1,0:T(8,128)(2,1)S(1)} %get-tuple-element.29), channel_id=1, source_target_pairs={{0,16},{4,20},{8,24},{12,28},{16,0},{20,4},{24,8},{28,12},{1,17},{... | collective-permute-start | bytes 98312 | tf_op jit(solution)/shard_map/ppermute | solution.py:179
  16.7 0.7 %copy-start.4 = (s32[2,8]{1,0:T(2,128)S(1)}, s32[2,8]{1,0:T(2,128)}, u32[]{:S(2)}) copy-start(s32[2,8]{1,0:T(2,128)} %cols_ref.1) | copy-start | bytes 196
  16.7 0.7 %copy-start.5 = (s32[2]{0:T(128)S(1)}, s32[2]{0:T(128)}, u32[]{:S(2)}) copy-start(s32[2]{0:T(128)} %counts_ref.1) | copy-start | bytes 28
  19.9 14.7 %all-to-all-start = ((bf16[32,16,128]{2,1,0:T(8,128)(2,1)}), bf16[32,16,128]{2,1,0:T(8,128)(2,1)S(1)}, u32[]{:S(2)}, u32[]{:S(2)}) async-start(bf16[32,16,128]{2,1,0:T(8,128)(2,1)} %get-tuple-element.34), calls=%async_computation | async-start | bytes 262144 | tf_op jit(solution)/shard_map/all_to_all | solution.py:237
  26.0 18.7 %collective-permute-start.9 = (bf16[256,256]{1,0:T(8,128)(2,1)S(1)}, bf16[256,256]{1,0:T(8,128)(2,1)S(1)}, u32[]{:S(2)}, u32[]{:S(2)}) collective-permute-start(bf16[256,256]{1,0:T(8,128)(2,1)S(1)} %get-tuple-element.40), channel_id=1, source_target_pairs={{0,1},{1,0},{2,3},{3,2},{4,5},{5,4},{6,7},{7,6},{8,9},{9,8},{10,11... | collective-permute-start | bytes 393224 | tf_op jit(solution)/shard_map/ppermute | solution.py:175
  27.9 16.9 %collective-permute-start.10 = (bf16[256,256]{1,0:T(8,128)(2,1)S(1)}, bf16[256,256]{1,0:T(8,128)(2,1)S(1)}, u32[]{:S(2)}, u32[]{:S(2)}) collective-permute-start(bf16[256,256]{1,0:T(8,128)(2,1)S(1)} %get-tuple-element.41), channel_id=1, source_target_pairs={{0,2},{1,3},{2,0},{3,1},{4,6},{5,7},{6,4},{7,5},{8,10},{9,11},{10,... | collective-permute-start | bytes 393224 | tf_op jit(solution)/shard_map/ppermute | solution.py:175
  30.3 14.4 %collective-permute-start.11 = (bf16[256,256]{1,0:T(8,128)(2,1)S(1)}, bf16[256,256]{1,0:T(8,128)(2,1)S(1)}, u32[]{:S(2)}, u32[]{:S(2)}) collective-permute-start(bf16[256,256]{1,0:T(8,128)(2,1)S(1)} %get-tuple-element.42), channel_id=1, source_target_pairs={{0,3},{1,2},{2,1},{3,0},{4,7},{5,6},{6,5},{7,4},{8,11},{9,10},{10,... | collective-permute-start | bytes 393224 | tf_op jit(solution)/shard_map/ppermute | solution.py:175
  30.5 7.5 %collective-permute-start.6 = (bf16[4,16,256]{2,1,0:T(8,128)(2,1)S(1)}, bf16[4,16,256]{2,1,0:T(8,128)(2,1)S(1)}, u32[]{:S(2)}, u32[]{:S(2)}) collective-permute-start(bf16[4,16,256]{2,1,0:T(8,128)(2,1)S(1)} %get-tuple-element.33), channel_id=1, source_target_pairs={{0,4},{4,0},{8,12},{12,8},{16,20},{20,16},{24,28},{28,24},{1,5},{5... | collective-permute-start | bytes 98312 | tf_op jit(solution)/shard_map/ppermute | solution.py:179
  35.4 12.9 %all-to-all-start.1 = ((bf16[32,16,128]{2,1,0:T(8,128)(2,1)}), bf16[32,16,128]{2,1,0:T(8,128)(2,1)S(1)}, u32[]{:S(2)}, u32[]{:S(2)}) async-start(bf16[32,16,128]{2,1,0:T(8,128)(2,1)} %sum_parts.1.refs_0_), calls=%async_computation.1 | async-start | bytes 262144 | tf_op jit(solution)/shard_map/all_to_all | solution.py:246
  38.9 4.2 %collective-permute-start.7 = (bf16[2,32,256]{2,1,0:T(8,128)(2,1)S(1)}, bf16[2,32,256]{2,1,0:T(8,128)(2,1)S(1)}, u32[]{:S(2)}, u32[]{:S(2)}) collective-permute-start(bf16[2,32,256]{2,1,0:T(8,128)(2,1)S(1)} %get-tuple-element.36), channel_id=1, source_target_pairs={{0,8},{4,12},{8,0},{12,4},{16,24},{20,28},{24,16},{28,20},{1,9},{5... | collective-permute-start | bytes 98312 | tf_op jit(solution)/shard_map/ppermute | solution.py:179
  43.1 4.1 %copy-start.3 = (s32[1,8,16]{2,1,0:T(8,128)S(1)}, s32[1,8,16]{2,1,0:T(8,128)}, u32[]{:S(2)}) copy-start(s32[1,8,16]{2,1,0:T(8,128)} %index_ref.3) | copy-start | bytes 1540
  43.1 4.1 %collective-permute-start.8 = (bf16[1,64,256]{2,1,0:T(8,128)(2,1)S(1)}, bf16[1,64,256]{2,1,0:T(8,128)(2,1)S(1)}, u32[]{:S(2)}, u32[]{:S(2)}) collective-permute-start(bf16[1,64,256]{2,1,0:T(8,128)(2,1)S(1)} %get-tuple-element.38), channel_id=1, source_target_pairs={{0,16},{4,20},{8,24},{12,28},{16,0},{20,4},{24,8},{28,12},{1,17},{... | collective-permute-start | bytes 98312 | tf_op jit(solution)/shard_map/ppermute | solution.py:179

commit v7 on v4

--- a/solution.py
+++ b/solution.py
@@ -43,13 +43,12 @@
     return jnp.where(at == flat, 1.0, 0.0).astype(BF16)
 
 
-def pick_kernel(index_ref, features_ref, vals_ref, cot_ref, out_ref, vals_out, cot_out, index, features, sems):
-    copies = [
-        pltpu.make_async_copy(index_ref, index, sems.at[0]),
-        pltpu.make_async_copy(features_ref, features, sems.at[1]),
-        pltpu.make_async_copy(cot_ref, cot_out, sems.at[2]),
-        pltpu.make_async_copy(vals_ref, vals_out, sems.at[3]),
-    ]
+def pick_kernel(index_ref, features_ref, *refs):
+    count = (len(refs) - 4) // 2
+    loads, out_ref, loaded = refs[:count], refs[count], refs[count + 1 : -3]
+    index, features, sems = refs[-3:]
+    pairs = [(index_ref, index), (features_ref, features), *zip(loads, loaded)]
+    copies = [pltpu.make_async_copy(*pair, sems.at[at]) for at, pair in enumerate(pairs)]
     for copy in copies:
         copy.start()
     copies[0].wait()
@@ -63,33 +62,31 @@
         copy.wait()
 
 
+def live_tiles(counts_ref, vals_ref, t):
+    return [
+        jnp.where(k < counts_ref[t], vals_ref[t, k], jnp.zeros_like(vals_ref[t, k]))
+        for k in range(vals_ref.shape[1])
+    ]
+
+
 def layer_kernel(rep, cols_ref, counts_ref, vals_ref, received_ref, bnd_ref, cot_ref, weight_ref, *refs):
     blocks = refs[:rep]
-    out_ref, own_ref = refs[rep], refs[rep + 1]
-    sends = refs[rep + 2 : 2 * rep + 1]
-    message_ref, panel, terms = refs[2 * rep + 1 :]
+    out_ref, grad_ref, message_ref, panel = refs[rep:]
     me = lax.axis_index("rep")
     tiles, slots = cols_ref.shape
-    width = weight_ref.shape[1]
     for shift, block in enumerate(blocks):
         owner = source(me, shift, rep)
         for t in range(tiles):
             panel[owner * tiles + t] = block[t * TILE : (t + 1) * TILE, :]
     groups, each = received_ref.shape[0], received_ref.shape[1]
     received = jnp.concatenate([received_ref[q] for q in range(groups)], axis=0)
-    adjacency = []
     forward = []
     backward = []
     for t in range(tiles):
-        live = [
-            jnp.where(k < counts_ref[t], vals_ref[t, k], jnp.zeros_like(vals_ref[t, k]))
-            for k in range(slots)
-        ]
+        live = live_tiles(counts_ref, vals_ref, t)
         chosen = jnp.concatenate([panel[cols_ref[t, k]] for k in range(slots)], axis=0)
-        stacked = jnp.concatenate(live, axis=0)
-        adjacency.append(stacked)
         forward.append(dot(jnp.concatenate(live, axis=1), chosen, 1, 0))
-        backward.append(dot(stacked, chosen, 0, 0))
+        backward.append(dot(jnp.concatenate(live, axis=0), chosen, 0, 0))
     outside = dot(bnd_ref[...], received, 1, 0)
     mixed = jnp.concatenate(forward, axis=0) + outside
     turned = (jnp.concatenate(backward, axis=0) + outside).astype(BF16)
@@ -100,16 +97,7 @@
     sig = jax.nn.sigmoid(pre)
     out_ref[...] = (pre * sig).astype(BF16)
     grad = (cot_ref[...].astype(F32) * sig * (1.0 + pre * (1.0 - sig))).astype(BF16)
-    terms[...] = jnp.zeros_like(terms)
-    for t in range(tiles):
-        parts = dot(adjacency[t], grad[t * TILE : (t + 1) * TILE], 1, 0)
-        for k in range(slots):
-            terms[cols_ref[t, k]] += parts[k * TILE : (k + 1) * TILE]
-    for t in range(tiles):
-        own_ref[t * TILE : (t + 1) * TILE, :] = terms[me * tiles + t]
-        for shift, send in enumerate(sends, 1):
-            owner = target(me, shift, rep)
-            send[t * TILE : (t + 1) * TILE, :] = terms[owner * tiles + t].astype(BF16)
+    grad_ref[...] = grad
     boundary = dot(bnd_ref[...], grad, 0, 0).astype(BF16)
     partial = dot(turned, grad, 0, 0).astype(BF16)
     share = partial.shape[0] // groups
@@ -119,6 +107,29 @@
         message_ref[q, each:, :] = partial[at : at + share]
 
 
+def terms_kernel(rep, layout, cols_ref, counts_ref, vals_ref, grad_ref, *refs):
+    outs, terms = refs[:-1], refs[-1]
+    me = lax.axis_index("rep")
+    tiles, slots = cols_ref.shape
+    terms[...] = jnp.zeros_like(terms)
+    for t in range(tiles):
+        stacked = jnp.concatenate(live_tiles(counts_ref, vals_ref, t), axis=0)
+        parts = dot(stacked, grad_ref[t * TILE : (t + 1) * TILE, :], 1, 0)
+        for k in range(slots):
+            terms[cols_ref[t, k]] += parts[k * TILE : (k + 1) * TILE]
+    for out_ref, shifts in zip(outs, layout):
+        for at, shift in enumerate(shifts):
+            owner = target(me, shift, rep)
+            for t in range(tiles):
+                row = (at * tiles + t) * TILE
+                out_ref[row : row + TILE, :] = terms[owner * tiles + t].astype(out_ref.dtype)
+
+
+def relay_kernel(far_ref, came_ref, out_ref):
+    rows = far_ref.shape[0]
+    out_ref[...] = (far_ref[...] + came_ref[rows:, :].astype(F32)).astype(BF16)
+
+
 def rep_sum_kernel(*refs):
     chunk, one, two, three = [ref[...].astype(F32) for ref in refs[:4]]
     refs[-1][...] = ((chunk + two) + (one + three)).astype(BF16)
@@ -139,7 +150,7 @@
     returned = jnp.concatenate([returned_ref[q, :each, :] for q in range(groups)], axis=0)
     total = own_ref[...] + dot(onehot, returned, 1, 0)
     for term in arrived:
-        total = total + term[...].astype(F32)
+        total = total + term[: own_ref.shape[0], :].astype(F32)
     out_ref[...] = dot(total.astype(BF16), weight_ref[...], 1, 1).astype(BF16)
 
 
@@ -157,56 +168,78 @@
         return lax.ppermute(value, "rep", [(i, target(i, shift, rep)) for i in range(rep)])
 
     blocks = [features] + [shifted(features, shift) for shift in range(1, rep)]
-    outgoing, tile_vals, cotangent = pl.pallas_call(
+    tiny = pl.CostEstimate(flops=1, bytes_accessed=1, transcendentals=0)
+    loads = [tile_vals, cotangent, tile_cols, tile_counts]
+    outgoing, tile_vals, cotangent, tile_cols, tile_counts = pl.pallas_call(
         pick_kernel,
         out_shape=[
             jax.ShapeDtypeStruct((groups, each, feats), BF16),
-            jax.ShapeDtypeStruct(tile_vals.shape, BF16),
-            jax.ShapeDtypeStruct(cotangent.shape, BF16),
-        ],
-        in_specs=[HBM] * 4,
-        out_specs=[VMEM] * 3,
+            *[jax.ShapeDtypeStruct(load.shape, load.dtype) for load in loads],
+        ],
+        in_specs=[HBM] * (2 + len(loads)),
+        out_specs=[VMEM] * (1 + len(loads)),
         scratch_shapes=[
             pltpu.VMEM(send_rows.shape, jnp.int32),
             pltpu.VMEM((rows, feats), BF16),
-            pltpu.SemaphoreType.DMA((4,)),
+            pltpu.SemaphoreType.DMA((2 + len(loads),)),
         ],
         compiler_params=params,
         name="pick_rows",
-    )(*[pltpu.with_memory_space_constraint(x, pltpu.HBM) for x in (send_rows, features, tile_vals, cotangent)])
+    )(*[pltpu.with_memory_space_constraint(x, pltpu.HBM) for x in (send_rows, features, *loads)])
     received = lax.all_to_all(outgoing, "dom", split_axis=0, concat_axis=0, tiled=True)
-    results = pl.pallas_call(
+    output, grad, message = pl.pallas_call(
         functools.partial(layer_kernel, rep),
         out_shape=[
             jax.ShapeDtypeStruct((rows, width), BF16),
-            jax.ShapeDtypeStruct((rows, width), F32),
-            *[jax.ShapeDtypeStruct((rows, width), BF16)] * (rep - 1),
+            jax.ShapeDtypeStruct((rows, width), BF16),
             jax.ShapeDtypeStruct((groups, each + share, width), BF16),
         ],
         in_specs=[SMEM] * 2 + [VMEM] * (5 + rep),
-        out_specs=[VMEM] * (rep + 2),
-        scratch_shapes=[
-            pltpu.VMEM((rep * tiles, TILE, feats), BF16),
-            pltpu.VMEM((rep * tiles, TILE, width), F32),
-        ],
+        out_specs=[VMEM] * 3,
+        scratch_shapes=[pltpu.VMEM((rep * tiles, TILE, feats), BF16)],
         compiler_params=params,
         name="layer",
     )(tile_cols, tile_counts, tile_vals, received, bnd_adj, cotangent, weight, *blocks)
-    output, own, sends, message = results[0], results[1], results[2:-1], results[-1]
     returned = lax.all_to_all(message, "dom", split_axis=0, concat_axis=0, tiled=True)
-    arrived = [shifted(send, shift) for shift, send in enumerate(sends, 1)]
+    relayed = rep == 4
+    layout = [(0,), (1, 3), (2,)] if relayed else [(shift,) for shift in range(rep)]
+    kinds = [F32, BF16, F32] if relayed else [F32] + [BF16] * (rep - 1)
+    own, *sends = pl.pallas_call(
+        functools.partial(terms_kernel, rep, layout),
+        out_shape=[
+            jax.ShapeDtypeStruct((len(shifts) * rows, width), kind)
+            for shifts, kind in zip(layout, kinds)
+        ],
+        in_specs=[SMEM] * 2 + [VMEM] * 2,
+        out_specs=[VMEM] * len(layout),
+        scratch_shapes=[pltpu.VMEM((rep * tiles, TILE, width), F32)],
+        compiler_params=params,
+        name="terms",
+    )(tile_cols, tile_counts, tile_vals, grad)
     chunk = jnp.sum(returned[:, each:].astype(F32), axis=0).astype(BF16)
-    if rep == 4:
+    if relayed:
+        came = shifted(sends[0], 1)
+        relay = pl.pallas_call(
+            relay_kernel,
+            out_shape=jax.ShapeDtypeStruct((rows, width), BF16),
+            in_specs=[VMEM] * 2,
+            out_specs=VMEM,
+            compiler_params=params,
+            cost_estimate=tiny,
+            name="relay",
+        )(sends[1], came)
+        arrived = [came, shifted(relay, 2)]
         piece = pl.pallas_call(
             rep_sum_kernel,
             out_shape=jax.ShapeDtypeStruct(chunk.shape, BF16),
-            in_specs=[VMEM] * (3 + rep),
+            in_specs=[VMEM] * 5,
             out_specs=VMEM,
             compiler_params=params,
-            cost_estimate=pl.CostEstimate(flops=1, bytes_accessed=1, transcendentals=0),
+            cost_estimate=tiny,
             name="rep_sum",
-        )(chunk, *[shifted(chunk, shift) for shift in (1, 2, 3)], *arrived)
+        )(chunk, *[shifted(chunk, shift) for shift in (1, 2, 3)], relay)
     else:
+        arrived = [shifted(send, shift) for shift, send in enumerate(sends, 1)]
         piece = jnp.sum(lax.all_gather(chunk, "rep").astype(F32), axis=0).astype(BF16)
     for bit in reversed(bits):
         got = lax.ppermute(piece, "dom", [(i, i ^ bit) for i in range(groups)])
@@ -216,16 +249,17 @@
             in_specs=[VMEM] * 2,
             out_specs=VMEM,
             compiler_params=params,
-            cost_estimate=pl.CostEstimate(flops=1, bytes_accessed=1, transcendentals=0),
+            cost_estimate=tiny,
             name="join",
         )(piece, got)
     grad_weight = piece
     grad_features = pl.pallas_call(
         final_kernel,
         out_shape=jax.ShapeDtypeStruct((rows, feats), BF16),
-        in_specs=[VMEM] * (3 + rep),
+        in_specs=[VMEM] * (4 + len(arrived)),
         out_specs=VMEM,
         compiler_params=params,
+        cost_estimate=pl.CostEstimate(flops=1_000_000_000, bytes_accessed=1, transcendentals=0),
         name="input_gradient",
     )(send_rows, returned, weight, own, *arrived)
     return (output, grad_features, grad_weight)

time: 51.6 us -> 49.4 us (0.957)
  starting transfers between devices: 21.9 us -> 19.5 us
  local copies, waits for them, and re-layouts: 1.25 us -> 0.02 us
  Pallas kernels: 5.62 us -> 6.46 us
  waiting for transfers between devices: 12.9 us -> 13.5 us
    ppermute x9 -> x8, waiting for transfers between devices: 7.29 us -> 2.51 us  [shifted(): lax.ppermute(value, 'rep', [(i, target(i, shift, rep)) for i in range(rep)])]
    ppermute x3, waiting for transfers between devices: 4.24 us -> 7.99 us  [body(): got = lax.ppermute(piece, 'dom', [(i, i ^ bit) for i in range(groups)])]
    ppermute x3, starting transfers between devices: 3.55 us -> 1.04 us  [body(): got = lax.ppermute(piece, 'dom', [(i, i ^ bit) for i in range(groups)])]
    all_to_all x1, waiting for transfers between devices: 1.37 us -> 3.04 us  [body(): lax.all_to_all(message, 'dom', split_axis=0, concat_axis=0, tiled=True)]
    unnamed x12 -> x8, local copies, waits for them, and re-layouts: 1.25 us -> 0.02 us
    pallas_call x0 -> x2, Pallas kernels: none -> 1.18 us  [the longest x1 1.15 us: body(): pl.pallas_call(functools.partial(terms_kernel, rep, layout), out_shape=[j...]
    ppermute x9 -> x8, starting transfers between devices: 14.9 us -> 14.8 us  [shifted(): lax.ppermute(value, 'rep', [(i, target(i, shift, rep)) for i in range(rep)])]
  transfers between devices with their start and end apart: 13 -> 12, of which waited for: 6 -> 6; matrix products, arithmetic and copies ran while one was open for 0% -> 0% of each run, Pallas kernels for 5% -> 7%
where the time goes in v7:
time: 49.4 us; the launch traced here: 49.1 us
  starting transfers between devices  19.5 us (39%)
  waiting for transfers between devices  13.5 us (27%)
  blocking collectives  8.86 us (18%)
  Pallas kernels  6.46 us (13%)
  between operations  0.71 us (1%)
    ppermute x8, starting transfers between devices, shifted(): lax.ppermute(value, 'rep', [(i, target(i, shift, rep)) for i in range(rep)])  14.8 us
    all_to_all x1, blocking collectives, body(): lax.all_to_all(outgoing, 'dom', split_axis=0, concat_axis=0, tiled=True)  8.86 us
    ppermute x3, waiting for transfers between devices, body(): got = lax.ppermute(piece, 'dom', [(i, i ^ bit) for i in range(groups)])  7.99 us
    all_to_all x1, starting transfers between devices, body(): lax.all_to_all(message, 'dom', split_axis=0, concat_axis=0, tiled=True)  3.72 us
    all_to_all x1, waiting for transfers between devices, body(): lax.all_to_all(message, 'dom', split_axis=0, concat_axis=0, tiled=True)  3.04 us
    ppermute x8, waiting for transfers between devices, shifted(): lax.ppermute(value, 'rep', [(i, target(i, shift, rep)) for i in range(rep)])  2.51 us
    pallas_call x1, Pallas kernels, body(): pl.pallas_call(functools.partial(layer_kernel, rep), out_shape=[jax.Shape...  2.23 us
    pallas_call x1, Pallas kernels, body(): pl.pallas_call(pick_kernel, out_shape=[jax.ShapeDtypeStruct((groups, each...  1.26 us
  transfers between devices with their start and end apart: 12, of which 6 were waited for; matrix products, arithmetic and copies ran while one was open for 0% of the time, Pallas kernels for 7%

profile of v7, /device:TPU:0, one launch (start us, length us, event | category | flops | bytes accessed | tf_op | source)
XLA Modules:
  0.0 49.1 jit_solution(3564981525442036132)
XLA Ops:
  0.6 3.1 %collective-permute-start = (bf16[256,256]{1,0:T(8,128)(2,1)}, bf16[256,256]{1,0:T(8,128)(2,1)S(1)}, u32[]{:S(2)}, u32[]{:S(2)}) collective-permute-start(bf16[256,256]{1,0:T(8,128)(2,1)} %refs_0_.3), channel_id=1, source_target_pairs={{0,1},{1,0},{2,3},{3,2},{4,5},{5,4},{6,7},{7,6},{8,9},{9,8},{10,11... | collective-permute-start | bytes 393224 | tf_op jit(solution)/shard_map/ppermute | solution.py:168
  3.7 2.6 %collective-permute-start.1 = (bf16[256,256]{1,0:T(8,128)(2,1)}, bf16[256,256]{1,0:T(8,128)(2,1)S(1)}, u32[]{:S(2)}, u32[]{:S(2)}) collective-permute-start(bf16[256,256]{1,0:T(8,128)(2,1)} %refs_0_.3), channel_id=1, source_target_pairs={{0,2},{1,3},{2,0},{3,1},{4,6},{5,7},{6,4},{7,5},{8,10},{9,11},{10,... | collective-permute-start | bytes 393224 | tf_op jit(solution)/shard_map/ppermute | solution.py:168
  6.3 0.0 collective-permute-start.2
  6.3 1.3 %pick_rows.1 = (bf16[8,16,256]{2,1,0:T(8,128)(2,1)S(1)}, bf16[2,8,128,128]{3,2,1,0:T(8,128)(2,1)S(1)}, bf16[256,256]{1,0:T(8,128)(2,1)S(1)}, s32[2,8]{1,0:T(2,128)S(1)}, s32[2]{0:T(128)S(1)}) custom-call(s32[1,8,16]{2,1,0:T(8,128)} %index_ref.3, bf16[256,256]{1,0:T(8,128)(2,1)} %refs_0_.3, bf16[2,8,128,128]{3,2,1,0:T(8,128)(2,1)} %refs_0_.2, ...), custom_call_target="tpu_custom_call" | custom-call | tf_op jit(solution)/shard_map/pick_rows/pallas_call | solution.py:173
  7.6 0.0 copy-start
  7.6 8.9 %all_to_all.10.received_ref = bf16[8,16,256]{2,1,0:T(8,128)(2,1)S(1)} all-to-all(bf16[8,16,256]{2,1,0:T(8,128)(2,1)S(1)} %get-tuple-element.17), channel_id=1, replica_groups=mesh['dom'=8,'rep'=4] {'dom'}, dimensions={0} | all-to-all | bytes 131072 | tf_op jit(solution)/shard_map/all_to_all | solution.py:189
  16.5 0.0 collective-permute-done.refs_1_
  16.5 0.4 collective-permute-done.1.refs_2_
  16.9 0.0 collective-permute-done.2.refs_3_
  16.9 2.2 %layer.1 = (bf16[256,256]{1,0:T(8,128)(2,1)}, bf16[256,256]{1,0:T(8,128)(2,1)S(1)}, bf16[8,48,256]{2,1,0:T(8,128)(2,1)}) custom-call(s32[2,8]{1,0:T(2,128)S(1)} %get-tuple-element.14.cols_ref, s32[2]{0:T(128)S(1)} %get-tuple-element.15.counts_ref, bf16[2,8,128,128]{3,2,1,0:T(8,128)(2,1)S(1)} %get-tuple-element.16.vals_ref, ...), custom_call_target="tpu_custom_call" | custom-call | tf_op jit(solution)/shard_map/layer/pallas_call | solution.py:190
  19.1 3.7 %all-to-all-start.1 = ((bf16[8,48,256]{2,1,0:T(8,128)(2,1)}), bf16[8,48,256]{2,1,0:T(8,128)(2,1)S(1)}, u32[]{:S(2)}, u32[]{:S(2)}) async-start(bf16[8,48,256]{2,1,0:T(8,128)(2,1)} %get-tuple-element.20), calls=%async_computation.1 | async-start | bytes 393216 | tf_op jit(solution)/shard_map/all_to_all | solution.py:203
  22.8 1.2 %terms.1 = (f32[256,256]{1,0:T(8,128)S(1)}, bf16[512,256]{1,0:T(8,128)(2,1)S(1)}, f32[256,256]{1,0:T(8,128)S(1)}) custom-call(s32[2,8]{1,0:T(2,128)S(1)} %get-tuple-element.14.cols_ref, s32[2]{0:T(128)S(1)} %get-tuple-element.15.counts_ref, bf16[2,8,128,128]{3,2,1,0:T(8,128)(2,1)S(1)} %get-tuple-element.16.vals_ref, ...), custom_call_target="tpu_custom_call" | custom-call | tf_op jit(solution)/shard_map/terms/pallas_call | solution.py:207
  24.0 2.0 %collective-permute-start.3 = (bf16[512,256]{1,0:T(8,128)(2,1)S(1)}, bf16[512,256]{1,0:T(8,128)(2,1)S(1)}, u32[]{:S(2)}, u32[]{:S(2)}) collective-permute-start(bf16[512,256]{1,0:T(8,128)(2,1)S(1)} %get-tuple-element.23), channel_id=1, source_target_pairs={{0,1},{1,0},{2,3},{3,2},{4,5},{5,4},{6,7},{7,6},{8,9},{9,8},{10,11... | collective-permute-start | bytes 786440 | tf_op jit(solution)/shard_map/ppermute | solution.py:168
  26.0 3.0 %all-to-all-done.1.returned_ref = bf16[8,48,256]{2,1,0:T(8,128)(2,1)S(1)} async-done(((bf16[8,48,256]{2,1,0:T(8,128)(2,1)}), bf16[8,48,256]{2,1,0:T(8,128)(2,1)S(1)}, u32[]{:S(2)}, u32[]{:S(2)}) %all-to-all-start.1) | async-done | bytes 196640 | tf_op jit(solution)/shard_map/all_to_all | solution.py:203
  29.1 2.0 %collective-permute-start.5 = (bf16[32,256]{1,0:T(8,128)(2,1)S(1)}, bf16[32,256]{1,0:T(8,128)(2,1)S(1)}, u32[]{:S(2)}, u32[]{:S(2)}) collective-permute-start(bf16[32,256]{1,0:T(8,128)(2,1)S(1)} %slice_reduce_fusion.refs_0_), channel_id=1, source_target_pairs={{0,1},{1,0},{2,3},{3,2},{4,5},{5,4},{6,7},{7,6},{8,9},{9,8},{10,11... | collective-permute-start | bytes 49160 | tf_op jit(solution)/shard_map/ppermute | solution.py:168
  31.1 1.4 %collective-permute-start.6 = (bf16[32,256]{1,0:T(8,128)(2,1)S(1)}, bf16[32,256]{1,0:T(8,128)(2,1)S(1)}, u32[]{:S(2)}, u32[]{:S(2)}) collective-permute-start(bf16[32,256]{1,0:T(8,128)(2,1)S(1)} %slice_reduce_fusion.refs_0_), channel_id=1, source_target_pairs={{0,2},{1,3},{2,0},{3,1},{4,6},{5,7},{6,4},{7,5},{8,10},{9,11},{10,... | collective-permute-start | bytes 49160 | tf_op jit(solution)/shard_map/ppermute | solution.py:168
  32.5 1.0 %collective-permute-start.7 = (bf16[32,256]{1,0:T(8,128)(2,1)S(1)}, bf16[32,256]{1,0:T(8,128)(2,1)S(1)}, u32[]{:S(2)}, u32[]{:S(2)}) collective-permute-start(bf16[32,256]{1,0:T(8,128)(2,1)S(1)} %slice_reduce_fusion.refs_0_), channel_id=1, source_target_pairs={{0,3},{1,2},{2,1},{3,0},{4,7},{5,6},{6,5},{7,4},{8,11},{9,10},{10,... | collective-permute-start | bytes 49160 | tf_op jit(solution)/shard_map/ppermute | solution.py:168
  33.6 0.0 collective-permute-done.3.came_ref.refs_0_
  33.6 2.6 %collective-permute-start.4 = (bf16[256,256]{1,0:T(8,128)(2,1)S(1)}, bf16[256,256]{1,0:T(8,128)(2,1)S(1)}, u32[]{:S(2)}, u32[]{:S(2)}) collective-permute-start(bf16[256,256]{1,0:T(8,128)(2,1)S(1)} %relay.1.refs_4_), channel_id=1, source_target_pairs={{0,2},{1,3},{2,0},{3,1},{4,6},{5,7},{6,4},{7,5},{8,10},{9,11},{10,... | collective-permute-start | bytes 393224 | tf_op jit(solution)/shard_map/ppermute | solution.py:168
  36.2 0.0 collective-permute-done.5.refs_1_
  36.2 0.0 collective-permute-done.6.refs_2_
  36.2 2.1 %collective-permute-done.7.refs_3_ = bf16[32,256]{1,0:T(8,128)(2,1)S(1)} collective-permute-done((bf16[32,256]{1,0:T(8,128)(2,1)S(1)}, bf16[32,256]{1,0:T(8,128)(2,1)S(1)}, u32[]{:S(2)}, u32[]{:S(2)}) %collective-permute-start.7) | collective-permute-done | bytes 16416 | tf_op jit(solution)/shard_map/ppermute | solution.py:168
  38.3 0.5 %collective-permute-start.8 = (bf16[32,256]{1,0:T(8,128)(2,1)S(1)}, bf16[32,256]{1,0:T(8,128)(2,1)S(1)}, u32[]{:S(2)}, u32[]{:S(2)}) collective-permute-start(bf16[32,256]{1,0:T(8,128)(2,1)S(1)} %rep_sum.1.own_ref), channel_id=1, source_target_pairs={{0,16},{4,20},{8,24},{12,28},{16,0},{20,4},{24,8},{28,12},{1,17},{... | collective-permute-start | bytes 49160 | tf_op jit(solution)/shard_map/ppermute | solution.py:245
  38.8 3.3 %collective-permute-done.8.got_ref = bf16[32,256]{1,0:T(8,128)(2,1)S(1)} collective-permute-done((bf16[32,256]{1,0:T(8,128)(2,1)S(1)}, bf16[32,256]{1,0:T(8,128)(2,1)S(1)}, u32[]{:S(2)}, u32[]{:S(2)}) %collective-permute-start.8) | collective-permute-done | bytes 16416 | tf_op jit(solution)/shard_map/ppermute | solution.py:245
  42.1 0.5 collective-permute-start.9
  42.6 3.5 %collective-permute-done.9.got_ref = bf16[64,256]{1,0:T(8,128)(2,1)S(1)} collective-permute-done((bf16[64,256]{1,0:T(8,128)(2,1)S(1)}, bf16[64,256]{1,0:T(8,128)(2,1)S(1)}, u32[]{:S(2)}, u32[]{:S(2)}) %collective-permute-start.9) | collective-permute-done | bytes 32800 | tf_op jit(solution)/shard_map/ppermute | solution.py:245
  46.0 0.0 copy-start.3
  46.0 0.1 collective-permute-start.10
  46.1 1.2 %collective-permute-done.10.got_ref = bf16[128,256]{1,0:T(8,128)(2,1)S(1)} collective-permute-done((bf16[128,256]{1,0:T(8,128)(2,1)S(1)}, bf16[128,256]{1,0:T(8,128)(2,1)S(1)}, u32[]{:S(2)}, u32[]{:S(2)}) %collective-permute-start.10) | collective-permute-done | bytes 65568 | tf_op jit(solution)/shard_map/ppermute | solution.py:245
  47.4 0.7 %join.5 = f32[256,256]{1,0:T(8,128)} custom-call(bf16[128,256]{1,0:T(8,128)(2,1)S(1)} %join.4.own_ref, bf16[128,256]{1,0:T(8,128)(2,1)S(1)} %collective-permute-done.10.got_ref), custom_call_target="tpu_custom_call" | custom-call | flops 1 | bytes 1 | tf_op jit(solution)/shard_map/join/pallas_call | solution.py:246
  48.1 0.0 collective-permute-done.4.refs_1_
  48.1 1.0 %input_gradient.1 = bf16[256,256]{1,0:T(8,128)(2,1)} custom-call(s32[1,8,16]{2,1,0:T(8,128)S(1)} %copy-done.3, bf16[8,48,256]{2,1,0:T(8,128)(2,1)S(1)} %all-to-all-done.1.returned_ref, bf16[256,256]{1,0:T(8,128)(2,1)S(1)} %copy-done.1, f32[256,256]{1,0:T(8,128)S(1)} %get-tuple-element.22.own_ref, ...), custom_call_target="tpu_custom_call" | custom-call | flops 1000000000 | bytes 1 | tf_op jit(solution)/shard_map/input_gradient/pallas_call | solution.py:256
  (11 shorter events, 0.1 us)
Async XLA Ops:
  0.6 15.8 %collective-permute-start = (bf16[256,256]{1,0:T(8,128)(2,1)}, bf16[256,256]{1,0:T(8,128)(2,1)S(1)}, u32[]{:S(2)}, u32[]{:S(2)}) collective-permute-start(bf16[256,256]{1,0:T(8,128)(2,1)} %refs_0_.3), channel_id=1, source_target_pairs={{0,1},{1,0},{2,3},{3,2},{4,5},{5,4},{6,7},{7,6},{8,9},{9,8},{10,11... | collective-permute-start | bytes 393224 | tf_op jit(solution)/shard_map/ppermute | solution.py:168
  3.7 13.2 %collective-permute-start.1 = (bf16[256,256]{1,0:T(8,128)(2,1)}, bf16[256,256]{1,0:T(8,128)(2,1)S(1)}, u32[]{:S(2)}, u32[]{:S(2)}) collective-permute-start(bf16[256,256]{1,0:T(8,128)(2,1)} %refs_0_.3), channel_id=1, source_target_pairs={{0,2},{1,3},{2,0},{3,1},{4,6},{5,7},{6,4},{7,5},{8,10},{9,11},{10,... | collective-permute-start | bytes 393224 | tf_op jit(solution)/shard_map/ppermute | solution.py:168
  6.3 10.6 %collective-permute-start.2 = (bf16[256,256]{1,0:T(8,128)(2,1)}, bf16[256,256]{1,0:T(8,128)(2,1)S(1)}, u32[]{:S(2)}, u32[]{:S(2)}) collective-permute-start(bf16[256,256]{1,0:T(8,128)(2,1)} %refs_0_.3), channel_id=1, source_target_pairs={{0,3},{1,2},{2,1},{3,0},{4,7},{5,6},{6,5},{7,4},{8,11},{9,10},{10,... | collective-permute-start | bytes 393224 | tf_op jit(solution)/shard_map/ppermute | solution.py:168
  6.3 10.6 %copy-start.1 = (bf16[256,256]{1,0:T(8,128)(2,1)S(1)}, bf16[256,256]{1,0:T(8,128)(2,1)}, u32[]{:S(2)}) copy-start(bf16[256,256]{1,0:T(8,128)(2,1)} %weight_ref.3) | copy-start | bytes 393220
  6.3 10.6 %copy-start.2 = (bf16[256,128]{1,0:T(8,128)(2,1)S(1)}, bf16[256,128]{1,0:T(8,128)(2,1)}, u32[]{:S(2)}) copy-start(bf16[256,128]{1,0:T(8,128)(2,1)} %bnd_ref.1) | copy-start | bytes 196612
  7.6 9.3 %copy-start = (bf16[256,256]{1,0:T(8,128)(2,1)S(1)}, bf16[256,256]{1,0:T(8,128)(2,1)}, u32[]{:S(2)}) copy-start(bf16[256,256]{1,0:T(8,128)(2,1)} %refs_0_.3) | copy-start | bytes 393220
  19.1 10.0 %all-to-all-start.1 = ((bf16[8,48,256]{2,1,0:T(8,128)(2,1)}), bf16[8,48,256]{2,1,0:T(8,128)(2,1)S(1)}, u32[]{:S(2)}, u32[]{:S(2)}) async-start(bf16[8,48,256]{2,1,0:T(8,128)(2,1)} %get-tuple-element.20), calls=%async_computation.1 | async-start | bytes 393216 | tf_op jit(solution)/shard_map/all_to_all | solution.py:203
  24.0 9.6 %collective-permute-start.3 = (bf16[512,256]{1,0:T(8,128)(2,1)S(1)}, bf16[512,256]{1,0:T(8,128)(2,1)S(1)}, u32[]{:S(2)}, u32[]{:S(2)}) collective-permute-start(bf16[512,256]{1,0:T(8,128)(2,1)S(1)} %get-tuple-element.23), channel_id=1, source_target_pairs={{0,1},{1,0},{2,3},{3,2},{4,5},{5,4},{6,7},{7,6},{8,9},{9,8},{10,11... | collective-permute-start | bytes 786440 | tf_op jit(solution)/shard_map/ppermute | solution.py:168
  29.1 7.1 %collective-permute-start.5 = (bf16[32,256]{1,0:T(8,128)(2,1)S(1)}, bf16[32,256]{1,0:T(8,128)(2,1)S(1)}, u32[]{:S(2)}, u32[]{:S(2)}) collective-permute-start(bf16[32,256]{1,0:T(8,128)(2,1)S(1)} %slice_reduce_fusion.refs_0_), channel_id=1, source_target_pairs={{0,1},{1,0},{2,3},{3,2},{4,5},{5,4},{6,7},{7,6},{8,9},{9,8},{10,11... | collective-permute-start | bytes 49160 | tf_op jit(solution)/shard_map/ppermute | solution.py:168
  31.1 5.1 %collective-permute-start.6 = (bf16[32,256]{1,0:T(8,128)(2,1)S(1)}, bf16[32,256]{1,0:T(8,128)(2,1)S(1)}, u32[]{:S(2)}, u32[]{:S(2)}) collective-permute-start(bf16[32,256]{1,0:T(8,128)(2,1)S(1)} %slice_reduce_fusion.refs_0_), channel_id=1, source_target_pairs={{0,2},{1,3},{2,0},{3,1},{4,6},{5,7},{6,4},{7,5},{8,10},{9,11},{10,... | collective-permute-start | bytes 49160 | tf_op jit(solution)/shard_map/ppermute | solution.py:168
  32.5 5.7 %collective-permute-start.7 = (bf16[32,256]{1,0:T(8,128)(2,1)S(1)}, bf16[32,256]{1,0:T(8,128)(2,1)S(1)}, u32[]{:S(2)}, u32[]{:S(2)}) collective-permute-start(bf16[32,256]{1,0:T(8,128)(2,1)S(1)} %slice_reduce_fusion.refs_0_), channel_id=1, source_target_pairs={{0,3},{1,2},{2,1},{3,0},{4,7},{5,6},{6,5},{7,4},{8,11},{9,10},{10,... | collective-permute-start | bytes 49160 | tf_op jit(solution)/shard_map/ppermute | solution.py:168
  33.6 14.5 %collective-permute-start.4 = (bf16[256,256]{1,0:T(8,128)(2,1)S(1)}, bf16[256,256]{1,0:T(8,128)(2,1)S(1)}, u32[]{:S(2)}, u32[]{:S(2)}) collective-permute-start(bf16[256,256]{1,0:T(8,128)(2,1)S(1)} %relay.1.refs_4_), channel_id=1, source_target_pairs={{0,2},{1,3},{2,0},{3,1},{4,6},{5,7},{6,4},{7,5},{8,10},{9,11},{10,... | collective-permute-start | bytes 393224 | tf_op jit(solution)/shard_map/ppermute | solution.py:168
  38.3 3.8 %collective-permute-start.8 = (bf16[32,256]{1,0:T(8,128)(2,1)S(1)}, bf16[32,256]{1,0:T(8,128)(2,1)S(1)}, u32[]{:S(2)}, u32[]{:S(2)}) collective-permute-start(bf16[32,256]{1,0:T(8,128)(2,1)S(1)} %rep_sum.1.own_ref), channel_id=1, source_target_pairs={{0,16},{4,20},{8,24},{12,28},{16,0},{20,4},{24,8},{28,12},{1,17},{... | collective-permute-start | bytes 49160 | tf_op jit(solution)/shard_map/ppermute | solution.py:245
  42.1 3.9 %collective-permute-start.9 = (bf16[64,256]{1,0:T(8,128)(2,1)S(1)}, bf16[64,256]{1,0:T(8,128)(2,1)S(1)}, u32[]{:S(2)}, u32[]{:S(2)}) collective-permute-start(bf16[64,256]{1,0:T(8,128)(2,1)S(1)} %join.3.own_ref), channel_id=1, source_target_pairs={{0,8},{4,12},{8,0},{12,4},{16,24},{20,28},{24,16},{28,20},{1,9},{5... | collective-permute-start | bytes 98312 | tf_op jit(solution)/shard_map/ppermute | solution.py:245
  46.0 2.1 %copy-start.3 = (s32[1,8,16]{2,1,0:T(8,128)S(1)}, s32[1,8,16]{2,1,0:T(8,128)}, u32[]{:S(2)}) copy-start(s32[1,8,16]{2,1,0:T(8,128)} %index_ref.3) | copy-start | bytes 1540
  46.0 1.3 %collective-permute-start.10 = (bf16[128,256]{1,0:T(8,128)(2,1)S(1)}, bf16[128,256]{1,0:T(8,128)(2,1)S(1)}, u32[]{:S(2)}, u32[]{:S(2)}) collective-permute-start(bf16[128,256]{1,0:T(8,128)(2,1)S(1)} %join.4.own_ref), channel_id=1, source_target_pairs={{0,4},{4,0},{8,12},{12,8},{16,20},{20,16},{24,28},{28,24},{1,5},{5... | collective-permute-start | bytes 196616 | tf_op jit(solution)/shard_map/ppermute | solution.py:245

commit v8 on v7

v8 whole, which is shorter than its diff:
```python
import functools

import jax
import jax.numpy as jnp
from jax import lax
from jax.experimental import pallas as pl
from jax.experimental.pallas import tpu as pltpu
from jax.sharding import PartitionSpec as P

TILE = 128
F32 = jnp.float32
BF16 = jnp.bfloat16
VMEM = pl.BlockSpec(memory_space=pltpu.VMEM)
HBM = pl.BlockSpec(memory_space=pltpu.HBM)
SMEM = pl.BlockSpec(memory_space=pltpu.SMEM)


def dot(a, b, contract_a, contract_b):
    return lax.dot_general(
        a, b, (((contract_a,), (contract_b,)), ((), ())), preferred_element_type=F32
    )


def target(me, shift, count):
    return me ^ shift if count & (count - 1) == 0 else (me + shift) % count


def source(me, shift, count):
    return me ^ shift if count & (count - 1) == 0 else (me - shift + count) % count


def wanted_rows(index_ref, rows, order):
    flat = jnp.concatenate([index_ref[0, pl.ds(q, 1), :] for q in order], axis=1)
    at = lax.broadcasted_iota(jnp.int32, (rows, flat.shape[1]), 0)
    return jnp.where(at == flat, 1.0, 0.0).astype(BF16)


def pick_kernel(index_ref, features_ref, *refs):
    count = (len(refs) - 5) // 2
    loads, send_ref, keep_ref, loaded = refs[:count], refs[count], refs[count + 1], refs[count + 2 : -3]
    index, features, sems = refs[-3:]
    pairs = [(index_ref, index), (features_ref, features), *zip(loads, loaded)]
    copies = [pltpu.make_async_copy(*pair, sems.at[at]) for at, pair in enumerate(pairs)]
    for copy in copies:
        copy.start()
    here = lax.axis_index("dom")
    groups, each = index_ref.shape[1:]
    copies[0].wait()
    onehot = wanted_rows(index, features_ref.shape[0], [here ^ s for s in range(groups)])
    copies[1].wait()
    picked = dot(onehot, features[...], 0, 0).astype(BF16)
    for s in range(groups):
        to_ref = send_ref if s % 2 else keep_ref
        to_ref[s // 2 * each : (s // 2 + 1) * each, :] = picked[s * each : (s + 1) * each]
    for copy in copies[2:]:
        copy.wait()


def stage_kernel(each, keep_ref, came_ref, *outs):
    for j, out_ref in enumerate(outs):
        out_ref[:each, :] = keep_ref[j * each : (j + 1) * each, :]
        out_ref[each:, :] = came_ref[j * each : (j + 1) * each, :]


def weighted_stage_kernel(each, keep_ref, half_ref, came_ref, own_ref, share_ref, *refs):
    outs, summed = refs[:-1], refs[-1]
    pairs = len(outs) + 1
    summed[...] = half_ref[...] + came_ref[pairs * each :, :].astype(F32)
    share = summed.shape[0] // pairs
    chip = lax.axis_index("dom") // 2
    for j in range(pairs):
        to_ref = outs[j - 1] if j else own_ref
        to_ref[:each, :] = keep_ref[j * each : (j + 1) * each, :]
        to_ref[each : 2 * each, :] = came_ref[j * each : (j + 1) * each, :]
        part = summed[pl.ds(pl.multiple_of((chip ^ j) * share, share), share), :]
        if j:
            to_ref[2 * each :, :] = part.astype(BF16)
        else:
            share_ref[...] = part


def share_sum_kernel(each, share_ref, *refs):
    total = share_ref[...]
    for ref in refs[:-1]:
        total = total + ref[2 * each :, :].astype(F32)
    refs[-1][...] = total.astype(BF16)


def half_kernel(*refs):
    shares, out_ref, whole = refs[:-2], refs[-2], refs[-1]
    share = shares[0].shape[0]
    chip = lax.axis_index("dom") // 2
    for j, ref in enumerate(shares):
        whole[pl.ds(pl.multiple_of((chip ^ j) * share, share), share), :] = ref[...].astype(F32)
    out_ref[...] = whole[...].astype(BF16)


def live_tiles(counts_ref, vals_ref, t):
    return [
        jnp.where(k < counts_ref[t], vals_ref[t, k], jnp.zeros_like(vals_ref[t, k]))
        for k in range(vals_ref.shape[1])
    ]


def layer_kernel(rep, pairs, cols_ref, counts_ref, vals_ref, bnd_ref, cot_ref, weight_ref, *refs):
    blocks = refs[:rep]
    received_refs = refs[rep : rep + pairs]
    out_ref, grad_ref, send_ref, keep_ref, half_ref, panel, received, boundary, partial = refs[rep + pairs :]
    here = lax.axis_index("dom")
    me = lax.axis_index("rep")
    tiles, slots = cols_ref.shape
    for shift, block in enumerate(blocks):
        owner = source(me, shift, rep)
        for t in range(tiles):
            panel[owner * tiles + t] = block[t * TILE : (t + 1) * TILE, :]
    each = received_refs[0].shape[0] // 2
    groups = 2 * pairs

    def rows_of(group):
        return pl.ds(pl.multiple_of(group * each, each), each)

    for o in range(groups):
        received[rows_of(here ^ o), :] = received_refs[o // 2][o % 2 * each : (o % 2 + 1) * each, :]
    forward = []
    backward = []
    for t in range(tiles):
        live = live_tiles(counts_ref, vals_ref, t)
        chosen = jnp.concatenate([panel[cols_ref[t, k]] for k in range(slots)], axis=0)
        forward.append(dot(jnp.concatenate(live, axis=1), chosen, 1, 0))
        backward.append(dot(jnp.concatenate(live, axis=0), chosen, 0, 0))
    outside = dot(bnd_ref[...], received[...], 1, 0)
    mixed = jnp.concatenate(forward, axis=0) + outside
    turned = (jnp.concatenate(backward, axis=0) + outside).astype(BF16)
    high = mixed.astype(BF16)
    low = (mixed - high.astype(F32)).astype(BF16)
    weight = weight_ref[...]
    pre = dot(high, weight, 1, 0) + dot(low, weight, 1, 0)
    sig = jax.nn.sigmoid(pre)
    out_ref[...] = (pre * sig).astype(BF16)
    grad = (cot_ref[...].astype(F32) * sig * (1.0 + pre * (1.0 - sig))).astype(BF16)
    grad_ref[...] = grad
    boundary[...] = dot(bnd_ref[...], grad, 0, 0).astype(BF16)
    for s in range(groups):
        to_ref = send_ref if s % 2 else keep_ref
        to_ref[s // 2 * each : (s // 2 + 1) * each, :] = boundary[rows_of(here ^ s), :]
    partial[...] = dot(turned, grad, 0, 0)
    half = half_ref.shape[0]
    mine = here % 2
    half_ref[...] = partial[pl.ds(pl.multiple_of(mine * half, half), half), :]
    send_ref[pairs * each :, :] = partial[pl.ds(pl.multiple_of((1 - mine) * half, half), half), :].astype(BF16)


def terms_kernel(rep, layout, cols_ref, counts_ref, vals_ref, grad_ref, *refs):
    outs, terms = refs[:-1], refs[-1]
    me = lax.axis_index("rep")
    tiles, slots = cols_ref.shape
    terms[...] = jnp.zeros_like(terms)
    for t in range(tiles):
        stacked = jnp.concatenate(live_tiles(counts_ref, vals_ref, t), axis=0)
        parts = dot(stacked, grad_ref[t * TILE : (t + 1) * TILE, :], 1, 0)
        for k in range(slots):
            terms[cols_ref[t, k]] += parts[k * TILE : (k + 1) * TILE]
    for out_ref, shifts in zip(outs, layout):
        for at, shift in enumerate(shifts):
            owner = target(me, shift, rep)
            for t in range(tiles):
                row = (at * tiles + t) * TILE
                out_ref[row : row + TILE, :] = terms[owner * tiles + t].astype(out_ref.dtype)


def relay_kernel(far_ref, came_ref, out_ref):
    rows = far_ref.shape[0]
    out_ref[...] = (far_ref[...] + came_ref[rows:, :].astype(F32)).astype(BF16)


def rep_sum_kernel(*refs):
    chunk, one, two, three = [ref[...].astype(F32) for ref in refs[:4]]
    refs[-1][...] = ((chunk + two) + (one + three)).astype(BF16)


def join_kernel(bit, own_ref, got_ref, out_ref):
    own, got = own_ref[...], got_ref[...]
    half = own.shape[0]
    upper = lax.rem(lax.axis_index("dom") // bit, 2) == 1
    out_ref[:half, :] = jnp.where(upper, got, own).astype(out_ref.dtype)
    out_ref[half:, :] = jnp.where(upper, own, got).astype(out_ref.dtype)


def final_kernel(pairs, index_ref, weight_ref, own_ref, *refs):
    returned, arrived, out_ref = refs[:pairs], refs[pairs:-1], refs[-1]
    groups, each = index_ref.shape[1:]
    here = lax.axis_index("dom")
    onehot = wanted_rows(index_ref, own_ref.shape[0], [here ^ o for o in range(groups)])
    returned = jnp.concatenate([ref[: 2 * each, :] for ref in returned], axis=0)
    total = own_ref[...] + dot(onehot, returned, 1, 0)
    for term in arrived:
        total = total + term[: own_ref.shape[0], :].astype(F32)
    out_ref[...] = dot(total.astype(BF16), weight_ref[...], 1, 1).astype(BF16)


def body(features, weight, tile_cols, tile_vals, tile_counts, send_rows, bnd_adj, cotangent):
    rows, feats = features.shape
    width = weight.shape[1]
    tiles, slots = tile_cols.shape
    groups, each = send_rows.shape[1], send_rows.shape[2]
    rep = lax.axis_size("rep")
    share = feats // groups
    pairs = groups // 2
    params = pltpu.CompilerParams(vmem_limit_bytes=40 * 1024 * 1024)

    def shifted(value, shift):
        return lax.ppermute(value, "rep", [(i, target(i, shift, rep)) for i in range(rep)])

    def across(value, bits):
        return lax.ppermute(value, "dom", [(i, i ^ bits) for i in range(groups)])

    def call(kernel, name, outs, operands, scratch=()):
        return pl.pallas_call(
            kernel,
            out_shape=outs,
            in_specs=[VMEM] * len(operands),
            out_specs=[VMEM] * len(outs),
            scratch_shapes=scratch,
            compiler_params=params,
            cost_estimate=pl.CostEstimate(flops=1, bytes_accessed=1, transcendentals=0),
            name=name,
        )(*operands)

    def shape(high, kind=BF16, wide=width):
        return jax.ShapeDtypeStruct((high, wide), kind)

    blocks = [features] + [shifted(features, shift) for shift in range(1, rep)]
    loads = [tile_vals, cotangent, tile_cols, tile_counts]
    send, keep, tile_vals, cotangent, tile_cols, tile_counts = pl.pallas_call(
        pick_kernel,
        out_shape=[
            *[shape(pairs * each, BF16, feats)] * 2,
            *[jax.ShapeDtypeStruct(load.shape, load.dtype) for load in loads],
        ],
        in_specs=[HBM] * (2 + len(loads)),
        out_specs=[VMEM] * (2 + len(loads)),
        scratch_shapes=[
            pltpu.VMEM(send_rows.shape, jnp.int32),
            pltpu.VMEM((rows, feats), BF16),
            pltpu.SemaphoreType.DMA((2 + len(loads),)),
        ],
        compiler_params=params,
        name="pick_rows",
    )(*[pltpu.with_memory_space_constraint(x, pltpu.HBM) for x in (send_rows, features, *loads)])
    received = call(
        functools.partial(stage_kernel, each),
        "pair_rows",
        [shape(2 * each, BF16, feats)] * pairs,
        (keep, across(send, 1)),
    )
    received = [received[0]] + [across(received[j], 2 * j) for j in range(1, pairs)]
    half = feats // 2
    output, grad, send, keep, mine = pl.pallas_call(
        functools.partial(layer_kernel, rep, pairs),
        out_shape=[
            shape(rows),
            shape(rows),
            shape(pairs * each + half),
            shape(pairs * each),
            shape(half, F32),
        ],
        in_specs=[SMEM] * 2 + [VMEM] * (4 + rep + pairs),
        out_specs=[VMEM] * 5,
        scratch_shapes=[
            pltpu.VMEM((rep * tiles, TILE, feats), BF16),
            pltpu.VMEM((groups * each, feats), BF16),
            pltpu.VMEM((groups * each, width), BF16),
            pltpu.VMEM((feats, width), F32),
        ],
        compiler_params=params,
        name="layer",
    )(tile_cols, tile_counts, tile_vals, bnd_adj, cotangent, weight, *blocks, *received)
    own_rows, own_share, *parts = call(
        functools.partial(weighted_stage_kernel, each),
        "pair_gradients",
        [shape(2 * each), shape(share, F32)] + [shape(2 * each + share)] * (pairs - 1),
        (keep, mine, across(send, 1)),
        [pltpu.VMEM((half, width), F32)],
    )
    parts = [across(part, 2 * j) for j, part in enumerate(parts, 1)]
    returned = [own_rows] + parts
    relayed = rep == 4
    layout = [(0,), (1, 3), (2,)] if relayed else [(shift,) for shift in range(rep)]
    kinds = [F32, BF16, F32] if relayed else [F32] + [BF16] * (rep - 1)
    own, *sends = pl.pallas_call(
        functools.partial(terms_kernel, rep, layout),
        out_shape=[
            jax.ShapeDtypeStruct((len(shifts) * rows, width), kind)
            for shifts, kind in zip(layout, kinds)
        ],
        in_specs=[SMEM] * 2 + [VMEM] * 2,
        out_specs=[VMEM] * len(layout),
        scratch_shapes=[pltpu.VMEM((rep * tiles, TILE, width), F32)],
        compiler_params=params,
        name="terms",
    )(tile_cols, tile_counts, tile_vals, grad)
    (chunk,) = call(
        functools.partial(share_sum_kernel, each), "share_sum", [shape(share)], (own_share, *parts)
    )
    if relayed:
        came = shifted(sends[0], 1)
        (relay,) = call(relay_kernel, "relay", [shape(rows)], (sends[1], came))
        arrived = [came, shifted(relay, 2)]
        small = [shifted(chunk, shift) for shift in (1, 2, 3)]
        (piece,) = call(rep_sum_kernel, "rep_sum", [shape(share)], (chunk, *small, relay))
    else:
        arrived = [shifted(send, shift) for shift, send in enumerate(sends, 1)]
        piece = jnp.sum(lax.all_gather(chunk, "rep").astype(F32), axis=0).astype(BF16)
    pieces = [piece] + [across(piece, 2 * j) for j in range(1, pairs)]
    (piece,) = call(half_kernel, "half", [shape(half)], pieces, [pltpu.VMEM((half, width), F32)])
    (grad_weight,) = call(
        functools.partial(join_kernel, 1), "join", [shape(feats, F32)], (piece, across(piece, 1))
    )
    grad_features = pl.pallas_call(
        functools.partial(final_kernel, pairs),
        out_shape=jax.ShapeDtypeStruct((rows, feats), BF16),
        in_specs=[VMEM] * (3 + pairs + len(arrived)),
        out_specs=VMEM,
        compiler_params=params,
        cost_estimate=pl.CostEstimate(flops=1_000_000_000, bytes_accessed=1, transcendentals=0),
        name="input_gradient",
    )(send_rows, weight, own, *returned, *arrived)
    return (output, grad_features, grad_weight)


def solution(mesh):
    placed = (
        P(("dom", "rep"), None),
        P(),
        P(("dom", "rep"), None),
        P(("dom", "rep"), None, None, None),
        P(("dom", "rep")),
        P(("dom", "rep"), None, None),
        P(("dom", "rep"), None),
        P(("dom", "rep"), None),
    )
    return jax.shard_map(
        body,
        mesh=mesh,
        in_specs=placed,
        out_specs=(P(("dom", "rep"), None), P(("dom", "rep"), None), P()),
        check_vma=False,
    )
```

time: 49.4 us -> 47.7 us (0.966)
  blocking collectives: 8.86 us -> 0 us
  starting transfers between devices: 19.5 us -> 27.8 us
  waiting for transfers between devices: 13.5 us -> 12.6 us
    ppermute x3 -> x12, starting transfers between devices: 1.04 us -> 13.1 us  [across(): return lax.ppermute(value, 'dom', [(i, i ^ bits) for i in range(groups)])]
    all_to_all x1 -> x0, blocking collectives: 8.86 us -> none  [body(): lax.all_to_all(outgoing, 'dom', split_axis=0, concat_axis=0, tiled=True)]
    all_to_all x1 -> x0, starting transfers between devices: 3.72 us -> none  [body(): lax.all_to_all(message, 'dom', split_axis=0, concat_axis=0, tiled=True)]
    all_to_all x1 -> x0, waiting for transfers between devices: 3.04 us -> none  [body(): lax.all_to_all(message, 'dom', split_axis=0, concat_axis=0, tiled=True)]
    ppermute x8, waiting for transfers between devices: 2.51 us -> 3.92 us  [shifted(): lax.ppermute(value, 'rep', [(i, target(i, shift, rep)) for i in range(rep)])]
    ppermute x3 -> x12, waiting for transfers between devices: 7.99 us -> 8.72 us  [across(): return lax.ppermute(value, 'dom', [(i, i ^ bits) for i in range(groups)])]
    pallas_call x8 -> x10, Pallas kernels: 5.31 us -> 5.21 us  [the longest x1 2.02 us: body(): pl.pallas_call(functools.partial(layer_kernel, rep, pairs), out_shape=[sh...]
  transfers between devices with their start and end apart: 12 -> 20, of which waited for: 6 -> 11; matrix products, arithmetic and copies ran while one was open for 0% -> 0% of each run, Pallas kernels for 7% -> 5%
where the time goes in v8:
time: 47.7 us; the launch traced here: 47.5 us
  starting transfers between devices  27.8 us (58%)
  waiting for transfers between devices  12.6 us (26%)
  Pallas kernels  6.37 us (13%)
  between operations  0.75 us (2%)
    ppermute x8, starting transfers between devices, shifted(): lax.ppermute(value, 'rep', [(i, target(i, shift, rep)) for i in range(rep)])  14.7 us
    ppermute x12, starting transfers between devices, across(): return lax.ppermute(value, 'dom', [(i, i ^ bits) for i in range(groups)])  13.1 us
    ppermute x12, waiting for transfers between devices, across(): return lax.ppermute(value, 'dom', [(i, i ^ bits) for i in range(groups)])  8.72 us
    ppermute x8, waiting for transfers between devices, shifted(): lax.ppermute(value, 'rep', [(i, target(i, shift, rep)) for i in range(rep)])  3.92 us
    pallas_call x1, Pallas kernels, body(): pl.pallas_call(functools.partial(layer_kernel, rep, pairs), out_shape=[sh...  2.02 us
    pallas_call x1, Pallas kernels, body(): pl.pallas_call(pick_kernel, out_shape=[*[shape(pairs * each, BF16, feats)...  1.3 us
    pallas_call x1, Pallas kernels, body(): pl.pallas_call(functools.partial(terms_kernel, rep, layout), out_shape=[j...  1.16 us
    pallas_call x1, Pallas kernels, body(): pl.pallas_call(functools.partial(final_kernel, pairs), out_shape=jax.Shap...  1.05 us
  transfers between devices with their start and end apart: 20, of which 11 were waited for; matrix products, arithmetic and copies ran while one was open for 0% of the time, Pallas kernels for 5%

profile of v8, /device:TPU:0, one launch (start us, length us, event | category | flops | bytes accessed | tf_op | source)
XLA Modules:
  0.0 47.5 jit_solution(15491594790921943258)
XLA Ops:
  0.6 4.1 %collective-permute-start.1 = (bf16[256,256]{1,0:T(8,128)(2,1)}, bf16[256,256]{1,0:T(8,128)(2,1)S(1)}, u32[]{:S(2)}, u32[]{:S(2)}) collective-permute-start(bf16[256,256]{1,0:T(8,128)(2,1)} %refs_0_.3), channel_id=1, source_target_pairs={{0,2},{1,3},{2,0},{3,1},{4,6},{5,7},{6,4},{7,5},{8,10},{9,11},{10,... | collective-permute-start | bytes 393224 | tf_op jit(solution)/shard_map/ppermute | solution.py:212
  4.7 1.6 %collective-permute-start = (bf16[256,256]{1,0:T(8,128)(2,1)}, bf16[256,256]{1,0:T(8,128)(2,1)S(1)}, u32[]{:S(2)}, u32[]{:S(2)}) collective-permute-start(bf16[256,256]{1,0:T(8,128)(2,1)} %refs_0_.3), channel_id=1, source_target_pairs={{0,1},{1,0},{2,3},{3,2},{4,5},{5,4},{6,7},{7,6},{8,9},{9,8},{10,11... | collective-permute-start | bytes 393224 | tf_op jit(solution)/shard_map/ppermute | solution.py:212
  6.3 1.3 %pick_rows.1 = (bf16[64,256]{1,0:T(8,128)(2,1)S(1)}, bf16[64,256]{1,0:T(8,128)(2,1)S(1)}, bf16[2,8,128,128]{3,2,1,0:T(8,128)(2,1)S(1)}, bf16[256,256]{1,0:T(8,12...) custom-call(s32[1,8,16]{2,1,0:T(8,128)} %index_ref.3, bf16[256,256]{1,0:T(8,128)(2,1)} %refs_0_.3, ...), custom_call_target="tpu_custom_call" | custom-call | tf_op jit(solution)/shard_map/pick_rows/pallas_call | solution.py:234
  7.7 1.2 %collective-permute-done.3.came_ref = bf16[64,256]{1,0:T(8,128)(2,1)S(1)} collective-permute-done((bf16[64,256]{1,0:T(8,128)(2,1)S(1)}, bf16[64,256]{1,0:T(8,128)(2,1)S(1)}, u32[]{:S(2)}, u32[]{:S(2)}) %collective-permute-start.3) | collective-permute-done | bytes 32800 | tf_op jit(solution)/shard_map/ppermute | solution.py:215
  8.9 1.7 %collective-permute-start.4 = (bf16[32,256]{1,0:T(8,128)(2,1)S(1)}, bf16[32,256]{1,0:T(8,128)(2,1)S(1)}, u32[]{:S(2)}, u32[]{:S(2)}) collective-permute-start(bf16[32,256]{1,0:T(8,128)(2,1)S(1)} %get-tuple-element.33), channel_id=1, source_target_pairs={{0,8},{4,12},{8,0},{12,4},{16,24},{20,28},{24,16},{28,20},{1,9},{5... | collective-permute-start | bytes 49160 | tf_op jit(solution)/shard_map/ppermute | solution.py:215
  10.6 1.5 %collective-permute-start.5 = (bf16[32,256]{1,0:T(8,128)(2,1)S(1)}, bf16[32,256]{1,0:T(8,128)(2,1)S(1)}, u32[]{:S(2)}, u32[]{:S(2)}) collective-permute-start(bf16[32,256]{1,0:T(8,128)(2,1)S(1)} %get-tuple-element.34), channel_id=1, source_target_pairs={{0,16},{4,20},{8,24},{12,28},{16,0},{20,4},{24,8},{28,12},{1,17},{... | collective-permute-start | bytes 49160 | tf_op jit(solution)/shard_map/ppermute | solution.py:215
  12.1 0.5 %collective-permute-done.4.refs_5_ = bf16[32,256]{1,0:T(8,128)(2,1)S(1)} collective-permute-done((bf16[32,256]{1,0:T(8,128)(2,1)S(1)}, bf16[32,256]{1,0:T(8,128)(2,1)S(1)}, u32[]{:S(2)}, u32[]{:S(2)}) %collective-permute-start.4) | collective-permute-done | bytes 16416 | tf_op jit(solution)/shard_map/ppermute | solution.py:215
  12.7 2.6 %collective-permute-start.6 = (bf16[32,256]{1,0:T(8,128)(2,1)S(1)}, bf16[32,256]{1,0:T(8,128)(2,1)S(1)}, u32[]{:S(2)}, u32[]{:S(2)}) collective-permute-start(bf16[32,256]{1,0:T(8,128)(2,1)S(1)} %get-tuple-element.35), channel_id=1, source_target_pairs={{0,24},{4,28},{8,16},{12,20},{16,8},{20,12},{24,0},{28,4},{1,25},{... | collective-permute-start | bytes 49160 | tf_op jit(solution)/shard_map/ppermute | solution.py:215
  15.3 2.0 %collective-permute-done.6.refs_7_ = bf16[32,256]{1,0:T(8,128)(2,1)S(1)} collective-permute-done((bf16[32,256]{1,0:T(8,128)(2,1)S(1)}, bf16[32,256]{1,0:T(8,128)(2,1)S(1)}, u32[]{:S(2)}, u32[]{:S(2)}) %collective-permute-start.6) | collective-permute-done | bytes 16416 | tf_op jit(solution)/shard_map/ppermute | solution.py:215
  17.3 2.0 %layer.1 = (bf16[256,256]{1,0:T(8,128)(2,1)}, bf16[256,256]{1,0:T(8,128)(2,1)S(1)}, bf16[192,256]{1,0:T(8,128)(2,1)S(1)}, bf16[64,256]{1,0:T(8,128)(2,1)S(1)}, f32[128,256]{1,0:T(8,128)S(1)}) custom-call(s32[2,8]{1,0:T(2,128)S(1)} %get-tuple-element.26.cols_ref, s32[2]{0:T(128)S(1)} %get-tuple-element.27.counts_ref, ...), custom_call_target="tpu_custom_call" | custom-call | tf_op jit(solution)/shard_map/layer/pallas_call | solution.py:258
  19.4 1.2 %terms.1 = (f32[256,256]{1,0:T(8,128)S(1)}, bf16[512,256]{1,0:T(8,128)(2,1)S(1)}, f32[256,256]{1,0:T(8,128)S(1)}) custom-call(s32[2,8]{1,0:T(2,128)S(1)} %get-tuple-element.26.cols_ref, s32[2]{0:T(128)S(1)} %get-tuple-element.27.counts_ref, bf16[2,8,128,128]{3,2,1,0:T(8,128)(2,1)S(1)} %get-tuple-element.28.vals_ref, ...), custom_call_target="tpu_custom_call" | custom-call | tf_op jit(solution)/shard_map/terms/pallas_call | solution.py:290
  20.5 0.9 %collective-permute-start.11 = (bf16[512,256]{1,0:T(8,128)(2,1)S(1)}, bf16[512,256]{1,0:T(8,128)(2,1)S(1)}, u32[]{:S(2)}, u32[]{:S(2)}) collective-permute-start(bf16[512,256]{1,0:T(8,128)(2,1)S(1)} %get-tuple-element.46), channel_id=1, source_target_pairs={{0,1},{1,0},{2,3},{3,2},{4,5},{5,4},{6,7},{7,6},{8,9},{9,8},{10,11... | collective-permute-start | bytes 786440 | tf_op jit(solution)/shard_map/ppermute | solution.py:212
  21.5 1.3 %collective-permute-done.7.came_ref = bf16[192,256]{1,0:T(8,128)(2,1)S(1)} collective-permute-done((bf16[192,256]{1,0:T(8,128)(2,1)S(1)}, bf16[192,256]{1,0:T(8,128)(2,1)S(1)}, u32[]{:S(2)}, u32[]{:S(2)}) %collective-permute-start.7) | collective-permute-done | bytes 98336 | tf_op jit(solution)/shard_map/ppermute | solution.py:215
  22.8 1.6 %collective-permute-start.8 = (bf16[64,256]{1,0:T(8,128)(2,1)S(1)}, bf16[64,256]{1,0:T(8,128)(2,1)S(1)}, u32[]{:S(2)}, u32[]{:S(2)}) collective-permute-start(bf16[64,256]{1,0:T(8,128)(2,1)S(1)} %get-tuple-element.43), channel_id=1, source_target_pairs={{0,8},{4,12},{8,0},{12,4},{16,24},{20,28},{24,16},{28,20},{1,9},{5... | collective-permute-start | bytes 98312 | tf_op jit(solution)/shard_map/ppermute | solution.py:215
  24.4 1.5 %collective-permute-start.9 = (bf16[64,256]{1,0:T(8,128)(2,1)S(1)}, bf16[64,256]{1,0:T(8,128)(2,1)S(1)}, u32[]{:S(2)}, u32[]{:S(2)}) collective-permute-start(bf16[64,256]{1,0:T(8,128)(2,1)S(1)} %get-tuple-element.44), channel_id=1, source_target_pairs={{0,16},{4,20},{8,24},{12,28},{16,0},{20,4},{24,8},{28,12},{1,17},{... | collective-permute-start | bytes 98312 | tf_op jit(solution)/shard_map/ppermute | solution.py:215
  25.9 0.5 collective-permute-start.10
  26.3 1.1 %collective-permute-done.11.came_ref.refs_4_ = bf16[512,256]{1,0:T(8,128)(2,1)S(1)} collective-permute-done((bf16[512,256]{1,0:T(8,128)(2,1)S(1)}, bf16[512,256]{1,0:T(8,128)(2,1)S(1)}, u32[]{:S(2)}, u32[]{:S(2)}) %collective-permute-start.11) | collective-permute-done | bytes 262176 | tf_op jit(solution)/shard_map/ppermute | solution.py:212
  27.5 3.6 %collective-permute-start.12 = (bf16[256,256]{1,0:T(8,128)(2,1)S(1)}, bf16[256,256]{1,0:T(8,128)(2,1)S(1)}, u32[]{:S(2)}, u32[]{:S(2)}) collective-permute-start(bf16[256,256]{1,0:T(8,128)(2,1)S(1)} %relay.1.refs_4_), channel_id=1, source_target_pairs={{0,2},{1,3},{2,0},{3,1},{4,6},{5,7},{6,4},{7,5},{8,10},{9,11},{10,... | collective-permute-start | bytes 393224 | tf_op jit(solution)/shard_map/ppermute | solution.py:212
  31.1 2.6 %collective-permute-start.15 = (bf16[32,256]{1,0:T(8,128)(2,1)S(1)}, bf16[32,256]{1,0:T(8,128)(2,1)S(1)}, u32[]{:S(2)}, u32[]{:S(2)}) collective-permute-start(bf16[32,256]{1,0:T(8,128)(2,1)S(1)} %share_sum.1.refs_0_), channel_id=1, source_target_pairs={{0,3},{1,2},{2,1},{3,0},{4,7},{5,6},{6,5},{7,4},{8,11},{9,10},{10,... | collective-permute-start | bytes 49160 | tf_op jit(solution)/shard_map/ppermute | solution.py:212
  33.8 0.6 %collective-permute-start.14 = (bf16[32,256]{1,0:T(8,128)(2,1)S(1)}, bf16[32,256]{1,0:T(8,128)(2,1)S(1)}, u32[]{:S(2)}, u32[]{:S(2)}) collective-permute-start(bf16[32,256]{1,0:T(8,128)(2,1)S(1)} %share_sum.1.refs_0_), channel_id=1, source_target_pairs={{0,2},{1,3},{2,0},{3,1},{4,6},{5,7},{6,4},{7,5},{8,10},{9,11},{10,... | collective-permute-start | bytes 49160 | tf_op jit(solution)/shard_map/ppermute | solution.py:212
  34.3 1.3 %collective-permute-start.13 = (bf16[32,256]{1,0:T(8,128)(2,1)S(1)}, bf16[32,256]{1,0:T(8,128)(2,1)S(1)}, u32[]{:S(2)}, u32[]{:S(2)}) collective-permute-start(bf16[32,256]{1,0:T(8,128)(2,1)S(1)} %share_sum.1.refs_0_), channel_id=1, source_target_pairs={{0,1},{1,0},{2,3},{3,2},{4,5},{5,4},{6,7},{7,6},{8,9},{9,8},{10,11... | collective-permute-start | bytes 49160 | tf_op jit(solution)/shard_map/ppermute | solution.py:212
  35.6 1.3 %collective-permute-done.15.refs_3_ = bf16[32,256]{1,0:T(8,128)(2,1)S(1)} collective-permute-done((bf16[32,256]{1,0:T(8,128)(2,1)S(1)}, bf16[32,256]{1,0:T(8,128)(2,1)S(1)}, u32[]{:S(2)}, u32[]{:S(2)}) %collective-permute-start.15) | collective-permute-done | bytes 16416 | tf_op jit(solution)/shard_map/ppermute | solution.py:212
  36.9 1.5 %collective-permute-done.14.refs_2_ = bf16[32,256]{1,0:T(8,128)(2,1)S(1)} collective-permute-done((bf16[32,256]{1,0:T(8,128)(2,1)S(1)}, bf16[32,256]{1,0:T(8,128)(2,1)S(1)}, u32[]{:S(2)}, u32[]{:S(2)}) %collective-permute-start.14) | collective-permute-done | bytes 16416 | tf_op jit(solution)/shard_map/ppermute | solution.py:212
  38.4 1.9 %collective-permute-start.18 = (bf16[32,256]{1,0:T(8,128)(2,1)S(1)}, bf16[32,256]{1,0:T(8,128)(2,1)S(1)}, u32[]{:S(2)}, u32[]{:S(2)}) collective-permute-start(bf16[32,256]{1,0:T(8,128)(2,1)S(1)} %rep_sum.1.refs_0_), channel_id=1, source_target_pairs={{0,24},{4,28},{8,16},{12,20},{16,8},{20,12},{24,0},{28,4},{1,25},{... | collective-permute-start | bytes 49160 | tf_op jit(solution)/shard_map/ppermute | solution.py:215
  40.3 0.3 collective-permute-start.17
  40.7 1.3 %collective-permute-start.16 = (bf16[32,256]{1,0:T(8,128)(2,1)S(1)}, bf16[32,256]{1,0:T(8,128)(2,1)S(1)}, u32[]{:S(2)}, u32[]{:S(2)}) collective-permute-start(bf16[32,256]{1,0:T(8,128)(2,1)S(1)} %rep_sum.1.refs_0_), channel_id=1, source_target_pairs={{0,8},{4,12},{8,0},{12,4},{16,24},{20,28},{24,16},{28,20},{1,9},{5... | collective-permute-start | bytes 49160 | tf_op jit(solution)/shard_map/ppermute | solution.py:215
  42.0 1.1 %collective-permute-done.18.refs_3_ = bf16[32,256]{1,0:T(8,128)(2,1)S(1)} collective-permute-done((bf16[32,256]{1,0:T(8,128)(2,1)S(1)}, bf16[32,256]{1,0:T(8,128)(2,1)S(1)}, u32[]{:S(2)}, u32[]{:S(2)}) %collective-permute-start.18) | collective-permute-done | bytes 16416 | tf_op jit(solution)/shard_map/ppermute | solution.py:215
  43.1 1.0 %collective-permute-done.17.refs_2_ = bf16[32,256]{1,0:T(8,128)(2,1)S(1)} collective-permute-done((bf16[32,256]{1,0:T(8,128)(2,1)S(1)}, bf16[32,256]{1,0:T(8,128)(2,1)S(1)}, u32[]{:S(2)}, u32[]{:S(2)}) %collective-permute-start.17) | collective-permute-done | bytes 16416 | tf_op jit(solution)/shard_map/ppermute | solution.py:215
  44.1 0.3 collective-permute-done.16.refs_1_
  44.5 1.2 %collective-permute-done.19.got_ref = bf16[128,256]{1,0:T(8,128)(2,1)S(1)} collective-permute-done((bf16[128,256]{1,0:T(8,128)(2,1)S(1)}, bf16[128,256]{1,0:T(8,128)(2,1)S(1)}, u32[]{:S(2)}, u32[]{:S(2)}) %collective-permute-start.19) | collective-permute-done | bytes 65568 | tf_op jit(solution)/shard_map/ppermute | solution.py:215
  45.8 0.7 %join.1 = f32[256,256]{1,0:T(8,128)} custom-call(bf16[128,256]{1,0:T(8,128)(2,1)S(1)} %half.1.own_ref, bf16[128,256]{1,0:T(8,128)(2,1)S(1)} %collective-permute-done.19.got_ref), custom_call_target="tpu_custom_call" | custom-call | flops 1 | bytes 1 | tf_op jit(solution)/shard_map/join/pallas_call | solution.py:218
  46.5 1.1 %input_gradient.1 = bf16[256,256]{1,0:T(8,128)(2,1)} custom-call(s32[1,8,16]{2,1,0:T(8,128)S(1)} %copy-done.3, bf16[256,256]{1,0:T(8,128)(2,1)S(1)} %copy-done.1, f32[256,256]{1,0:T(8,128)S(1)} %get-tuple-element.38.own_ref, bf16[32,256]{1,0:T(8,128)(2,1)S(1)} %get-tuple-element.42.refs_0_, bf16[64,256]{1,0:T(8,128)(2,1)S(1)} %collective-permute-done.8.refs_1_.refs_0_, ...), custom_call_target="tpu_custom_call" | custom-call | flops 1000000000 | bytes 1 | tf_op jit(solution)/shard_map/input_gradient/pallas_call | solution.py:319
  (27 shorter events, 0.3 us)
Async XLA Ops:
  0.6 16.7 %collective-permute-start.1 = (bf16[256,256]{1,0:T(8,128)(2,1)}, bf16[256,256]{1,0:T(8,128)(2,1)S(1)}, u32[]{:S(2)}, u32[]{:S(2)}) collective-permute-start(bf16[256,256]{1,0:T(8,128)(2,1)} %refs_0_.3), channel_id=1, source_target_pairs={{0,2},{1,3},{2,0},{3,1},{4,6},{5,7},{6,4},{7,5},{8,10},{9,11},{10,... | collective-permute-start | bytes 393224 | tf_op jit(solution)/shard_map/ppermute | solution.py:212
  4.7 12.6 %collective-permute-start = (bf16[256,256]{1,0:T(8,128)(2,1)}, bf16[256,256]{1,0:T(8,128)(2,1)S(1)}, u32[]{:S(2)}, u32[]{:S(2)}) collective-permute-start(bf16[256,256]{1,0:T(8,128)(2,1)} %refs_0_.3), channel_id=1, source_target_pairs={{0,1},{1,0},{2,3},{3,2},{4,5},{5,4},{6,7},{7,6},{8,9},{9,8},{10,11... | collective-permute-start | bytes 393224 | tf_op jit(solution)/shard_map/ppermute | solution.py:212
  6.3 11.0 %collective-permute-start.2 = (bf16[256,256]{1,0:T(8,128)(2,1)}, bf16[256,256]{1,0:T(8,128)(2,1)S(1)}, u32[]{:S(2)}, u32[]{:S(2)}) collective-permute-start(bf16[256,256]{1,0:T(8,128)(2,1)} %refs_0_.3), channel_id=1, source_target_pairs={{0,3},{1,2},{2,1},{3,0},{4,7},{5,6},{6,5},{7,4},{8,11},{9,10},{10,... | collective-permute-start | bytes 393224 | tf_op jit(solution)/shard_map/ppermute | solution.py:212
  6.3 11.0 %copy-start = (bf16[256,256]{1,0:T(8,128)(2,1)S(1)}, bf16[256,256]{1,0:T(8,128)(2,1)}, u32[]{:S(2)}) copy-start(bf16[256,256]{1,0:T(8,128)(2,1)} %refs_0_.3) | copy-start | bytes 393220
  6.3 11.0 %copy-start.1 = (bf16[256,256]{1,0:T(8,128)(2,1)S(1)}, bf16[256,256]{1,0:T(8,128)(2,1)}, u32[]{:S(2)}) copy-start(bf16[256,256]{1,0:T(8,128)(2,1)} %weight_ref.3) | copy-start | bytes 393220
  7.6 9.7 %copy-start.2 = (bf16[256,128]{1,0:T(8,128)(2,1)S(1)}, bf16[256,128]{1,0:T(8,128)(2,1)}, u32[]{:S(2)}) copy-start(bf16[256,128]{1,0:T(8,128)(2,1)} %bnd_ref.1) | copy-start | bytes 196612
  7.6 1.3 %collective-permute-start.3 = (bf16[64,256]{1,0:T(8,128)(2,1)S(1)}, bf16[64,256]{1,0:T(8,128)(2,1)S(1)}, u32[]{:S(2)}, u32[]{:S(2)}) collective-permute-start(bf16[64,256]{1,0:T(8,128)(2,1)S(1)} %get-tuple-element.31), channel_id=1, source_target_pairs={{0,4},{4,0},{8,12},{12,8},{16,20},{20,16},{24,28},{28,24},{1,5},{5... | collective-permute-start | bytes 98312 | tf_op jit(solution)/shard_map/ppermute | solution.py:215
  8.9 3.7 %collective-permute-start.4 = (bf16[32,256]{1,0:T(8,128)(2,1)S(1)}, bf16[32,256]{1,0:T(8,128)(2,1)S(1)}, u32[]{:S(2)}, u32[]{:S(2)}) collective-permute-start(bf16[32,256]{1,0:T(8,128)(2,1)S(1)} %get-tuple-element.33), channel_id=1, source_target_pairs={{0,8},{4,12},{8,0},{12,4},{16,24},{20,28},{24,16},{28,20},{1,9},{5... | collective-permute-start | bytes 49160 | tf_op jit(solution)/shard_map/ppermute | solution.py:215
  10.6 4.7 %collective-permute-start.5 = (bf16[32,256]{1,0:T(8,128)(2,1)S(1)}, bf16[32,256]{1,0:T(8,128)(2,1)S(1)}, u32[]{:S(2)}, u32[]{:S(2)}) collective-permute-start(bf16[32,256]{1,0:T(8,128)(2,1)S(1)} %get-tuple-element.34), channel_id=1, source_target_pairs={{0,16},{4,20},{8,24},{12,28},{16,0},{20,4},{24,8},{28,12},{1,17},{... | collective-permute-start | bytes 49160 | tf_op jit(solution)/shard_map/ppermute | solution.py:215
  12.7 4.6 %collective-permute-start.6 = (bf16[32,256]{1,0:T(8,128)(2,1)S(1)}, bf16[32,256]{1,0:T(8,128)(2,1)S(1)}, u32[]{:S(2)}, u32[]{:S(2)}) collective-permute-start(bf16[32,256]{1,0:T(8,128)(2,1)S(1)} %get-tuple-element.35), channel_id=1, source_target_pairs={{0,24},{4,28},{8,16},{12,20},{16,8},{20,12},{24,0},{28,4},{1,25},{... | collective-permute-start | bytes 49160 | tf_op jit(solution)/shard_map/ppermute | solution.py:215
  20.5 6.9 %collective-permute-start.11 = (bf16[512,256]{1,0:T(8,128)(2,1)S(1)}, bf16[512,256]{1,0:T(8,128)(2,1)S(1)}, u32[]{:S(2)}, u32[]{:S(2)}) collective-permute-start(bf16[512,256]{1,0:T(8,128)(2,1)S(1)} %get-tuple-element.46), channel_id=1, source_target_pairs={{0,1},{1,0},{2,3},{3,2},{4,5},{5,4},{6,7},{7,6},{8,9},{9,8},{10,11... | collective-permute-start | bytes 786440 | tf_op jit(solution)/shard_map/ppermute | solution.py:212
  21.5 1.3 %collective-permute-start.7 = (bf16[192,256]{1,0:T(8,128)(2,1)S(1)}, bf16[192,256]{1,0:T(8,128)(2,1)S(1)}, u32[]{:S(2)}, u32[]{:S(2)}) collective-permute-start(bf16[192,256]{1,0:T(8,128)(2,1)S(1)} %get-tuple-element.41), channel_id=1, source_target_pairs={{0,4},{4,0},{8,12},{12,8},{16,20},{20,16},{24,28},{28,24},{1,5},{5... | collective-permute-start | bytes 294920 | tf_op jit(solution)/shard_map/ppermute | solution.py:215
  22.8 8.3 %collective-permute-start.8 = (bf16[64,256]{1,0:T(8,128)(2,1)S(1)}, bf16[64,256]{1,0:T(8,128)(2,1)S(1)}, u32[]{:S(2)}, u32[]{:S(2)}) collective-permute-start(bf16[64,256]{1,0:T(8,128)(2,1)S(1)} %get-tuple-element.43), channel_id=1, source_target_pairs={{0,8},{4,12},{8,0},{12,4},{16,24},{20,28},{24,16},{28,20},{1,9},{5... | collective-permute-start | bytes 98312 | tf_op jit(solution)/shard_map/ppermute | solution.py:215
  24.4 6.7 %collective-permute-start.9 = (bf16[64,256]{1,0:T(8,128)(2,1)S(1)}, bf16[64,256]{1,0:T(8,128)(2,1)S(1)}, u32[]{:S(2)}, u32[]{:S(2)}) collective-permute-start(bf16[64,256]{1,0:T(8,128)(2,1)S(1)} %get-tuple-element.44), channel_id=1, source_target_pairs={{0,16},{4,20},{8,24},{12,28},{16,0},{20,4},{24,8},{28,12},{1,17},{... | collective-permute-start | bytes 98312 | tf_op jit(solution)/shard_map/ppermute | solution.py:215
  25.9 5.2 %collective-permute-start.10 = (bf16[64,256]{1,0:T(8,128)(2,1)S(1)}, bf16[64,256]{1,0:T(8,128)(2,1)S(1)}, u32[]{:S(2)}, u32[]{:S(2)}) collective-permute-start(bf16[64,256]{1,0:T(8,128)(2,1)S(1)} %get-tuple-element.45), channel_id=1, source_target_pairs={{0,24},{4,28},{8,16},{12,20},{16,8},{20,12},{24,0},{28,4},{1,25},{... | collective-permute-start | bytes 98312 | tf_op jit(solution)/shard_map/ppermute | solution.py:215
  27.5 19.0 %collective-permute-start.12 = (bf16[256,256]{1,0:T(8,128)(2,1)S(1)}, bf16[256,256]{1,0:T(8,128)(2,1)S(1)}, u32[]{:S(2)}, u32[]{:S(2)}) collective-permute-start(bf16[256,256]{1,0:T(8,128)(2,1)S(1)} %relay.1.refs_4_), channel_id=1, source_target_pairs={{0,2},{1,3},{2,0},{3,1},{4,6},{5,7},{6,4},{7,5},{8,10},{9,11},{10,... | collective-permute-start | bytes 393224 | tf_op jit(solution)/shard_map/ppermute | solution.py:212
  31.1 5.7 %collective-permute-start.15 = (bf16[32,256]{1,0:T(8,128)(2,1)S(1)}, bf16[32,256]{1,0:T(8,128)(2,1)S(1)}, u32[]{:S(2)}, u32[]{:S(2)}) collective-permute-start(bf16[32,256]{1,0:T(8,128)(2,1)S(1)} %share_sum.1.refs_0_), channel_id=1, source_target_pairs={{0,3},{1,2},{2,1},{3,0},{4,7},{5,6},{6,5},{7,4},{8,11},{9,10},{10,... | collective-permute-start | bytes 49160 | tf_op jit(solution)/shard_map/ppermute | solution.py:212
  33.8 4.6 %collective-permute-start.14 = (bf16[32,256]{1,0:T(8,128)(2,1)S(1)}, bf16[32,256]{1,0:T(8,128)(2,1)S(1)}, u32[]{:S(2)}, u32[]{:S(2)}) collective-permute-start(bf16[32,256]{1,0:T(8,128)(2,1)S(1)} %share_sum.1.refs_0_), channel_id=1, source_target_pairs={{0,2},{1,3},{2,0},{3,1},{4,6},{5,7},{6,4},{7,5},{8,10},{9,11},{10,... | collective-permute-start | bytes 49160 | tf_op jit(solution)/shard_map/ppermute | solution.py:212
  34.3 4.1 %collective-permute-start.13 = (bf16[32,256]{1,0:T(8,128)(2,1)S(1)}, bf16[32,256]{1,0:T(8,128)(2,1)S(1)}, u32[]{:S(2)}, u32[]{:S(2)}) collective-permute-start(bf16[32,256]{1,0:T(8,128)(2,1)S(1)} %share_sum.1.refs_0_), channel_id=1, source_target_pairs={{0,1},{1,0},{2,3},{3,2},{4,5},{5,4},{6,7},{7,6},{8,9},{9,8},{10,11... | collective-permute-start | bytes 49160 | tf_op jit(solution)/shard_map/ppermute | solution.py:212
  38.4 4.7 %collective-permute-start.18 = (bf16[32,256]{1,0:T(8,128)(2,1)S(1)}, bf16[32,256]{1,0:T(8,128)(2,1)S(1)}, u32[]{:S(2)}, u32[]{:S(2)}) collective-permute-start(bf16[32,256]{1,0:T(8,128)(2,1)S(1)} %rep_sum.1.refs_0_), channel_id=1, source_target_pairs={{0,24},{4,28},{8,16},{12,20},{16,8},{20,12},{24,0},{28,4},{1,25},{... | collective-permute-start | bytes 49160 | tf_op jit(solution)/shard_map/ppermute | solution.py:215
  40.3 3.7 %collective-permute-start.17 = (bf16[32,256]{1,0:T(8,128)(2,1)S(1)}, bf16[32,256]{1,0:T(8,128)(2,1)S(1)}, u32[]{:S(2)}, u32[]{:S(2)}) collective-permute-start(bf16[32,256]{1,0:T(8,128)(2,1)S(1)} %rep_sum.1.refs_0_), channel_id=1, source_target_pairs={{0,16},{4,20},{8,24},{12,28},{16,0},{20,4},{24,8},{28,12},{1,17},{... | collective-permute-start | bytes 49160 | tf_op jit(solution)/shard_map/ppermute | solution.py:215
  40.7 3.7 %collective-permute-start.16 = (bf16[32,256]{1,0:T(8,128)(2,1)S(1)}, bf16[32,256]{1,0:T(8,128)(2,1)S(1)}, u32[]{:S(2)}, u32[]{:S(2)}) collective-permute-start(bf16[32,256]{1,0:T(8,128)(2,1)S(1)} %rep_sum.1.refs_0_), channel_id=1, source_target_pairs={{0,8},{4,12},{8,0},{12,4},{16,24},{20,28},{24,16},{28,20},{1,9},{5... | collective-permute-start | bytes 49160 | tf_op jit(solution)/shard_map/ppermute | solution.py:215
  44.4 2.1 %copy-start.3 = (s32[1,8,16]{2,1,0:T(8,128)S(1)}, s32[1,8,16]{2,1,0:T(8,128)}, u32[]{:S(2)}) copy-start(s32[1,8,16]{2,1,0:T(8,128)} %index_ref.3) | copy-start | bytes 1540
  44.4 1.3 %collective-permute-start.19 = (bf16[128,256]{1,0:T(8,128)(2,1)S(1)}, bf16[128,256]{1,0:T(8,128)(2,1)S(1)}, u32[]{:S(2)}, u32[]{:S(2)}) collective-permute-start(bf16[128,256]{1,0:T(8,128)(2,1)S(1)} %half.1.own_ref), channel_id=1, source_target_pairs={{0,4},{4,0},{8,12},{12,8},{16,20},{20,16},{24,28},{28,24},{1,5},{5... | collective-permute-start | bytes 196616 | tf_op jit(solution)/shard_map/ppermute | solution.py:215

commit v9 on v8

--- a/solution.py
+++ b/solution.py
@@ -150,7 +150,8 @@
     send_ref[pairs * each :, :] = partial[pl.ds(pl.multiple_of((1 - mine) * half, half), half), :].astype(BF16)
 
 
-def terms_kernel(rep, layout, cols_ref, counts_ref, vals_ref, grad_ref, *refs):
+def terms_kernel(rep, layout, cols_ref, counts_ref, vals_ref, grad_ref, order_ref, *refs):
+    del order_ref
     outs, terms = refs[:-1], refs[-1]
     me = lax.axis_index("rep")
     tiles, slots = cols_ref.shape
@@ -168,7 +169,8 @@
                 out_ref[row : row + TILE, :] = terms[owner * tiles + t].astype(out_ref.dtype)
 
 
-def relay_kernel(far_ref, came_ref, out_ref):
+def relay_kernel(far_ref, came_ref, *refs):
+    out_ref = refs[-1]
     rows = far_ref.shape[0]
     out_ref[...] = (far_ref[...] + came_ref[rows:, :].astype(F32)).astype(BF16)
 
@@ -178,7 +180,8 @@
     refs[-1][...] = ((chunk + two) + (one + three)).astype(BF16)
 
 
-def join_kernel(bit, own_ref, got_ref, out_ref):
+def join_kernel(bit, own_ref, got_ref, order_ref, out_ref):
+    del order_ref
     own, got = own_ref[...], got_ref[...]
     half = own.shape[0]
     upper = lax.rem(lax.axis_index("dom") // bit, 2) == 1
@@ -214,7 +217,7 @@
     def across(value, bits):
         return lax.ppermute(value, "dom", [(i, i ^ bits) for i in range(groups)])
 
-    def call(kernel, name, outs, operands, scratch=()):
+    def call(kernel, name, outs, operands, scratch=(), flops=1):
         return pl.pallas_call(
             kernel,
             out_shape=outs,
@@ -222,7 +225,7 @@
             out_specs=[VMEM] * len(outs),
             scratch_shapes=scratch,
             compiler_params=params,
-            cost_estimate=pl.CostEstimate(flops=1, bytes_accessed=1, transcendentals=0),
+            cost_estimate=pl.CostEstimate(flops=flops, bytes_accessed=1, transcendentals=0),
             name=name,
         )(*operands)
 
@@ -293,38 +296,45 @@
             jax.ShapeDtypeStruct((len(shifts) * rows, width), kind)
             for shifts, kind in zip(layout, kinds)
         ],
-        in_specs=[SMEM] * 2 + [VMEM] * 2,
+        in_specs=[SMEM] * 2 + [VMEM] * 3,
         out_specs=[VMEM] * len(layout),
         scratch_shapes=[pltpu.VMEM((rep * tiles, TILE, width), F32)],
         compiler_params=params,
+        cost_estimate=pl.CostEstimate(flops=500000001, bytes_accessed=1, transcendentals=0),
         name="terms",
-    )(tile_cols, tile_counts, tile_vals, grad)
+    )(tile_cols, tile_counts, tile_vals, grad, own_rows)
     (chunk,) = call(
-        functools.partial(share_sum_kernel, each), "share_sum", [shape(share)], (own_share, *parts)
+        functools.partial(share_sum_kernel, each), "share_sum", [shape(share)], (own_share, *parts), flops=4000000001
     )
     if relayed:
         came = shifted(sends[0], 1)
-        (relay,) = call(relay_kernel, "relay", [shape(rows)], (sends[1], came))
+        small = [shifted(chunk, shift) for shift in (1, 2, 3)]
+        (relay,) = call(relay_kernel, "relay", [shape(rows)], (sends[1], came, chunk))
         arrived = [came, shifted(relay, 2)]
-        small = [shifted(chunk, shift) for shift in (1, 2, 3)]
-        (piece,) = call(rep_sum_kernel, "rep_sum", [shape(share)], (chunk, *small, relay))
+        (piece,) = call(rep_sum_kernel, "rep_sum", [shape(share)], (chunk, *small), flops=1000000001)
     else:
         arrived = [shifted(send, shift) for shift, send in enumerate(sends, 1)]
         piece = jnp.sum(lax.all_gather(chunk, "rep").astype(F32), axis=0).astype(BF16)
     pieces = [piece] + [across(piece, 2 * j) for j in range(1, pairs)]
-    (piece,) = call(half_kernel, "half", [shape(half)], pieces, [pltpu.VMEM((half, width), F32)])
-    (grad_weight,) = call(
-        functools.partial(join_kernel, 1), "join", [shape(feats, F32)], (piece, across(piece, 1))
-    )
+    (piece,) = call(half_kernel, "half", [shape(half)], pieces, [pltpu.VMEM((half, width), F32)], 1)
     grad_features = pl.pallas_call(
         functools.partial(final_kernel, pairs),
         out_shape=jax.ShapeDtypeStruct((rows, feats), BF16),
         in_specs=[VMEM] * (3 + pairs + len(arrived)),
         out_specs=VMEM,
         compiler_params=params,
-        cost_estimate=pl.CostEstimate(flops=1_000_000_000, bytes_accessed=1, transcendentals=0),
+        cost_estimate=pl.CostEstimate(flops=1, bytes_accessed=1, transcendentals=0),
         name="input_gradient",
     )(send_rows, weight, own, *returned, *arrived)
+    grad_weight = pl.pallas_call(
+        functools.partial(join_kernel, 1),
+        out_shape=shape(feats, F32),
+        in_specs=[VMEM, VMEM, HBM],
+        out_specs=VMEM,
+        compiler_params=params,
+        cost_estimate=pl.CostEstimate(flops=1, bytes_accessed=1, transcendentals=0),
+        name="join",
+    )(piece, across(piece, 1), pltpu.with_memory_space_constraint(grad_features, pltpu.HBM))
     return (output, grad_features, grad_weight)
 
 

time: 47.7 us -> 47.1 us (0.987)
  waiting for transfers between devices: 12.6 us -> 11.8 us
  local copies, waits for them, and re-layouts: 0.02 us -> 0.59 us
    ppermute x8, waiting for transfers between devices: 3.92 us -> 2.68 us  [shifted(): lax.ppermute(value, 'rep', [(i, target(i, shift, rep)) for i in range(rep)])]
    pallas_call x0 -> x1, Pallas kernels: none -> 0.73 us  [body(): pl.pallas_call(functools.partial(join_kernel, 1), out_shape=shape(feats,...]
    pallas_call x7 -> x6, Pallas kernels: 0.84 us -> 0.12 us  [call(): pl.pallas_call(kernel, out_shape=outs, in_specs=[VMEM] * len(operands), o...]
    unnamed x8, local copies, waits for them, and re-layouts: 0.02 us -> 0.59 us
  transfers between devices with their start and end apart: 20 -> 20, of which waited for: 11 -> 10; matrix products, arithmetic and copies ran while one was open for 0% -> 0% of each run, Pallas kernels for 5% -> 8%
where the time goes in v9:
time: 47.1 us; the launch traced here: 47 us
  starting transfers between devices  27.5 us (58%)
  waiting for transfers between devices  11.8 us (25%)
  Pallas kernels  6.37 us (14%)
  between operations  0.75 us (2%)
  local copies, waits for them, and re-layouts  0.59 us (1%)
    ppermute x8, starting transfers between devices, shifted(): lax.ppermute(value, 'rep', [(i, target(i, shift, rep)) for i in range(rep)])  14.4 us
    ppermute x12, starting transfers between devices, across(): return lax.ppermute(value, 'dom', [(i, i ^ bits) for i in range(groups)])  13.1 us
    ppermute x12, waiting for transfers between devices, across(): return lax.ppermute(value, 'dom', [(i, i ^ bits) for i in range(groups)])  9.08 us
    ppermute x8, waiting for transfers between devices, shifted(): lax.ppermute(value, 'rep', [(i, target(i, shift, rep)) for i in range(rep)])  2.68 us
    pallas_call x1, Pallas kernels, body(): pl.pallas_call(functools.partial(layer_kernel, rep, pairs), out_shape=[sh...  2.02 us
    pallas_call x1, Pallas kernels, body(): pl.pallas_call(pick_kernel, out_shape=[*[shape(pairs * each, BF16, feats)...  1.3 us
    pallas_call x1, Pallas kernels, body(): pl.pallas_call(functools.partial(terms_kernel, rep, layout), out_shape=[j...  1.16 us
    pallas_call x1, Pallas kernels, body(): pl.pallas_call(functools.partial(final_kernel, pairs), out_shape=jax.Shap...  1.05 us
  transfers between devices with their start and end apart: 20, of which 10 were waited for; matrix products, arithmetic and copies ran while one was open for 0% of the time, Pallas kernels for 8%

profile of v9, /device:TPU:0, one launch (start us, length us, event | category | flops | bytes accessed | tf_op | source)
XLA Modules:
  0.0 47.0 jit_solution(1707383896331550533)
XLA Ops:
  0.6 3.1 %collective-permute-start = (bf16[256,256]{1,0:T(8,128)(2,1)}, bf16[256,256]{1,0:T(8,128)(2,1)S(1)}, u32[]{:S(2)}, u32[]{:S(2)}) collective-permute-start(bf16[256,256]{1,0:T(8,128)(2,1)} %refs_0_.3), channel_id=1, source_target_pairs={{0,1},{1,0},{2,3},{3,2},{4,5},{5,4},{6,7},{7,6},{8,9},{9,8},{10,11... | collective-permute-start | bytes 393224 | tf_op jit(solution)/shard_map/ppermute | solution.py:215
  3.7 2.6 %collective-permute-start.1 = (bf16[256,256]{1,0:T(8,128)(2,1)}, bf16[256,256]{1,0:T(8,128)(2,1)S(1)}, u32[]{:S(2)}, u32[]{:S(2)}) collective-permute-start(bf16[256,256]{1,0:T(8,128)(2,1)} %refs_0_.3), channel_id=1, source_target_pairs={{0,2},{1,3},{2,0},{3,1},{4,6},{5,7},{6,4},{7,5},{8,10},{9,11},{10,... | collective-permute-start | bytes 393224 | tf_op jit(solution)/shard_map/ppermute | solution.py:215
  6.3 1.3 %pick_rows.1 = (bf16[64,256]{1,0:T(8,128)(2,1)S(1)}, bf16[64,256]{1,0:T(8,128)(2,1)S(1)}, bf16[2,8,128,128]{3,2,1,0:T(8,128)(2,1)S(1)}, bf16[256,256]{1,0:T(8,12...) custom-call(s32[1,8,16]{2,1,0:T(8,128)} %index_ref.3, bf16[256,256]{1,0:T(8,128)(2,1)} %refs_0_.3, ...), custom_call_target="tpu_custom_call" | custom-call | tf_op jit(solution)/shard_map/pick_rows/pallas_call | solution.py:237
  7.7 1.2 %collective-permute-done.3.came_ref = bf16[64,256]{1,0:T(8,128)(2,1)S(1)} collective-permute-done((bf16[64,256]{1,0:T(8,128)(2,1)S(1)}, bf16[64,256]{1,0:T(8,128)(2,1)S(1)}, u32[]{:S(2)}, u32[]{:S(2)}) %collective-permute-start.3) | collective-permute-done | bytes 32800 | tf_op jit(solution)/shard_map/ppermute | solution.py:218
  8.9 1.7 %collective-permute-start.4 = (bf16[32,256]{1,0:T(8,128)(2,1)S(1)}, bf16[32,256]{1,0:T(8,128)(2,1)S(1)}, u32[]{:S(2)}, u32[]{:S(2)}) collective-permute-start(bf16[32,256]{1,0:T(8,128)(2,1)S(1)} %get-tuple-element.33), channel_id=1, source_target_pairs={{0,8},{4,12},{8,0},{12,4},{16,24},{20,28},{24,16},{28,20},{1,9},{5... | collective-permute-start | bytes 49160 | tf_op jit(solution)/shard_map/ppermute | solution.py:218
  10.6 1.5 %collective-permute-start.5 = (bf16[32,256]{1,0:T(8,128)(2,1)S(1)}, bf16[32,256]{1,0:T(8,128)(2,1)S(1)}, u32[]{:S(2)}, u32[]{:S(2)}) collective-permute-start(bf16[32,256]{1,0:T(8,128)(2,1)S(1)} %get-tuple-element.34), channel_id=1, source_target_pairs={{0,16},{4,20},{8,24},{12,28},{16,0},{20,4},{24,8},{28,12},{1,17},{... | collective-permute-start | bytes 49160 | tf_op jit(solution)/shard_map/ppermute | solution.py:218
  12.1 0.5 %collective-permute-done.4.refs_5_ = bf16[32,256]{1,0:T(8,128)(2,1)S(1)} collective-permute-done((bf16[32,256]{1,0:T(8,128)(2,1)S(1)}, bf16[32,256]{1,0:T(8,128)(2,1)S(1)}, u32[]{:S(2)}, u32[]{:S(2)}) %collective-permute-start.4) | collective-permute-done | bytes 16416 | tf_op jit(solution)/shard_map/ppermute | solution.py:218
  12.7 2.6 %collective-permute-start.6 = (bf16[32,256]{1,0:T(8,128)(2,1)S(1)}, bf16[32,256]{1,0:T(8,128)(2,1)S(1)}, u32[]{:S(2)}, u32[]{:S(2)}) collective-permute-start(bf16[32,256]{1,0:T(8,128)(2,1)S(1)} %get-tuple-element.35), channel_id=1, source_target_pairs={{0,24},{4,28},{8,16},{12,20},{16,8},{20,12},{24,0},{28,4},{1,25},{... | collective-permute-start | bytes 49160 | tf_op jit(solution)/shard_map/ppermute | solution.py:218
  15.3 2.0 %collective-permute-done.6.refs_7_ = bf16[32,256]{1,0:T(8,128)(2,1)S(1)} collective-permute-done((bf16[32,256]{1,0:T(8,128)(2,1)S(1)}, bf16[32,256]{1,0:T(8,128)(2,1)S(1)}, u32[]{:S(2)}, u32[]{:S(2)}) %collective-permute-start.6) | collective-permute-done | bytes 16416 | tf_op jit(solution)/shard_map/ppermute | solution.py:218
  17.3 2.0 %layer.1 = (bf16[256,256]{1,0:T(8,128)(2,1)}, bf16[256,256]{1,0:T(8,128)(2,1)S(1)}, bf16[192,256]{1,0:T(8,128)(2,1)S(1)}, bf16[64,256]{1,0:T(8,128)(2,1)S(1)}, f32[128,256]{1,0:T(8,128)S(1)}) custom-call(s32[2,8]{1,0:T(2,128)S(1)} %get-tuple-element.26.cols_ref, s32[2]{0:T(128)S(1)} %get-tuple-element.27.counts_ref, ...), custom_call_target="tpu_custom_call" | custom-call | tf_op jit(solution)/shard_map/layer/pallas_call | solution.py:261
  19.4 1.3 %collective-permute-done.7.came_ref = bf16[192,256]{1,0:T(8,128)(2,1)S(1)} collective-permute-done((bf16[192,256]{1,0:T(8,128)(2,1)S(1)}, bf16[192,256]{1,0:T(8,128)(2,1)S(1)}, u32[]{:S(2)}, u32[]{:S(2)}) %collective-permute-start.7) | collective-permute-done | bytes 98336 | tf_op jit(solution)/shard_map/ppermute | solution.py:218
  20.7 1.7 %collective-permute-start.8 = (bf16[64,256]{1,0:T(8,128)(2,1)S(1)}, bf16[64,256]{1,0:T(8,128)(2,1)S(1)}, u32[]{:S(2)}, u32[]{:S(2)}) collective-permute-start(bf16[64,256]{1,0:T(8,128)(2,1)S(1)} %get-tuple-element.43), channel_id=1, source_target_pairs={{0,8},{4,12},{8,0},{12,4},{16,24},{20,28},{24,16},{28,20},{1,9},{5... | collective-permute-start | bytes 98312 | tf_op jit(solution)/shard_map/ppermute | solution.py:218
  22.4 1.5 %collective-permute-start.9 = (bf16[64,256]{1,0:T(8,128)(2,1)S(1)}, bf16[64,256]{1,0:T(8,128)(2,1)S(1)}, u32[]{:S(2)}, u32[]{:S(2)}) collective-permute-start(bf16[64,256]{1,0:T(8,128)(2,1)S(1)} %get-tuple-element.44), channel_id=1, source_target_pairs={{0,16},{4,20},{8,24},{12,28},{16,0},{20,4},{24,8},{28,12},{1,17},{... | collective-permute-start | bytes 98312 | tf_op jit(solution)/shard_map/ppermute | solution.py:218
  24.0 0.3 collective-permute-start.10
  24.2 1.2 %terms.1 = (f32[256,256]{1,0:T(8,128)S(1)}, bf16[512,256]{1,0:T(8,128)(2,1)S(1)}, f32[256,256]{1,0:T(8,128)S(1)}) custom-call(s32[2,8]{1,0:T(2,128)S(1)} %get-tuple-element.26.cols_ref, s32[2]{0:T(128)S(1)} %get-tuple-element.27.counts_ref, bf16[2,8,128,128]{3,2,1,0:T(8,128)(2,1)S(1)} %get-tuple-element.28.vals_ref, ...), custom_call_target="tpu_custom_call" | custom-call | flops 500000000 | bytes 1 | tf_op jit(solution)/shard_map/terms/pallas_call | solution.py:293
  25.4 1.6 %collective-permute-start.11 = (bf16[512,256]{1,0:T(8,128)(2,1)S(1)}, bf16[512,256]{1,0:T(8,128)(2,1)S(1)}, u32[]{:S(2)}, u32[]{:S(2)}) collective-permute-start(bf16[512,256]{1,0:T(8,128)(2,1)S(1)} %get-tuple-element.46), channel_id=1, source_target_pairs={{0,1},{1,0},{2,3},{3,2},{4,5},{5,4},{6,7},{7,6},{8,9},{9,8},{10,11... | collective-permute-start | bytes 786440 | tf_op jit(solution)/shard_map/ppermute | solution.py:215
  27.0 1.8 %collective-permute-done.10.refs_2_.refs_3_ = bf16[64,256]{1,0:T(8,128)(2,1)S(1)} collective-permute-done((bf16[64,256]{1,0:T(8,128)(2,1)S(1)}, bf16[64,256]{1,0:T(8,128)(2,1)S(1)}, u32[]{:S(2)}, u32[]{:S(2)}) %collective-permute-start.10) | collective-permute-done | bytes 32800 | tf_op jit(solution)/shard_map/ppermute | solution.py:218
  28.8 1.4 %collective-permute-start.13 = (bf16[32,256]{1,0:T(8,128)(2,1)S(1)}, bf16[32,256]{1,0:T(8,128)(2,1)S(1)}, u32[]{:S(2)}, u32[]{:S(2)}) collective-permute-start(bf16[32,256]{1,0:T(8,128)(2,1)S(1)} %share_sum.1.refs_0_), channel_id=1, source_target_pairs={{0,1},{1,0},{2,3},{3,2},{4,5},{5,4},{6,7},{7,6},{8,9},{9,8},{10,11... | collective-permute-start | bytes 49160 | tf_op jit(solution)/shard_map/ppermute | solution.py:215
  30.2 2.8 %collective-permute-start.14 = (bf16[32,256]{1,0:T(8,128)(2,1)S(1)}, bf16[32,256]{1,0:T(8,128)(2,1)S(1)}, u32[]{:S(2)}, u32[]{:S(2)}) collective-permute-start(bf16[32,256]{1,0:T(8,128)(2,1)S(1)} %share_sum.1.refs_0_), channel_id=1, source_target_pairs={{0,2},{1,3},{2,0},{3,1},{4,6},{5,7},{6,4},{7,5},{8,10},{9,11},{10,... | collective-permute-start | bytes 49160 | tf_op jit(solution)/shard_map/ppermute | solution.py:215
  33.0 0.2 collective-permute-start.15
  33.2 0.1 collective-permute-done.11.came_ref.refs_4_
  33.4 2.7 %collective-permute-start.12 = (bf16[256,256]{1,0:T(8,128)(2,1)S(1)}, bf16[256,256]{1,0:T(8,128)(2,1)S(1)}, u32[]{:S(2)}, u32[]{:S(2)}) collective-permute-start(bf16[256,256]{1,0:T(8,128)(2,1)S(1)} %relay.1), channel_id=1, source_target_pairs={{0,2},{1,3},{2,0},{3,1},{4,6},{5,7},{6,4},{7,5},{8,10},{9,11},{10,... | collective-permute-start | bytes 393224 | tf_op jit(solution)/shard_map/ppermute | solution.py:215
  36.1 2.5 %collective-permute-done.15.refs_3_ = bf16[32,256]{1,0:T(8,128)(2,1)S(1)} collective-permute-done((bf16[32,256]{1,0:T(8,128)(2,1)S(1)}, bf16[32,256]{1,0:T(8,128)(2,1)S(1)}, u32[]{:S(2)}, u32[]{:S(2)}) %collective-permute-start.15) | collective-permute-done | bytes 16416 | tf_op jit(solution)/shard_map/ppermute | solution.py:215
  38.7 0.7 %collective-permute-start.16 = (bf16[32,256]{1,0:T(8,128)(2,1)S(1)}, bf16[32,256]{1,0:T(8,128)(2,1)S(1)}, u32[]{:S(2)}, u32[]{:S(2)}) collective-permute-start(bf16[32,256]{1,0:T(8,128)(2,1)S(1)} %rep_sum.1.refs_0_), channel_id=1, source_target_pairs={{0,8},{4,12},{8,0},{12,4},{16,24},{20,28},{24,16},{28,20},{1,9},{5... | collective-permute-start | bytes 49160 | tf_op jit(solution)/shard_map/ppermute | solution.py:218
  39.4 0.5 %collective-permute-start.17 = (bf16[32,256]{1,0:T(8,128)(2,1)S(1)}, bf16[32,256]{1,0:T(8,128)(2,1)S(1)}, u32[]{:S(2)}, u32[]{:S(2)}) collective-permute-start(bf16[32,256]{1,0:T(8,128)(2,1)S(1)} %rep_sum.1.refs_0_), channel_id=1, source_target_pairs={{0,16},{4,20},{8,24},{12,28},{16,0},{20,4},{24,8},{28,12},{1,17},{... | collective-permute-start | bytes 49160 | tf_op jit(solution)/shard_map/ppermute | solution.py:218
  39.8 2.4 %collective-permute-start.18 = (bf16[32,256]{1,0:T(8,128)(2,1)S(1)}, bf16[32,256]{1,0:T(8,128)(2,1)S(1)}, u32[]{:S(2)}, u32[]{:S(2)}) collective-permute-start(bf16[32,256]{1,0:T(8,128)(2,1)S(1)} %rep_sum.1.refs_0_), channel_id=1, source_target_pairs={{0,24},{4,28},{8,16},{12,20},{16,8},{20,12},{24,0},{28,4},{1,25},{... | collective-permute-start | bytes 49160 | tf_op jit(solution)/shard_map/ppermute | solution.py:218
  42.2 0.2 collective-permute-done.16.refs_1_
  42.5 0.6 %collective-permute-done.17.refs_2_ = bf16[32,256]{1,0:T(8,128)(2,1)S(1)} collective-permute-done((bf16[32,256]{1,0:T(8,128)(2,1)S(1)}, bf16[32,256]{1,0:T(8,128)(2,1)S(1)}, u32[]{:S(2)}, u32[]{:S(2)}) %collective-permute-start.17) | collective-permute-done | bytes 16416 | tf_op jit(solution)/shard_map/ppermute | solution.py:218
  43.1 1.4 %collective-permute-done.18.refs_3_ = bf16[32,256]{1,0:T(8,128)(2,1)S(1)} collective-permute-done((bf16[32,256]{1,0:T(8,128)(2,1)S(1)}, bf16[32,256]{1,0:T(8,128)(2,1)S(1)}, u32[]{:S(2)}, u32[]{:S(2)}) %collective-permute-start.18) | collective-permute-done | bytes 16416 | tf_op jit(solution)/shard_map/ppermute | solution.py:218
  44.6 0.6 %copy-done.3 = s32[1,8,16]{2,1,0:T(8,128)S(1)} copy-done((s32[1,8,16]{2,1,0:T(8,128)S(1)}, s32[1,8,16]{2,1,0:T(8,128)}, u32[]{:S(2)}) %copy-start.3) | copy-done | bytes 536
  45.2 1.0 %input_gradient.1.order_ref = bf16[256,256]{1,0:T(8,128)(2,1)} custom-call(s32[1,8,16]{2,1,0:T(8,128)S(1)} %copy-done.3, bf16[256,256]{1,0:T(8,128)(2,1)S(1)} %copy-done.1, f32[256,256]{1,0:T(8,128)S(1)} %get-tuple-element.42.own_ref, bf16[32,256]{1,0:T(8,128)(2,1)S(1)} %get-tuple-element.41.order_ref.refs_0_, ...), custom_call_target="tpu_custom_call" | custom-call | flops 1 | bytes 1 | tf_op jit(solution)/shard_map/input_gradient/pallas_call | solution.py:320
  46.2 0.7 %join.1 = f32[256,256]{1,0:T(8,128)} custom-call(bf16[128,256]{1,0:T(8,128)(2,1)S(1)} %half.1.own_ref, bf16[128,256]{1,0:T(8,128)(2,1)S(1)} %collective-permute-done.19.got_ref, bf16[256,256]{1,0:T(8,128)(2,1)} %input_gradient.1.order_ref), custom_call_target="tpu_custom_call" | custom-call | flops 1 | bytes 1 | tf_op jit(solution)/shard_map/join/pallas_call | solution.py:329
  (27 shorter events, 0.3 us)
Async XLA Ops:
  0.6 16.7 %collective-permute-start = (bf16[256,256]{1,0:T(8,128)(2,1)}, bf16[256,256]{1,0:T(8,128)(2,1)S(1)}, u32[]{:S(2)}, u32[]{:S(2)}) collective-permute-start(bf16[256,256]{1,0:T(8,128)(2,1)} %refs_0_.3), channel_id=1, source_target_pairs={{0,1},{1,0},{2,3},{3,2},{4,5},{5,4},{6,7},{7,6},{8,9},{9,8},{10,11... | collective-permute-start | bytes 393224 | tf_op jit(solution)/shard_map/ppermute | solution.py:215
  3.7 13.6 %collective-permute-start.1 = (bf16[256,256]{1,0:T(8,128)(2,1)}, bf16[256,256]{1,0:T(8,128)(2,1)S(1)}, u32[]{:S(2)}, u32[]{:S(2)}) collective-permute-start(bf16[256,256]{1,0:T(8,128)(2,1)} %refs_0_.3), channel_id=1, source_target_pairs={{0,2},{1,3},{2,0},{3,1},{4,6},{5,7},{6,4},{7,5},{8,10},{9,11},{10,... | collective-permute-start | bytes 393224 | tf_op jit(solution)/shard_map/ppermute | solution.py:215
  6.3 11.0 %collective-permute-start.2 = (bf16[256,256]{1,0:T(8,128)(2,1)}, bf16[256,256]{1,0:T(8,128)(2,1)S(1)}, u32[]{:S(2)}, u32[]{:S(2)}) collective-permute-start(bf16[256,256]{1,0:T(8,128)(2,1)} %refs_0_.3), channel_id=1, source_target_pairs={{0,3},{1,2},{2,1},{3,0},{4,7},{5,6},{6,5},{7,4},{8,11},{9,10},{10,... | collective-permute-start | bytes 393224 | tf_op jit(solution)/shard_map/ppermute | solution.py:215
  6.3 11.0 %copy-start = (bf16[256,256]{1,0:T(8,128)(2,1)S(1)}, bf16[256,256]{1,0:T(8,128)(2,1)}, u32[]{:S(2)}) copy-start(bf16[256,256]{1,0:T(8,128)(2,1)} %refs_0_.3) | copy-start | bytes 393220
  6.3 11.0 %copy-start.1 = (bf16[256,256]{1,0:T(8,128)(2,1)S(1)}, bf16[256,256]{1,0:T(8,128)(2,1)}, u32[]{:S(2)}) copy-start(bf16[256,256]{1,0:T(8,128)(2,1)} %weight_ref.3) | copy-start | bytes 393220
  7.6 9.7 %copy-start.2 = (bf16[256,128]{1,0:T(8,128)(2,1)S(1)}, bf16[256,128]{1,0:T(8,128)(2,1)}, u32[]{:S(2)}) copy-start(bf16[256,128]{1,0:T(8,128)(2,1)} %bnd_ref.1) | copy-start | bytes 196612
  7.6 1.3 %collective-permute-start.3 = (bf16[64,256]{1,0:T(8,128)(2,1)S(1)}, bf16[64,256]{1,0:T(8,128)(2,1)S(1)}, u32[]{:S(2)}, u32[]{:S(2)}) collective-permute-start(bf16[64,256]{1,0:T(8,128)(2,1)S(1)} %get-tuple-element.31), channel_id=1, source_target_pairs={{0,4},{4,0},{8,12},{12,8},{16,20},{20,16},{24,28},{28,24},{1,5},{5... | collective-permute-start | bytes 98312 | tf_op jit(solution)/shard_map/ppermute | solution.py:218
  8.9 3.7 %collective-permute-start.4 = (bf16[32,256]{1,0:T(8,128)(2,1)S(1)}, bf16[32,256]{1,0:T(8,128)(2,1)S(1)}, u32[]{:S(2)}, u32[]{:S(2)}) collective-permute-start(bf16[32,256]{1,0:T(8,128)(2,1)S(1)} %get-tuple-element.33), channel_id=1, source_target_pairs={{0,8},{4,12},{8,0},{12,4},{16,24},{20,28},{24,16},{28,20},{1,9},{5... | collective-permute-start | bytes 49160 | tf_op jit(solution)/shard_map/ppermute | solution.py:218
  10.6 4.7 %collective-permute-start.5 = (bf16[32,256]{1,0:T(8,128)(2,1)S(1)}, bf16[32,256]{1,0:T(8,128)(2,1)S(1)}, u32[]{:S(2)}, u32[]{:S(2)}) collective-permute-start(bf16[32,256]{1,0:T(8,128)(2,1)S(1)} %get-tuple-element.34), channel_id=1, source_target_pairs={{0,16},{4,20},{8,24},{12,28},{16,0},{20,4},{24,8},{28,12},{1,17},{... | collective-permute-start | bytes 49160 | tf_op jit(solution)/shard_map/ppermute | solution.py:218
  12.7 4.6 %collective-permute-start.6 = (bf16[32,256]{1,0:T(8,128)(2,1)S(1)}, bf16[32,256]{1,0:T(8,128)(2,1)S(1)}, u32[]{:S(2)}, u32[]{:S(2)}) collective-permute-start(bf16[32,256]{1,0:T(8,128)(2,1)S(1)} %get-tuple-element.35), channel_id=1, source_target_pairs={{0,24},{4,28},{8,16},{12,20},{16,8},{20,12},{24,0},{28,4},{1,25},{... | collective-permute-start | bytes 49160 | tf_op jit(solution)/shard_map/ppermute | solution.py:218
  19.4 1.3 %collective-permute-start.7 = (bf16[192,256]{1,0:T(8,128)(2,1)S(1)}, bf16[192,256]{1,0:T(8,128)(2,1)S(1)}, u32[]{:S(2)}, u32[]{:S(2)}) collective-permute-start(bf16[192,256]{1,0:T(8,128)(2,1)S(1)} %get-tuple-element.40), channel_id=1, source_target_pairs={{0,4},{4,0},{8,12},{12,8},{16,20},{20,16},{24,28},{28,24},{1,5},{5... | collective-permute-start | bytes 294920 | tf_op jit(solution)/shard_map/ppermute | solution.py:218
  20.7 6.3 %collective-permute-start.8 = (bf16[64,256]{1,0:T(8,128)(2,1)S(1)}, bf16[64,256]{1,0:T(8,128)(2,1)S(1)}, u32[]{:S(2)}, u32[]{:S(2)}) collective-permute-start(bf16[64,256]{1,0:T(8,128)(2,1)S(1)} %get-tuple-element.43), channel_id=1, source_target_pairs={{0,8},{4,12},{8,0},{12,4},{16,24},{20,28},{24,16},{28,20},{1,9},{5... | collective-permute-start | bytes 98312 | tf_op jit(solution)/shard_map/ppermute | solution.py:218
  22.4 4.6 %collective-permute-start.9 = (bf16[64,256]{1,0:T(8,128)(2,1)S(1)}, bf16[64,256]{1,0:T(8,128)(2,1)S(1)}, u32[]{:S(2)}, u32[]{:S(2)}) collective-permute-start(bf16[64,256]{1,0:T(8,128)(2,1)S(1)} %get-tuple-element.44), channel_id=1, source_target_pairs={{0,16},{4,20},{8,24},{12,28},{16,0},{20,4},{24,8},{28,12},{1,17},{... | collective-permute-start | bytes 98312 | tf_op jit(solution)/shard_map/ppermute | solution.py:218
  24.0 4.8 %collective-permute-start.10 = (bf16[64,256]{1,0:T(8,128)(2,1)S(1)}, bf16[64,256]{1,0:T(8,128)(2,1)S(1)}, u32[]{:S(2)}, u32[]{:S(2)}) collective-permute-start(bf16[64,256]{1,0:T(8,128)(2,1)S(1)} %get-tuple-element.45), channel_id=1, source_target_pairs={{0,24},{4,28},{8,16},{12,20},{16,8},{20,12},{24,0},{28,4},{1,25},{... | collective-permute-start | bytes 98312 | tf_op jit(solution)/shard_map/ppermute | solution.py:218
  25.4 8.0 %collective-permute-start.11 = (bf16[512,256]{1,0:T(8,128)(2,1)S(1)}, bf16[512,256]{1,0:T(8,128)(2,1)S(1)}, u32[]{:S(2)}, u32[]{:S(2)}) collective-permute-start(bf16[512,256]{1,0:T(8,128)(2,1)S(1)} %get-tuple-element.46), channel_id=1, source_target_pairs={{0,1},{1,0},{2,3},{3,2},{4,5},{5,4},{6,7},{7,6},{8,9},{9,8},{10,11... | collective-permute-start | bytes 786440 | tf_op jit(solution)/shard_map/ppermute | solution.py:215
  28.8 7.3 %collective-permute-start.13 = (bf16[32,256]{1,0:T(8,128)(2,1)S(1)}, bf16[32,256]{1,0:T(8,128)(2,1)S(1)}, u32[]{:S(2)}, u32[]{:S(2)}) collective-permute-start(bf16[32,256]{1,0:T(8,128)(2,1)S(1)} %share_sum.1.refs_0_), channel_id=1, source_target_pairs={{0,1},{1,0},{2,3},{3,2},{4,5},{5,4},{6,7},{7,6},{8,9},{9,8},{10,11... | collective-permute-start | bytes 49160 | tf_op jit(solution)/shard_map/ppermute | solution.py:215
  30.2 5.9 %collective-permute-start.14 = (bf16[32,256]{1,0:T(8,128)(2,1)S(1)}, bf16[32,256]{1,0:T(8,128)(2,1)S(1)}, u32[]{:S(2)}, u32[]{:S(2)}) collective-permute-start(bf16[32,256]{1,0:T(8,128)(2,1)S(1)} %share_sum.1.refs_0_), channel_id=1, source_target_pairs={{0,2},{1,3},{2,0},{3,1},{4,6},{5,7},{6,4},{7,5},{8,10},{9,11},{10,... | collective-permute-start | bytes 49160 | tf_op jit(solution)/shard_map/ppermute | solution.py:215
  33.0 5.6 %collective-permute-start.15 = (bf16[32,256]{1,0:T(8,128)(2,1)S(1)}, bf16[32,256]{1,0:T(8,128)(2,1)S(1)}, u32[]{:S(2)}, u32[]{:S(2)}) collective-permute-start(bf16[32,256]{1,0:T(8,128)(2,1)S(1)} %share_sum.1.refs_0_), channel_id=1, source_target_pairs={{0,3},{1,2},{2,1},{3,0},{4,7},{5,6},{6,5},{7,4},{8,11},{9,10},{10,... | collective-permute-start | bytes 49160 | tf_op jit(solution)/shard_map/ppermute | solution.py:215
  33.4 11.2 %collective-permute-start.12 = (bf16[256,256]{1,0:T(8,128)(2,1)S(1)}, bf16[256,256]{1,0:T(8,128)(2,1)S(1)}, u32[]{:S(2)}, u32[]{:S(2)}) collective-permute-start(bf16[256,256]{1,0:T(8,128)(2,1)S(1)} %relay.1), channel_id=1, source_target_pairs={{0,2},{1,3},{2,0},{3,1},{4,6},{5,7},{6,4},{7,5},{8,10},{9,11},{10,... | collective-permute-start | bytes 393224 | tf_op jit(solution)/shard_map/ppermute | solution.py:215
  38.7 3.8 %collective-permute-start.16 = (bf16[32,256]{1,0:T(8,128)(2,1)S(1)}, bf16[32,256]{1,0:T(8,128)(2,1)S(1)}, u32[]{:S(2)}, u32[]{:S(2)}) collective-permute-start(bf16[32,256]{1,0:T(8,128)(2,1)S(1)} %rep_sum.1.refs_0_), channel_id=1, source_target_pairs={{0,8},{4,12},{8,0},{12,4},{16,24},{20,28},{24,16},{28,20},{1,9},{5... | collective-permute-start | bytes 49160 | tf_op jit(solution)/shard_map/ppermute | solution.py:218
  39.4 3.7 %collective-permute-start.17 = (bf16[32,256]{1,0:T(8,128)(2,1)S(1)}, bf16[32,256]{1,0:T(8,128)(2,1)S(1)}, u32[]{:S(2)}, u32[]{:S(2)}) collective-permute-start(bf16[32,256]{1,0:T(8,128)(2,1)S(1)} %rep_sum.1.refs_0_), channel_id=1, source_target_pairs={{0,16},{4,20},{8,24},{12,28},{16,0},{20,4},{24,8},{28,12},{1,17},{... | collective-permute-start | bytes 49160 | tf_op jit(solution)/shard_map/ppermute | solution.py:218
  39.8 4.6 %collective-permute-start.18 = (bf16[32,256]{1,0:T(8,128)(2,1)S(1)}, bf16[32,256]{1,0:T(8,128)(2,1)S(1)}, u32[]{:S(2)}, u32[]{:S(2)}) collective-permute-start(bf16[32,256]{1,0:T(8,128)(2,1)S(1)} %rep_sum.1.refs_0_), channel_id=1, source_target_pairs={{0,24},{4,28},{8,16},{12,20},{16,8},{20,12},{24,0},{28,4},{1,25},{... | collective-permute-start | bytes 49160 | tf_op jit(solution)/shard_map/ppermute | solution.py:218
  44.5 0.7 %copy-start.3 = (s32[1,8,16]{2,1,0:T(8,128)S(1)}, s32[1,8,16]{2,1,0:T(8,128)}, u32[]{:S(2)}) copy-start(s32[1,8,16]{2,1,0:T(8,128)} %index_ref.3) | copy-start | bytes 1540
  44.5 1.7 %collective-permute-start.19 = (bf16[128,256]{1,0:T(8,128)(2,1)S(1)}, bf16[128,256]{1,0:T(8,128)(2,1)S(1)}, u32[]{:S(2)}, u32[]{:S(2)}) collective-permute-start(bf16[128,256]{1,0:T(8,128)(2,1)S(1)} %half.1.own_ref), channel_id=1, source_target_pairs={{0,4},{4,0},{8,12},{12,8},{16,20},{20,16},{24,28},{28,24},{1,5},{5... | collective-permute-start | bytes 196616 | tf_op jit(solution)/shard_map/ppermute | solution.py:218

commit v10 on v9

--- a/solution.py
+++ b/solution.py
@@ -37,8 +37,8 @@
 
 def pick_kernel(index_ref, features_ref, *refs):
     count = (len(refs) - 5) // 2
-    loads, send_ref, keep_ref, loaded = refs[:count], refs[count], refs[count + 1], refs[count + 2 : -3]
-    index, features, sems = refs[-3:]
+    loads, send_ref, keep_ref, index, loaded = refs[:count], *refs[count : count + 3], refs[count + 3 : -2]
+    features, sems = refs[-2:]
     pairs = [(index_ref, index), (features_ref, features), *zip(loads, loaded)]
     copies = [pltpu.make_async_copy(*pair, sems.at[at]) for at, pair in enumerate(pairs)]
     for copy in copies:
@@ -175,9 +175,8 @@
     out_ref[...] = (far_ref[...] + came_ref[rows:, :].astype(F32)).astype(BF16)
 
 
-def rep_sum_kernel(*refs):
-    chunk, one, two, three = [ref[...].astype(F32) for ref in refs[:4]]
-    refs[-1][...] = ((chunk + two) + (one + three)).astype(BF16)
+def pair_sum_kernel(own_ref, came_ref, out_ref):
+    out_ref[...] = (own_ref[...].astype(F32) + came_ref[...].astype(F32)).astype(BF16)
 
 
 def join_kernel(bit, own_ref, got_ref, order_ref, out_ref):
@@ -233,17 +232,18 @@
         return jax.ShapeDtypeStruct((high, wide), kind)
 
     blocks = [features] + [shifted(features, shift) for shift in range(1, rep)]
+    relayed = rep == 4
     loads = [tile_vals, cotangent, tile_cols, tile_counts]
-    send, keep, tile_vals, cotangent, tile_cols, tile_counts = pl.pallas_call(
+    send, keep, index, tile_vals, cotangent, tile_cols, tile_counts = pl.pallas_call(
         pick_kernel,
         out_shape=[
             *[shape(pairs * each, BF16, feats)] * 2,
+            jax.ShapeDtypeStruct(send_rows.shape, jnp.int32),
             *[jax.ShapeDtypeStruct(load.shape, load.dtype) for load in loads],
         ],
         in_specs=[HBM] * (2 + len(loads)),
-        out_specs=[VMEM] * (2 + len(loads)),
+        out_specs=[VMEM] * (3 + len(loads)),
         scratch_shapes=[
-            pltpu.VMEM(send_rows.shape, jnp.int32),
             pltpu.VMEM((rows, feats), BF16),
             pltpu.SemaphoreType.DMA((2 + len(loads),)),
         ],
@@ -287,7 +287,6 @@
     )
     parts = [across(part, 2 * j) for j, part in enumerate(parts, 1)]
     returned = [own_rows] + parts
-    relayed = rep == 4
     layout = [(0,), (1, 3), (2,)] if relayed else [(shift,) for shift in range(rep)]
     kinds = [F32, BF16, F32] if relayed else [F32] + [BF16] * (rep - 1)
     own, *sends = pl.pallas_call(
@@ -308,10 +307,14 @@
     )
     if relayed:
         came = shifted(sends[0], 1)
-        small = [shifted(chunk, shift) for shift in (1, 2, 3)]
-        (relay,) = call(relay_kernel, "relay", [shape(rows)], (sends[1], came, chunk))
+        (near,) = call(
+            pair_sum_kernel, "pair_sum", [shape(share)], (chunk, shifted(chunk, 1)), flops=1000000001
+        )
+        (piece,) = call(
+            pair_sum_kernel, "rep_sum", [shape(share)], (near, shifted(near, 2)), flops=1000000001
+        )
+        (relay,) = call(relay_kernel, "relay", [shape(rows)], (sends[1], came, near))
         arrived = [came, shifted(relay, 2)]
-        (piece,) = call(rep_sum_kernel, "rep_sum", [shape(share)], (chunk, *small), flops=1000000001)
     else:
         arrived = [shifted(send, shift) for shift, send in enumerate(sends, 1)]
         piece = jnp.sum(lax.all_gather(chunk, "rep").astype(F32), axis=0).astype(BF16)
@@ -325,7 +328,7 @@
         compiler_params=params,
         cost_estimate=pl.CostEstimate(flops=1, bytes_accessed=1, transcendentals=0),
         name="input_gradient",
-    )(send_rows, weight, own, *returned, *arrived)
+    )(index, weight, own, *returned, *arrived)
     grad_weight = pl.pallas_call(
         functools.partial(join_kernel, 1),
         out_shape=shape(feats, F32),

time: 47.1 us -> 48.8 us (1.036); the launches traced: 47 us -> 48.1 us
  waiting for transfers between devices: 11.8 us -> 16.3 us
  starting transfers between devices: 27.5 us -> 24.7 us
  local copies, waits for them, and re-layouts: 0.59 us -> 0.01 us
    ppermute x8 -> x7, starting transfers between devices: 14.4 us -> 11.7 us  [shifted(): lax.ppermute(value, 'rep', [(i, target(i, shift, rep)) for i in range(rep)])]
    ppermute x8 -> x7, waiting for transfers between devices: 2.68 us -> 4.98 us  [shifted(): lax.ppermute(value, 'rep', [(i, target(i, shift, rep)) for i in range(rep)])]
    ppermute x12, waiting for transfers between devices: 9.08 us -> 11.3 us  [across(): return lax.ppermute(value, 'dom', [(i, i ^ bits) for i in range(groups)])]
    unnamed x8 -> x6, local copies, waits for them, and re-layouts: 0.59 us -> 0.01 us
  transfers between devices with their start and end apart: 20 -> 19, of which waited for: 10 -> 11; matrix products, arithmetic and copies ran while one was open for 0% -> 0% of each run, Pallas kernels for 8% -> 7%
where the time goes in v10:
time: 48.8 us; the launch traced here: 48.1 us
  starting transfers between devices  24.7 us (51%)
  waiting for transfers between devices  16.3 us (33%)
  Pallas kernels  6.38 us (13%)
  between operations  0.74 us (2%)
    ppermute x12, starting transfers between devices, across(): return lax.ppermute(value, 'dom', [(i, i ^ bits) for i in range(groups)])  13 us
    ppermute x7, starting transfers between devices, shifted(): lax.ppermute(value, 'rep', [(i, target(i, shift, rep)) for i in range(rep)])  11.7 us
    ppermute x12, waiting for transfers between devices, across(): return lax.ppermute(value, 'dom', [(i, i ^ bits) for i in range(groups)])  11.3 us
    ppermute x7, waiting for transfers between devices, shifted(): lax.ppermute(value, 'rep', [(i, target(i, shift, rep)) for i in range(rep)])  4.98 us
    pallas_call x1, Pallas kernels, body(): pl.pallas_call(functools.partial(layer_kernel, rep, pairs), out_shape=[sh...  2.02 us
    pallas_call x1, Pallas kernels, body(): pl.pallas_call(pick_kernel, out_shape=[*[shape(pairs * each, BF16, feats)...  1.3 us
    pallas_call x1, Pallas kernels, body(): pl.pallas_call(functools.partial(terms_kernel, rep, layout), out_shape=[j...  1.16 us
    pallas_call x1, Pallas kernels, body(): pl.pallas_call(functools.partial(final_kernel, pairs), out_shape=jax.Shap...  1.05 us
  transfers between devices with their start and end apart: 19, of which 11 were waited for; matrix products, arithmetic and copies ran while one was open for 0% of the time, Pallas kernels for 7%

profile of v10, /device:TPU:0, one launch (start us, length us, event | category | flops | bytes accessed | tf_op | source)
XLA Modules:
  0.0 48.1 jit_solution(8410375744413571252)
XLA Ops:
  0.6 3.1 %collective-permute-start = (bf16[256,256]{1,0:T(8,128)(2,1)}, bf16[256,256]{1,0:T(8,128)(2,1)S(1)}, u32[]{:S(2)}, u32[]{:S(2)}) collective-permute-start(bf16[256,256]{1,0:T(8,128)(2,1)} %refs_0_.3), channel_id=1, source_target_pairs={{0,1},{1,0},{2,3},{3,2},{4,5},{5,4},{6,7},{7,6},{8,9},{9,8},{10,11... | collective-permute-start | bytes 393224 | tf_op jit(solution)/shard_map/ppermute | solution.py:214
  3.7 2.6 %collective-permute-start.1 = (bf16[256,256]{1,0:T(8,128)(2,1)}, bf16[256,256]{1,0:T(8,128)(2,1)S(1)}, u32[]{:S(2)}, u32[]{:S(2)}) collective-permute-start(bf16[256,256]{1,0:T(8,128)(2,1)} %refs_0_.3), channel_id=1, source_target_pairs={{0,2},{1,3},{2,0},{3,1},{4,6},{5,7},{6,4},{7,5},{8,10},{9,11},{10,... | collective-permute-start | bytes 393224 | tf_op jit(solution)/shard_map/ppermute | solution.py:214
  6.3 1.3 %pick_rows.1 = (bf16[64,256]{1,0:T(8,128)(2,1)S(1)}, bf16[64,256]{1,0:T(8,128)(2,1)S(1)}, s32[1,8,16]{2,1,0:T(8,128)S(1)}, bf16[2,8,128,128]{3,2,1,0:T(8,128)(2,...) custom-call(s32[1,8,16]{2,1,0:T(8,128)} %index_ref.1, bf16[256,256]{1,0:T(8,128)(2,1)} %refs_0_.3, ...), custom_call_target="tpu_custom_call" | custom-call | tf_op jit(solution)/shard_map/pick_rows/pallas_call | solution.py:237
  7.6 0.1 collective-permute-start.3
  7.7 1.2 %collective-permute-done.3.came_ref = bf16[64,256]{1,0:T(8,128)(2,1)S(1)} collective-permute-done((bf16[64,256]{1,0:T(8,128)(2,1)S(1)}, bf16[64,256]{1,0:T(8,128)(2,1)S(1)}, u32[]{:S(2)}, u32[]{:S(2)}) %collective-permute-start.3) | collective-permute-done | bytes 32800 | tf_op jit(solution)/shard_map/ppermute | solution.py:217
  8.9 1.7 %collective-permute-start.4 = (bf16[32,256]{1,0:T(8,128)(2,1)S(1)}, bf16[32,256]{1,0:T(8,128)(2,1)S(1)}, u32[]{:S(2)}, u32[]{:S(2)}) collective-permute-start(bf16[32,256]{1,0:T(8,128)(2,1)S(1)} %get-tuple-element.34), channel_id=1, source_target_pairs={{0,8},{4,12},{8,0},{12,4},{16,24},{20,28},{24,16},{28,20},{1,9},{5... | collective-permute-start | bytes 49160 | tf_op jit(solution)/shard_map/ppermute | solution.py:217
  10.6 1.5 %collective-permute-start.5 = (bf16[32,256]{1,0:T(8,128)(2,1)S(1)}, bf16[32,256]{1,0:T(8,128)(2,1)S(1)}, u32[]{:S(2)}, u32[]{:S(2)}) collective-permute-start(bf16[32,256]{1,0:T(8,128)(2,1)S(1)} %get-tuple-element.35), channel_id=1, source_target_pairs={{0,16},{4,20},{8,24},{12,28},{16,0},{20,4},{24,8},{28,12},{1,17},{... | collective-permute-start | bytes 49160 | tf_op jit(solution)/shard_map/ppermute | solution.py:217
  12.1 0.5 %collective-permute-done.4.refs_5_ = bf16[32,256]{1,0:T(8,128)(2,1)S(1)} collective-permute-done((bf16[32,256]{1,0:T(8,128)(2,1)S(1)}, bf16[32,256]{1,0:T(8,128)(2,1)S(1)}, u32[]{:S(2)}, u32[]{:S(2)}) %collective-permute-start.4) | collective-permute-done | bytes 16416 | tf_op jit(solution)/shard_map/ppermute | solution.py:217
  12.7 2.6 %collective-permute-start.6 = (bf16[32,256]{1,0:T(8,128)(2,1)S(1)}, bf16[32,256]{1,0:T(8,128)(2,1)S(1)}, u32[]{:S(2)}, u32[]{:S(2)}) collective-permute-start(bf16[32,256]{1,0:T(8,128)(2,1)S(1)} %get-tuple-element.36), channel_id=1, source_target_pairs={{0,24},{4,28},{8,16},{12,20},{16,8},{20,12},{24,0},{28,4},{1,25},{... | collective-permute-start | bytes 49160 | tf_op jit(solution)/shard_map/ppermute | solution.py:217
  15.3 2.0 %collective-permute-done.6.refs_7_ = bf16[32,256]{1,0:T(8,128)(2,1)S(1)} collective-permute-done((bf16[32,256]{1,0:T(8,128)(2,1)S(1)}, bf16[32,256]{1,0:T(8,128)(2,1)S(1)}, u32[]{:S(2)}, u32[]{:S(2)}) %collective-permute-start.6) | collective-permute-done | bytes 16416 | tf_op jit(solution)/shard_map/ppermute | solution.py:217
  17.3 2.0 %layer.1 = (bf16[256,256]{1,0:T(8,128)(2,1)}, bf16[256,256]{1,0:T(8,128)(2,1)S(1)}, bf16[192,256]{1,0:T(8,128)(2,1)S(1)}, bf16[64,256]{1,0:T(8,128)(2,1)S(1)}, f32[128,256]{1,0:T(8,128)S(1)}) custom-call(s32[2,8]{1,0:T(2,128)S(1)} %get-tuple-element.27.cols_ref, s32[2]{0:T(128)S(1)} %get-tuple-element.28.counts_ref, ...), custom_call_target="tpu_custom_call" | custom-call | tf_op jit(solution)/shard_map/layer/pallas_call | solution.py:261
  19.4 1.3 %collective-permute-done.7.came_ref = bf16[192,256]{1,0:T(8,128)(2,1)S(1)} collective-permute-done((bf16[192,256]{1,0:T(8,128)(2,1)S(1)}, bf16[192,256]{1,0:T(8,128)(2,1)S(1)}, u32[]{:S(2)}, u32[]{:S(2)}) %collective-permute-start.7) | collective-permute-done | bytes 98336 | tf_op jit(solution)/shard_map/ppermute | solution.py:217
  20.7 1.7 %collective-permute-start.8 = (bf16[64,256]{1,0:T(8,128)(2,1)S(1)}, bf16[64,256]{1,0:T(8,128)(2,1)S(1)}, u32[]{:S(2)}, u32[]{:S(2)}) collective-permute-start(bf16[64,256]{1,0:T(8,128)(2,1)S(1)} %get-tuple-element.45), channel_id=1, source_target_pairs={{0,8},{4,12},{8,0},{12,4},{16,24},{20,28},{24,16},{28,20},{1,9},{5... | collective-permute-start | bytes 98312 | tf_op jit(solution)/shard_map/ppermute | solution.py:217
  22.4 1.5 %collective-permute-start.9 = (bf16[64,256]{1,0:T(8,128)(2,1)S(1)}, bf16[64,256]{1,0:T(8,128)(2,1)S(1)}, u32[]{:S(2)}, u32[]{:S(2)}) collective-permute-start(bf16[64,256]{1,0:T(8,128)(2,1)S(1)} %get-tuple-element.46), channel_id=1, source_target_pairs={{0,16},{4,20},{8,24},{12,28},{16,0},{20,4},{24,8},{28,12},{1,17},{... | collective-permute-start | bytes 98312 | tf_op jit(solution)/shard_map/ppermute | solution.py:217
  24.0 0.3 collective-permute-start.10
  24.3 1.2 %terms.1 = (f32[256,256]{1,0:T(8,128)S(1)}, bf16[512,256]{1,0:T(8,128)(2,1)S(1)}, f32[256,256]{1,0:T(8,128)S(1)}) custom-call(s32[2,8]{1,0:T(2,128)S(1)} %get-tuple-element.27.cols_ref, s32[2]{0:T(128)S(1)} %get-tuple-element.28.counts_ref, bf16[2,8,128,128]{3,2,1,0:T(8,128)(2,1)S(1)} %get-tuple-element.29.vals_ref, ...), custom_call_target="tpu_custom_call" | custom-call | flops 500000000 | bytes 1 | tf_op jit(solution)/shard_map/terms/pallas_call | solution.py:292
  25.4 1.6 %collective-permute-start.11 = (bf16[512,256]{1,0:T(8,128)(2,1)S(1)}, bf16[512,256]{1,0:T(8,128)(2,1)S(1)}, u32[]{:S(2)}, u32[]{:S(2)}) collective-permute-start(bf16[512,256]{1,0:T(8,128)(2,1)S(1)} %get-tuple-element.48), channel_id=1, source_target_pairs={{0,1},{1,0},{2,3},{3,2},{4,5},{5,4},{6,7},{7,6},{8,9},{9,8},{10,11... | collective-permute-start | bytes 786440 | tf_op jit(solution)/shard_map/ppermute | solution.py:214
  27.0 1.8 %collective-permute-done.10.refs_2_.refs_3_ = bf16[64,256]{1,0:T(8,128)(2,1)S(1)} collective-permute-done((bf16[64,256]{1,0:T(8,128)(2,1)S(1)}, bf16[64,256]{1,0:T(8,128)(2,1)S(1)}, u32[]{:S(2)}, u32[]{:S(2)}) %collective-permute-start.10) | collective-permute-done | bytes 32800 | tf_op jit(solution)/shard_map/ppermute | solution.py:217
  28.8 1.4 %collective-permute-start.12 = (bf16[32,256]{1,0:T(8,128)(2,1)S(1)}, bf16[32,256]{1,0:T(8,128)(2,1)S(1)}, u32[]{:S(2)}, u32[]{:S(2)}) collective-permute-start(bf16[32,256]{1,0:T(8,128)(2,1)S(1)} %share_sum.1.own_ref), channel_id=1, source_target_pairs={{0,1},{1,0},{2,3},{3,2},{4,5},{5,4},{6,7},{7,6},{8,9},{9,8},{10,11... | collective-permute-start | bytes 49160 | tf_op jit(solution)/shard_map/ppermute | solution.py:214
  30.2 3.2 %collective-permute-done.12.came_ref = bf16[32,256]{1,0:T(8,128)(2,1)S(1)} collective-permute-done((bf16[32,256]{1,0:T(8,128)(2,1)S(1)}, bf16[32,256]{1,0:T(8,128)(2,1)S(1)}, u32[]{:S(2)}, u32[]{:S(2)}) %collective-permute-start.12) | collective-permute-done | bytes 16416 | tf_op jit(solution)/shard_map/ppermute | solution.py:214
  33.4 2.6 %collective-permute-start.14 = (bf16[32,256]{1,0:T(8,128)(2,1)S(1)}, bf16[32,256]{1,0:T(8,128)(2,1)S(1)}, u32[]{:S(2)}, u32[]{:S(2)}) collective-permute-start(bf16[32,256]{1,0:T(8,128)(2,1)S(1)} %pair_sum.1.refs_0_.own_ref), channel_id=1, source_target_pairs={{0,2},{1,3},{2,0},{3,1},{4,6},{5,7},{6,4},{7,5},{8,10},{9,11},{10,... | collective-permute-start | bytes 49160 | tf_op jit(solution)/shard_map/ppermute | solution.py:214
  36.0 0.4 collective-permute-start.13
  36.4 1.8 %collective-permute-done.14.came_ref = bf16[32,256]{1,0:T(8,128)(2,1)S(1)} collective-permute-done((bf16[32,256]{1,0:T(8,128)(2,1)S(1)}, bf16[32,256]{1,0:T(8,128)(2,1)S(1)}, u32[]{:S(2)}, u32[]{:S(2)}) %collective-permute-start.14) | collective-permute-done | bytes 16416 | tf_op jit(solution)/shard_map/ppermute | solution.py:214
  38.2 1.7 %collective-permute-start.15 = (bf16[32,256]{1,0:T(8,128)(2,1)S(1)}, bf16[32,256]{1,0:T(8,128)(2,1)S(1)}, u32[]{:S(2)}, u32[]{:S(2)}) collective-permute-start(bf16[32,256]{1,0:T(8,128)(2,1)S(1)} %rep_sum.1.refs_0_), channel_id=1, source_target_pairs={{0,8},{4,12},{8,0},{12,4},{16,24},{20,28},{24,16},{28,20},{1,9},{5... | collective-permute-start | bytes 49160 | tf_op jit(solution)/shard_map/ppermute | solution.py:217
  39.9 1.5 %collective-permute-start.16 = (bf16[32,256]{1,0:T(8,128)(2,1)S(1)}, bf16[32,256]{1,0:T(8,128)(2,1)S(1)}, u32[]{:S(2)}, u32[]{:S(2)}) collective-permute-start(bf16[32,256]{1,0:T(8,128)(2,1)S(1)} %rep_sum.1.refs_0_), channel_id=1, source_target_pairs={{0,16},{4,20},{8,24},{12,28},{16,0},{20,4},{24,8},{28,12},{1,17},{... | collective-permute-start | bytes 49160 | tf_op jit(solution)/shard_map/ppermute | solution.py:217
  41.4 0.3 collective-permute-start.17
  41.7 0.2 collective-permute-done.15.refs_1_
  41.9 1.7 %collective-permute-done.16.refs_2_ = bf16[32,256]{1,0:T(8,128)(2,1)S(1)} collective-permute-done((bf16[32,256]{1,0:T(8,128)(2,1)S(1)}, bf16[32,256]{1,0:T(8,128)(2,1)S(1)}, u32[]{:S(2)}, u32[]{:S(2)}) %collective-permute-start.16) | collective-permute-done | bytes 16416 | tf_op jit(solution)/shard_map/ppermute | solution.py:217
  43.6 2.4 %collective-permute-done.17.refs_3_ = bf16[32,256]{1,0:T(8,128)(2,1)S(1)} collective-permute-done((bf16[32,256]{1,0:T(8,128)(2,1)S(1)}, bf16[32,256]{1,0:T(8,128)(2,1)S(1)}, u32[]{:S(2)}, u32[]{:S(2)}) %collective-permute-start.17) | collective-permute-done | bytes 16416 | tf_op jit(solution)/shard_map/ppermute | solution.py:217
  46.1 1.1 %input_gradient.1.order_ref = bf16[256,256]{1,0:T(8,128)(2,1)} custom-call(s32[1,8,16]{2,1,0:T(8,128)S(1)} %get-tuple-element.38.index_ref, bf16[256,256]{1,0:T(8,128)(2,1)S(1)} %copy-done.1, f32[256,256]{1,0:T(8,128)S(1)} %get-tuple-element.44.own_ref, bf16[32,256]{1,0:T(8,128)(2,1)S(1)} %get-tuple-element.43.order_ref.refs_0_, ...), custom_call_target="tpu_custom_call" | custom-call | flops 1 | bytes 1 | tf_op jit(solution)/shard_map/input_gradient/pallas_call | solution.py:323
  47.2 0.2 collective-permute-done.18.got_ref
  47.4 0.7 %join.1 = f32[256,256]{1,0:T(8,128)} custom-call(bf16[128,256]{1,0:T(8,128)(2,1)S(1)} %half.1.own_ref, bf16[128,256]{1,0:T(8,128)(2,1)S(1)} %collective-permute-done.18.got_ref, bf16[256,256]{1,0:T(8,128)(2,1)} %input_gradient.1.order_ref), custom_call_target="tpu_custom_call" | custom-call | flops 1 | bytes 1 | tf_op jit(solution)/shard_map/join/pallas_call | solution.py:332
  (24 shorter events, 0.2 us)
Async XLA Ops:
  0.6 16.7 %collective-permute-start = (bf16[256,256]{1,0:T(8,128)(2,1)}, bf16[256,256]{1,0:T(8,128)(2,1)S(1)}, u32[]{:S(2)}, u32[]{:S(2)}) collective-permute-start(bf16[256,256]{1,0:T(8,128)(2,1)} %refs_0_.3), channel_id=1, source_target_pairs={{0,1},{1,0},{2,3},{3,2},{4,5},{5,4},{6,7},{7,6},{8,9},{9,8},{10,11... | collective-permute-start | bytes 393224 | tf_op jit(solution)/shard_map/ppermute | solution.py:214
  3.7 13.6 %collective-permute-start.1 = (bf16[256,256]{1,0:T(8,128)(2,1)}, bf16[256,256]{1,0:T(8,128)(2,1)S(1)}, u32[]{:S(2)}, u32[]{:S(2)}) collective-permute-start(bf16[256,256]{1,0:T(8,128)(2,1)} %refs_0_.3), channel_id=1, source_target_pairs={{0,2},{1,3},{2,0},{3,1},{4,6},{5,7},{6,4},{7,5},{8,10},{9,11},{10,... | collective-permute-start | bytes 393224 | tf_op jit(solution)/shard_map/ppermute | solution.py:214
  6.3 11.0 %collective-permute-start.2 = (bf16[256,256]{1,0:T(8,128)(2,1)}, bf16[256,256]{1,0:T(8,128)(2,1)S(1)}, u32[]{:S(2)}, u32[]{:S(2)}) collective-permute-start(bf16[256,256]{1,0:T(8,128)(2,1)} %refs_0_.3), channel_id=1, source_target_pairs={{0,3},{1,2},{2,1},{3,0},{4,7},{5,6},{6,5},{7,4},{8,11},{9,10},{10,... | collective-permute-start | bytes 393224 | tf_op jit(solution)/shard_map/ppermute | solution.py:214
  6.3 11.0 %copy-start = (bf16[256,256]{1,0:T(8,128)(2,1)S(1)}, bf16[256,256]{1,0:T(8,128)(2,1)}, u32[]{:S(2)}) copy-start(bf16[256,256]{1,0:T(8,128)(2,1)} %refs_0_.3) | copy-start | bytes 393220
  6.3 11.0 %copy-start.1 = (bf16[256,256]{1,0:T(8,128)(2,1)S(1)}, bf16[256,256]{1,0:T(8,128)(2,1)}, u32[]{:S(2)}) copy-start(bf16[256,256]{1,0:T(8,128)(2,1)} %weight_ref.3) | copy-start | bytes 393220
  7.6 9.7 %copy-start.2 = (bf16[256,128]{1,0:T(8,128)(2,1)S(1)}, bf16[256,128]{1,0:T(8,128)(2,1)}, u32[]{:S(2)}) copy-start(bf16[256,128]{1,0:T(8,128)(2,1)} %bnd_ref.1) | copy-start | bytes 196612
  7.6 1.3 %collective-permute-start.3 = (bf16[64,256]{1,0:T(8,128)(2,1)S(1)}, bf16[64,256]{1,0:T(8,128)(2,1)S(1)}, u32[]{:S(2)}, u32[]{:S(2)}) collective-permute-start(bf16[64,256]{1,0:T(8,128)(2,1)S(1)} %get-tuple-element.32), channel_id=1, source_target_pairs={{0,4},{4,0},{8,12},{12,8},{16,20},{20,16},{24,28},{28,24},{1,5},{5... | collective-permute-start | bytes 98312 | tf_op jit(solution)/shard_map/ppermute | solution.py:217
  8.9 3.7 %collective-permute-start.4 = (bf16[32,256]{1,0:T(8,128)(2,1)S(1)}, bf16[32,256]{1,0:T(8,128)(2,1)S(1)}, u32[]{:S(2)}, u32[]{:S(2)}) collective-permute-start(bf16[32,256]{1,0:T(8,128)(2,1)S(1)} %get-tuple-element.34), channel_id=1, source_target_pairs={{0,8},{4,12},{8,0},{12,4},{16,24},{20,28},{24,16},{28,20},{1,9},{5... | collective-permute-start | bytes 49160 | tf_op jit(solution)/shard_map/ppermute | solution.py:217
  10.6 4.7 %collective-permute-start.5 = (bf16[32,256]{1,0:T(8,128)(2,1)S(1)}, bf16[32,256]{1,0:T(8,128)(2,1)S(1)}, u32[]{:S(2)}, u32[]{:S(2)}) collective-permute-start(bf16[32,256]{1,0:T(8,128)(2,1)S(1)} %get-tuple-element.35), channel_id=1, source_target_pairs={{0,16},{4,20},{8,24},{12,28},{16,0},{20,4},{24,8},{28,12},{1,17},{... | collective-permute-start | bytes 49160 | tf_op jit(solution)/shard_map/ppermute | solution.py:217
  12.7 4.6 %collective-permute-start.6 = (bf16[32,256]{1,0:T(8,128)(2,1)S(1)}, bf16[32,256]{1,0:T(8,128)(2,1)S(1)}, u32[]{:S(2)}, u32[]{:S(2)}) collective-permute-start(bf16[32,256]{1,0:T(8,128)(2,1)S(1)} %get-tuple-element.36), channel_id=1, source_target_pairs={{0,24},{4,28},{8,16},{12,20},{16,8},{20,12},{24,0},{28,4},{1,25},{... | collective-permute-start | bytes 49160 | tf_op jit(solution)/shard_map/ppermute | solution.py:217
  19.4 1.3 %collective-permute-start.7 = (bf16[192,256]{1,0:T(8,128)(2,1)S(1)}, bf16[192,256]{1,0:T(8,128)(2,1)S(1)}, u32[]{:S(2)}, u32[]{:S(2)}) collective-permute-start(bf16[192,256]{1,0:T(8,128)(2,1)S(1)} %get-tuple-element.42), channel_id=1, source_target_pairs={{0,4},{4,0},{8,12},{12,8},{16,20},{20,16},{24,28},{28,24},{1,5},{5... | collective-permute-start | bytes 294920 | tf_op jit(solution)/shard_map/ppermute | solution.py:217
  20.7 6.3 %collective-permute-start.8 = (bf16[64,256]{1,0:T(8,128)(2,1)S(1)}, bf16[64,256]{1,0:T(8,128)(2,1)S(1)}, u32[]{:S(2)}, u32[]{:S(2)}) collective-permute-start(bf16[64,256]{1,0:T(8,128)(2,1)S(1)} %get-tuple-element.45), channel_id=1, source_target_pairs={{0,8},{4,12},{8,0},{12,4},{16,24},{20,28},{24,16},{28,20},{1,9},{5... | collective-permute-start | bytes 98312 | tf_op jit(solution)/shard_map/ppermute | solution.py:217
  22.4 4.6 %collective-permute-start.9 = (bf16[64,256]{1,0:T(8,128)(2,1)S(1)}, bf16[64,256]{1,0:T(8,128)(2,1)S(1)}, u32[]{:S(2)}, u32[]{:S(2)}) collective-permute-start(bf16[64,256]{1,0:T(8,128)(2,1)S(1)} %get-tuple-element.46), channel_id=1, source_target_pairs={{0,16},{4,20},{8,24},{12,28},{16,0},{20,4},{24,8},{28,12},{1,17},{... | collective-permute-start | bytes 98312 | tf_op jit(solution)/shard_map/ppermute | solution.py:217
  24.0 4.8 %collective-permute-start.10 = (bf16[64,256]{1,0:T(8,128)(2,1)S(1)}, bf16[64,256]{1,0:T(8,128)(2,1)S(1)}, u32[]{:S(2)}, u32[]{:S(2)}) collective-permute-start(bf16[64,256]{1,0:T(8,128)(2,1)S(1)} %get-tuple-element.47), channel_id=1, source_target_pairs={{0,24},{4,28},{8,16},{12,20},{16,8},{20,12},{24,0},{28,4},{1,25},{... | collective-permute-start | bytes 98312 | tf_op jit(solution)/shard_map/ppermute | solution.py:217
  25.4 10.6 %collective-permute-start.11 = (bf16[512,256]{1,0:T(8,128)(2,1)S(1)}, bf16[512,256]{1,0:T(8,128)(2,1)S(1)}, u32[]{:S(2)}, u32[]{:S(2)}) collective-permute-start(bf16[512,256]{1,0:T(8,128)(2,1)S(1)} %get-tuple-element.48), channel_id=1, source_target_pairs={{0,1},{1,0},{2,3},{3,2},{4,5},{5,4},{6,7},{7,6},{8,9},{9,8},{10,11... | collective-permute-start | bytes 786440 | tf_op jit(solution)/shard_map/ppermute | solution.py:214
  28.8 4.6 %collective-permute-start.12 = (bf16[32,256]{1,0:T(8,128)(2,1)S(1)}, bf16[32,256]{1,0:T(8,128)(2,1)S(1)}, u32[]{:S(2)}, u32[]{:S(2)}) collective-permute-start(bf16[32,256]{1,0:T(8,128)(2,1)S(1)} %share_sum.1.own_ref), channel_id=1, source_target_pairs={{0,1},{1,0},{2,3},{3,2},{4,5},{5,4},{6,7},{7,6},{8,9},{9,8},{10,11... | collective-permute-start | bytes 49160 | tf_op jit(solution)/shard_map/ppermute | solution.py:214
  33.4 4.8 %collective-permute-start.14 = (bf16[32,256]{1,0:T(8,128)(2,1)S(1)}, bf16[32,256]{1,0:T(8,128)(2,1)S(1)}, u32[]{:S(2)}, u32[]{:S(2)}) collective-permute-start(bf16[32,256]{1,0:T(8,128)(2,1)S(1)} %pair_sum.1.refs_0_.own_ref), channel_id=1, source_target_pairs={{0,2},{1,3},{2,0},{3,1},{4,6},{5,7},{6,4},{7,5},{8,10},{9,11},{10,... | collective-permute-start | bytes 49160 | tf_op jit(solution)/shard_map/ppermute | solution.py:214
  36.0 10.1 %collective-permute-start.13 = (bf16[256,256]{1,0:T(8,128)(2,1)S(1)}, bf16[256,256]{1,0:T(8,128)(2,1)S(1)}, u32[]{:S(2)}, u32[]{:S(2)}) collective-permute-start(bf16[256,256]{1,0:T(8,128)(2,1)S(1)} %relay.1), channel_id=1, source_target_pairs={{0,2},{1,3},{2,0},{3,1},{4,6},{5,7},{6,4},{7,5},{8,10},{9,11},{10,... | collective-permute-start | bytes 393224 | tf_op jit(solution)/shard_map/ppermute | solution.py:214
  38.2 3.7 %collective-permute-start.15 = (bf16[32,256]{1,0:T(8,128)(2,1)S(1)}, bf16[32,256]{1,0:T(8,128)(2,1)S(1)}, u32[]{:S(2)}, u32[]{:S(2)}) collective-permute-start(bf16[32,256]{1,0:T(8,128)(2,1)S(1)} %rep_sum.1.refs_0_), channel_id=1, source_target_pairs={{0,8},{4,12},{8,0},{12,4},{16,24},{20,28},{24,16},{28,20},{1,9},{5... | collective-permute-start | bytes 49160 | tf_op jit(solution)/shard_map/ppermute | solution.py:217
  39.9 3.7 %collective-permute-start.16 = (bf16[32,256]{1,0:T(8,128)(2,1)S(1)}, bf16[32,256]{1,0:T(8,128)(2,1)S(1)}, u32[]{:S(2)}, u32[]{:S(2)}) collective-permute-start(bf16[32,256]{1,0:T(8,128)(2,1)S(1)} %rep_sum.1.refs_0_), channel_id=1, source_target_pairs={{0,16},{4,20},{8,24},{12,28},{16,0},{20,4},{24,8},{28,12},{1,17},{... | collective-permute-start | bytes 49160 | tf_op jit(solution)/shard_map/ppermute | solution.py:217
  41.4 4.6 %collective-permute-start.17 = (bf16[32,256]{1,0:T(8,128)(2,1)S(1)}, bf16[32,256]{1,0:T(8,128)(2,1)S(1)}, u32[]{:S(2)}, u32[]{:S(2)}) collective-permute-start(bf16[32,256]{1,0:T(8,128)(2,1)S(1)} %rep_sum.1.refs_0_), channel_id=1, source_target_pairs={{0,24},{4,28},{8,16},{12,20},{16,8},{20,12},{24,0},{28,4},{1,25},{... | collective-permute-start | bytes 49160 | tf_op jit(solution)/shard_map/ppermute | solution.py:217
  46.0 1.3 %collective-permute-start.18 = (bf16[128,256]{1,0:T(8,128)(2,1)S(1)}, bf16[128,256]{1,0:T(8,128)(2,1)S(1)}, u32[]{:S(2)}, u32[]{:S(2)}) collective-permute-start(bf16[128,256]{1,0:T(8,128)(2,1)S(1)} %half.1.own_ref), channel_id=1, source_target_pairs={{0,4},{4,0},{8,12},{12,8},{16,20},{20,16},{24,28},{28,24},{1,5},{5... | collective-permute-start | bytes 196616 | tf_op jit(solution)/shard_map/ppermute | solution.py:217

commit v11 on v10

--- a/solution.py
+++ b/solution.py
@@ -62,7 +62,8 @@
         out_ref[each:, :] = came_ref[j * each : (j + 1) * each, :]
 
 
-def weighted_stage_kernel(each, keep_ref, half_ref, came_ref, own_ref, share_ref, *refs):
+def weighted_stage_kernel(each, keep_ref, half_ref, came_ref, order_ref, own_ref, share_ref, *refs):
+    del order_ref
     outs, summed = refs[:-1], refs[-1]
     pairs = len(outs) + 1
     summed[...] = half_ref[...] + came_ref[pairs * each :, :].astype(F32)
@@ -150,8 +151,7 @@
     send_ref[pairs * each :, :] = partial[pl.ds(pl.multiple_of((1 - mine) * half, half), half), :].astype(BF16)
 
 
-def terms_kernel(rep, layout, cols_ref, counts_ref, vals_ref, grad_ref, order_ref, *refs):
-    del order_ref
+def terms_kernel(rep, layout, cols_ref, counts_ref, vals_ref, grad_ref, *refs):
     outs, terms = refs[:-1], refs[-1]
     me = lax.axis_index("rep")
     tiles, slots = cols_ref.shape
@@ -278,15 +278,6 @@
         compiler_params=params,
         name="layer",
     )(tile_cols, tile_counts, tile_vals, bnd_adj, cotangent, weight, *blocks, *received)
-    own_rows, own_share, *parts = call(
-        functools.partial(weighted_stage_kernel, each),
-        "pair_gradients",
-        [shape(2 * each), shape(share, F32)] + [shape(2 * each + share)] * (pairs - 1),
-        (keep, mine, across(send, 1)),
-        [pltpu.VMEM((half, width), F32)],
-    )
-    parts = [across(part, 2 * j) for j, part in enumerate(parts, 1)]
-    returned = [own_rows] + parts
     layout = [(0,), (1, 3), (2,)] if relayed else [(shift,) for shift in range(rep)]
     kinds = [F32, BF16, F32] if relayed else [F32] + [BF16] * (rep - 1)
     own, *sends = pl.pallas_call(
@@ -295,15 +286,24 @@
             jax.ShapeDtypeStruct((len(shifts) * rows, width), kind)
             for shifts, kind in zip(layout, kinds)
         ],
-        in_specs=[SMEM] * 2 + [VMEM] * 3,
+        in_specs=[SMEM] * 2 + [VMEM] * 2,
         out_specs=[VMEM] * len(layout),
         scratch_shapes=[pltpu.VMEM((rep * tiles, TILE, width), F32)],
         compiler_params=params,
         cost_estimate=pl.CostEstimate(flops=500000001, bytes_accessed=1, transcendentals=0),
         name="terms",
-    )(tile_cols, tile_counts, tile_vals, grad, own_rows)
+    )(tile_cols, tile_counts, tile_vals, grad)
+    own_rows, own_share, *parts = call(
+        functools.partial(weighted_stage_kernel, each),
+        "pair_gradients",
+        [shape(2 * each), shape(share, F32)] + [shape(2 * each + share)] * (pairs - 1),
+        (keep, mine, across(send, 1), own),
+        [pltpu.VMEM((half, width), F32)],
+    )
+    parts = [across(part, 2 * j) for j, part in enumerate(parts, 1)]
+    returned = [own_rows] + parts
     (chunk,) = call(
-        functools.partial(share_sum_kernel, each), "share_sum", [shape(share)], (own_share, *parts), flops=4000000001
+        functools.partial(share_sum_kernel, each), "share_sum", [shape(share)], (own_share, *parts), flops=1000000001
     )
     if relayed:
         came = shifted(sends[0], 1)

time: 48.8 us -> 47.6 us (0.975); the launches traced: 48.1 us -> 47.5 us
  waiting for transfers between devices: 16.3 us -> 15.7 us
  transfers between devices with their start and end apart: 19 -> 19, of which waited for: 11 -> 12; matrix products, arithmetic and copies ran while one was open for 0% -> 0% of each run, Pallas kernels for 7% -> 8%
where the time goes in v11:
time: 47.6 us; the launch traced here: 47.5 us
  starting transfers between devices  24.6 us (52%)
  waiting for transfers between devices  15.7 us (33%)
  Pallas kernels  6.38 us (13%)
  between operations  0.74 us (2%)
    ppermute x12, starting transfers between devices, across(): return lax.ppermute(value, 'dom', [(i, i ^ bits) for i in range(groups)])  13 us
    ppermute x7, starting transfers between devices, shifted(): lax.ppermute(value, 'rep', [(i, target(i, shift, rep)) for i in range(rep)])  11.6 us
    ppermute x12, waiting for transfers between devices, across(): return lax.ppermute(value, 'dom', [(i, i ^ bits) for i in range(groups)])  11 us
    ppermute x7, waiting for transfers between devices, shifted(): lax.ppermute(value, 'rep', [(i, target(i, shift, rep)) for i in range(rep)])  4.72 us
    pallas_call x1, Pallas kernels, body(): pl.pallas_call(functools.partial(layer_kernel, rep, pairs), out_shape=[sh...  2.02 us
    pallas_call x1, Pallas kernels, body(): pl.pallas_call(pick_kernel, out_shape=[*[shape(pairs * each, BF16, feats)...  1.3 us
    pallas_call x1, Pallas kernels, body(): pl.pallas_call(functools.partial(terms_kernel, rep, layout), out_shape=[j...  1.16 us
    pallas_call x1, Pallas kernels, body(): pl.pallas_call(functools.partial(final_kernel, pairs), out_shape=jax.Shap...  1.05 us
  transfers between devices with their start and end apart: 19, of which 12 were waited for; matrix products, arithmetic and copies ran while one was open for 0% of the time, Pallas kernels for 8%

profile of v11, /device:TPU:0, one launch (start us, length us, event | category | flops | bytes accessed | tf_op | source)
XLA Modules:
  0.0 47.5 jit_solution(3651734719536565455)
XLA Ops:
  0.6 4.1 %collective-permute-start.1 = (bf16[256,256]{1,0:T(8,128)(2,1)}, bf16[256,256]{1,0:T(8,128)(2,1)S(1)}, u32[]{:S(2)}, u32[]{:S(2)}) collective-permute-start(bf16[256,256]{1,0:T(8,128)(2,1)} %refs_0_.3), channel_id=1, source_target_pairs={{0,2},{1,3},{2,0},{3,1},{4,6},{5,7},{6,4},{7,5},{8,10},{9,11},{10,... | collective-permute-start | bytes 393224 | tf_op jit(solution)/shard_map/ppermute | solution.py:214
  4.7 1.6 %collective-permute-start = (bf16[256,256]{1,0:T(8,128)(2,1)}, bf16[256,256]{1,0:T(8,128)(2,1)S(1)}, u32[]{:S(2)}, u32[]{:S(2)}) collective-permute-start(bf16[256,256]{1,0:T(8,128)(2,1)} %refs_0_.3), channel_id=1, source_target_pairs={{0,1},{1,0},{2,3},{3,2},{4,5},{5,4},{6,7},{7,6},{8,9},{9,8},{10,11... | collective-permute-start | bytes 393224 | tf_op jit(solution)/shard_map/ppermute | solution.py:214
  6.3 1.3 %pick_rows.1 = (bf16[64,256]{1,0:T(8,128)(2,1)S(1)}, bf16[64,256]{1,0:T(8,128)(2,1)S(1)}, s32[1,8,16]{2,1,0:T(8,128)S(1)}, bf16[2,8,128,128]{3,2,1,0:T(8,128)(2,...) custom-call(s32[1,8,16]{2,1,0:T(8,128)} %index_ref.1, bf16[256,256]{1,0:T(8,128)(2,1)} %refs_0_.3, ...), custom_call_target="tpu_custom_call" | custom-call | tf_op jit(solution)/shard_map/pick_rows/pallas_call | solution.py:237
  7.7 1.2 %collective-permute-done.3.came_ref = bf16[64,256]{1,0:T(8,128)(2,1)S(1)} collective-permute-done((bf16[64,256]{1,0:T(8,128)(2,1)S(1)}, bf16[64,256]{1,0:T(8,128)(2,1)S(1)}, u32[]{:S(2)}, u32[]{:S(2)}) %collective-permute-start.3) | collective-permute-done | bytes 32800 | tf_op jit(solution)/shard_map/ppermute | solution.py:217
  8.9 1.7 %collective-permute-start.4 = (bf16[32,256]{1,0:T(8,128)(2,1)S(1)}, bf16[32,256]{1,0:T(8,128)(2,1)S(1)}, u32[]{:S(2)}, u32[]{:S(2)}) collective-permute-start(bf16[32,256]{1,0:T(8,128)(2,1)S(1)} %get-tuple-element.34), channel_id=1, source_target_pairs={{0,8},{4,12},{8,0},{12,4},{16,24},{20,28},{24,16},{28,20},{1,9},{5... | collective-permute-start | bytes 49160 | tf_op jit(solution)/shard_map/ppermute | solution.py:217
  10.6 1.5 %collective-permute-start.5 = (bf16[32,256]{1,0:T(8,128)(2,1)S(1)}, bf16[32,256]{1,0:T(8,128)(2,1)S(1)}, u32[]{:S(2)}, u32[]{:S(2)}) collective-permute-start(bf16[32,256]{1,0:T(8,128)(2,1)S(1)} %get-tuple-element.35), channel_id=1, source_target_pairs={{0,16},{4,20},{8,24},{12,28},{16,0},{20,4},{24,8},{28,12},{1,17},{... | collective-permute-start | bytes 49160 | tf_op jit(solution)/shard_map/ppermute | solution.py:217
  12.1 0.5 %collective-permute-done.4.refs_5_ = bf16[32,256]{1,0:T(8,128)(2,1)S(1)} collective-permute-done((bf16[32,256]{1,0:T(8,128)(2,1)S(1)}, bf16[32,256]{1,0:T(8,128)(2,1)S(1)}, u32[]{:S(2)}, u32[]{:S(2)}) %collective-permute-start.4) | collective-permute-done | bytes 16416 | tf_op jit(solution)/shard_map/ppermute | solution.py:217
  12.7 2.6 %collective-permute-start.6 = (bf16[32,256]{1,0:T(8,128)(2,1)S(1)}, bf16[32,256]{1,0:T(8,128)(2,1)S(1)}, u32[]{:S(2)}, u32[]{:S(2)}) collective-permute-start(bf16[32,256]{1,0:T(8,128)(2,1)S(1)} %get-tuple-element.36), channel_id=1, source_target_pairs={{0,24},{4,28},{8,16},{12,20},{16,8},{20,12},{24,0},{28,4},{1,25},{... | collective-permute-start | bytes 49160 | tf_op jit(solution)/shard_map/ppermute | solution.py:217
  15.3 2.0 %collective-permute-done.6.refs_7_ = bf16[32,256]{1,0:T(8,128)(2,1)S(1)} collective-permute-done((bf16[32,256]{1,0:T(8,128)(2,1)S(1)}, bf16[32,256]{1,0:T(8,128)(2,1)S(1)}, u32[]{:S(2)}, u32[]{:S(2)}) %collective-permute-start.6) | collective-permute-done | bytes 16416 | tf_op jit(solution)/shard_map/ppermute | solution.py:217
  17.3 2.0 %layer.1 = (bf16[256,256]{1,0:T(8,128)(2,1)}, bf16[256,256]{1,0:T(8,128)(2,1)S(1)}, bf16[192,256]{1,0:T(8,128)(2,1)S(1)}, bf16[64,256]{1,0:T(8,128)(2,1)S(1)}, f32[128,256]{1,0:T(8,128)S(1)}) custom-call(s32[2,8]{1,0:T(2,128)S(1)} %get-tuple-element.27.cols_ref, s32[2]{0:T(128)S(1)} %get-tuple-element.28.counts_ref, ...), custom_call_target="tpu_custom_call" | custom-call | tf_op jit(solution)/shard_map/layer/pallas_call | solution.py:261
  19.4 1.2 %terms.1 = (f32[256,256]{1,0:T(8,128)S(1)}, bf16[512,256]{1,0:T(8,128)(2,1)S(1)}, f32[256,256]{1,0:T(8,128)S(1)}) custom-call(s32[2,8]{1,0:T(2,128)S(1)} %get-tuple-element.27.cols_ref, s32[2]{0:T(128)S(1)} %get-tuple-element.28.counts_ref, bf16[2,8,128,128]{3,2,1,0:T(8,128)(2,1)S(1)} %get-tuple-element.29.vals_ref, ...), custom_call_target="tpu_custom_call" | custom-call | flops 500000000 | bytes 1 | tf_op jit(solution)/shard_map/terms/pallas_call | solution.py:283
  20.5 0.9 %collective-permute-start.11 = (bf16[512,256]{1,0:T(8,128)(2,1)S(1)}, bf16[512,256]{1,0:T(8,128)(2,1)S(1)}, u32[]{:S(2)}, u32[]{:S(2)}) collective-permute-start(bf16[512,256]{1,0:T(8,128)(2,1)S(1)} %get-tuple-element.48), channel_id=1, source_target_pairs={{0,1},{1,0},{2,3},{3,2},{4,5},{5,4},{6,7},{7,6},{8,9},{9,8},{10,11... | collective-permute-start | bytes 786440 | tf_op jit(solution)/shard_map/ppermute | solution.py:214
  21.5 1.6 %collective-permute-start.8 = (bf16[64,256]{1,0:T(8,128)(2,1)S(1)}, bf16[64,256]{1,0:T(8,128)(2,1)S(1)}, u32[]{:S(2)}, u32[]{:S(2)}) collective-permute-start(bf16[64,256]{1,0:T(8,128)(2,1)S(1)} %get-tuple-element.45), channel_id=1, source_target_pairs={{0,8},{4,12},{8,0},{12,4},{16,24},{20,28},{24,16},{28,20},{1,9},{5... | collective-permute-start | bytes 98312 | tf_op jit(solution)/shard_map/ppermute | solution.py:217
  23.1 1.5 %collective-permute-start.9 = (bf16[64,256]{1,0:T(8,128)(2,1)S(1)}, bf16[64,256]{1,0:T(8,128)(2,1)S(1)}, u32[]{:S(2)}, u32[]{:S(2)}) collective-permute-start(bf16[64,256]{1,0:T(8,128)(2,1)S(1)} %get-tuple-element.46), channel_id=1, source_target_pairs={{0,16},{4,20},{8,24},{12,28},{16,0},{20,4},{24,8},{28,12},{1,17},{... | collective-permute-start | bytes 98312 | tf_op jit(solution)/shard_map/ppermute | solution.py:217
  24.6 0.5 %collective-permute-start.10 = (bf16[64,256]{1,0:T(8,128)(2,1)S(1)}, bf16[64,256]{1,0:T(8,128)(2,1)S(1)}, u32[]{:S(2)}, u32[]{:S(2)}) collective-permute-start(bf16[64,256]{1,0:T(8,128)(2,1)S(1)} %get-tuple-element.47), channel_id=1, source_target_pairs={{0,24},{4,28},{8,16},{12,20},{16,8},{20,12},{24,0},{28,4},{1,25},{... | collective-permute-start | bytes 98312 | tf_op jit(solution)/shard_map/ppermute | solution.py:217
  25.1 0.4 collective-permute-done.8.refs_0_.refs_1_
  25.5 1.5 %collective-permute-done.9.refs_1_.refs_2_ = bf16[64,256]{1,0:T(8,128)(2,1)S(1)} collective-permute-done((bf16[64,256]{1,0:T(8,128)(2,1)S(1)}, bf16[64,256]{1,0:T(8,128)(2,1)S(1)}, u32[]{:S(2)}, u32[]{:S(2)}) %collective-permute-start.9) | collective-permute-done | bytes 32800 | tf_op jit(solution)/shard_map/ppermute | solution.py:217
  27.0 2.4 %collective-permute-done.10.refs_2_.refs_3_ = bf16[64,256]{1,0:T(8,128)(2,1)S(1)} collective-permute-done((bf16[64,256]{1,0:T(8,128)(2,1)S(1)}, bf16[64,256]{1,0:T(8,128)(2,1)S(1)}, u32[]{:S(2)}, u32[]{:S(2)}) %collective-permute-start.10) | collective-permute-done | bytes 32800 | tf_op jit(solution)/shard_map/ppermute | solution.py:217
  29.4 1.4 %collective-permute-start.12 = (bf16[32,256]{1,0:T(8,128)(2,1)S(1)}, bf16[32,256]{1,0:T(8,128)(2,1)S(1)}, u32[]{:S(2)}, u32[]{:S(2)}) collective-permute-start(bf16[32,256]{1,0:T(8,128)(2,1)S(1)} %share_sum.1.own_ref), channel_id=1, source_target_pairs={{0,1},{1,0},{2,3},{3,2},{4,5},{5,4},{6,7},{7,6},{8,9},{9,8},{10,11... | collective-permute-start | bytes 49160 | tf_op jit(solution)/shard_map/ppermute | solution.py:214
  30.8 2.4 %collective-permute-done.12.came_ref = bf16[32,256]{1,0:T(8,128)(2,1)S(1)} collective-permute-done((bf16[32,256]{1,0:T(8,128)(2,1)S(1)}, bf16[32,256]{1,0:T(8,128)(2,1)S(1)}, u32[]{:S(2)}, u32[]{:S(2)}) %collective-permute-start.12) | collective-permute-done | bytes 16416 | tf_op jit(solution)/shard_map/ppermute | solution.py:214
  33.2 3.5 %collective-permute-start.14 = (bf16[32,256]{1,0:T(8,128)(2,1)S(1)}, bf16[32,256]{1,0:T(8,128)(2,1)S(1)}, u32[]{:S(2)}, u32[]{:S(2)}) collective-permute-start(bf16[32,256]{1,0:T(8,128)(2,1)S(1)} %pair_sum.1.refs_0_.own_ref), channel_id=1, source_target_pairs={{0,2},{1,3},{2,0},{3,1},{4,6},{5,7},{6,4},{7,5},{8,10},{9,11},{10,... | collective-permute-start | bytes 49160 | tf_op jit(solution)/shard_map/ppermute | solution.py:214
  36.7 0.1 collective-permute-start.13
  36.8 2.3 %collective-permute-done.14.came_ref = bf16[32,256]{1,0:T(8,128)(2,1)S(1)} collective-permute-done((bf16[32,256]{1,0:T(8,128)(2,1)S(1)}, bf16[32,256]{1,0:T(8,128)(2,1)S(1)}, u32[]{:S(2)}, u32[]{:S(2)}) %collective-permute-start.14) | collective-permute-done | bytes 16416 | tf_op jit(solution)/shard_map/ppermute | solution.py:214
  39.2 1.6 %collective-permute-start.17 = (bf16[32,256]{1,0:T(8,128)(2,1)S(1)}, bf16[32,256]{1,0:T(8,128)(2,1)S(1)}, u32[]{:S(2)}, u32[]{:S(2)}) collective-permute-start(bf16[32,256]{1,0:T(8,128)(2,1)S(1)} %rep_sum.1.refs_0_), channel_id=1, source_target_pairs={{0,24},{4,28},{8,16},{12,20},{16,8},{20,12},{24,0},{28,4},{1,25},{... | collective-permute-start | bytes 49160 | tf_op jit(solution)/shard_map/ppermute | solution.py:217
  40.8 0.9 %collective-permute-start.16 = (bf16[32,256]{1,0:T(8,128)(2,1)S(1)}, bf16[32,256]{1,0:T(8,128)(2,1)S(1)}, u32[]{:S(2)}, u32[]{:S(2)}) collective-permute-start(bf16[32,256]{1,0:T(8,128)(2,1)S(1)} %rep_sum.1.refs_0_), channel_id=1, source_target_pairs={{0,16},{4,20},{8,24},{12,28},{16,0},{20,4},{24,8},{28,12},{1,17},{... | collective-permute-start | bytes 49160 | tf_op jit(solution)/shard_map/ppermute | solution.py:217
  41.7 1.0 %collective-permute-start.15 = (bf16[32,256]{1,0:T(8,128)(2,1)S(1)}, bf16[32,256]{1,0:T(8,128)(2,1)S(1)}, u32[]{:S(2)}, u32[]{:S(2)}) collective-permute-start(bf16[32,256]{1,0:T(8,128)(2,1)S(1)} %rep_sum.1.refs_0_), channel_id=1, source_target_pairs={{0,8},{4,12},{8,0},{12,4},{16,24},{20,28},{24,16},{28,20},{1,9},{5... | collective-permute-start | bytes 49160 | tf_op jit(solution)/shard_map/ppermute | solution.py:217
  42.6 1.1 %collective-permute-done.17.refs_3_ = bf16[32,256]{1,0:T(8,128)(2,1)S(1)} collective-permute-done((bf16[32,256]{1,0:T(8,128)(2,1)S(1)}, bf16[32,256]{1,0:T(8,128)(2,1)S(1)}, u32[]{:S(2)}, u32[]{:S(2)}) %collective-permute-start.17) | collective-permute-done | bytes 16416 | tf_op jit(solution)/shard_map/ppermute | solution.py:217
  43.8 0.7 %collective-permute-done.16.refs_2_ = bf16[32,256]{1,0:T(8,128)(2,1)S(1)} collective-permute-done((bf16[32,256]{1,0:T(8,128)(2,1)S(1)}, bf16[32,256]{1,0:T(8,128)(2,1)S(1)}, u32[]{:S(2)}, u32[]{:S(2)}) %collective-permute-start.16) | collective-permute-done | bytes 16416 | tf_op jit(solution)/shard_map/ppermute | solution.py:217
  44.5 0.9 %collective-permute-done.15.refs_1_ = bf16[32,256]{1,0:T(8,128)(2,1)S(1)} collective-permute-done((bf16[32,256]{1,0:T(8,128)(2,1)S(1)}, bf16[32,256]{1,0:T(8,128)(2,1)S(1)}, u32[]{:S(2)}, u32[]{:S(2)}) %collective-permute-start.15) | collective-permute-done | bytes 16416 | tf_op jit(solution)/shard_map/ppermute | solution.py:217
  45.5 1.1 %input_gradient.1.order_ref = bf16[256,256]{1,0:T(8,128)(2,1)} custom-call(s32[1,8,16]{2,1,0:T(8,128)S(1)} %get-tuple-element.38.index_ref, bf16[256,256]{1,0:T(8,128)(2,1)S(1)} %copy-done.1, f32[256,256]{1,0:T(8,128)S(1)} %get-tuple-element.40.order_ref.own_ref, bf16[32,256]{1,0:T(8,128)(2,1)S(1)} %get-tuple-element.44.refs_0_, ...), custom_call_target="tpu_custom_call" | custom-call | flops 1 | bytes 1 | tf_op jit(solution)/shard_map/input_gradient/pallas_call | solution.py:323
  46.6 0.2 collective-permute-done.18.got_ref
  46.8 0.7 %join.1 = f32[256,256]{1,0:T(8,128)} custom-call(bf16[128,256]{1,0:T(8,128)(2,1)S(1)} %half.1.own_ref, bf16[128,256]{1,0:T(8,128)(2,1)S(1)} %collective-permute-done.18.got_ref, bf16[256,256]{1,0:T(8,128)(2,1)} %input_gradient.1.order_ref), custom_call_target="tpu_custom_call" | custom-call | flops 1 | bytes 1 | tf_op jit(solution)/shard_map/join/pallas_call | solution.py:332
  (24 shorter events, 0.3 us)
Async XLA Ops:
  0.6 16.7 %collective-permute-start.1 = (bf16[256,256]{1,0:T(8,128)(2,1)}, bf16[256,256]{1,0:T(8,128)(2,1)S(1)}, u32[]{:S(2)}, u32[]{:S(2)}) collective-permute-start(bf16[256,256]{1,0:T(8,128)(2,1)} %refs_0_.3), channel_id=1, source_target_pairs={{0,2},{1,3},{2,0},{3,1},{4,6},{5,7},{6,4},{7,5},{8,10},{9,11},{10,... | collective-permute-start | bytes 393224 | tf_op jit(solution)/shard_map/ppermute | solution.py:214
  4.7 12.6 %collective-permute-start = (bf16[256,256]{1,0:T(8,128)(2,1)}, bf16[256,256]{1,0:T(8,128)(2,1)S(1)}, u32[]{:S(2)}, u32[]{:S(2)}) collective-permute-start(bf16[256,256]{1,0:T(8,128)(2,1)} %refs_0_.3), channel_id=1, source_target_pairs={{0,1},{1,0},{2,3},{3,2},{4,5},{5,4},{6,7},{7,6},{8,9},{9,8},{10,11... | collective-permute-start | bytes 393224 | tf_op jit(solution)/shard_map/ppermute | solution.py:214
  6.3 11.0 %collective-permute-start.2 = (bf16[256,256]{1,0:T(8,128)(2,1)}, bf16[256,256]{1,0:T(8,128)(2,1)S(1)}, u32[]{:S(2)}, u32[]{:S(2)}) collective-permute-start(bf16[256,256]{1,0:T(8,128)(2,1)} %refs_0_.3), channel_id=1, source_target_pairs={{0,3},{1,2},{2,1},{3,0},{4,7},{5,6},{6,5},{7,4},{8,11},{9,10},{10,... | collective-permute-start | bytes 393224 | tf_op jit(solution)/shard_map/ppermute | solution.py:214
  6.3 11.0 %copy-start = (bf16[256,256]{1,0:T(8,128)(2,1)S(1)}, bf16[256,256]{1,0:T(8,128)(2,1)}, u32[]{:S(2)}) copy-start(bf16[256,256]{1,0:T(8,128)(2,1)} %refs_0_.3) | copy-start | bytes 393220
  6.3 11.0 %copy-start.1 = (bf16[256,256]{1,0:T(8,128)(2,1)S(1)}, bf16[256,256]{1,0:T(8,128)(2,1)}, u32[]{:S(2)}) copy-start(bf16[256,256]{1,0:T(8,128)(2,1)} %weight_ref.3) | copy-start | bytes 393220
  7.6 9.7 %copy-start.2 = (bf16[256,128]{1,0:T(8,128)(2,1)S(1)}, bf16[256,128]{1,0:T(8,128)(2,1)}, u32[]{:S(2)}) copy-start(bf16[256,128]{1,0:T(8,128)(2,1)} %bnd_ref.1) | copy-start | bytes 196612
  7.6 1.3 %collective-permute-start.3 = (bf16[64,256]{1,0:T(8,128)(2,1)S(1)}, bf16[64,256]{1,0:T(8,128)(2,1)S(1)}, u32[]{:S(2)}, u32[]{:S(2)}) collective-permute-start(bf16[64,256]{1,0:T(8,128)(2,1)S(1)} %get-tuple-element.32), channel_id=1, source_target_pairs={{0,4},{4,0},{8,12},{12,8},{16,20},{20,16},{24,28},{28,24},{1,5},{5... | collective-permute-start | bytes 98312 | tf_op jit(solution)/shard_map/ppermute | solution.py:217
  8.9 3.7 %collective-permute-start.4 = (bf16[32,256]{1,0:T(8,128)(2,1)S(1)}, bf16[32,256]{1,0:T(8,128)(2,1)S(1)}, u32[]{:S(2)}, u32[]{:S(2)}) collective-permute-start(bf16[32,256]{1,0:T(8,128)(2,1)S(1)} %get-tuple-element.34), channel_id=1, source_target_pairs={{0,8},{4,12},{8,0},{12,4},{16,24},{20,28},{24,16},{28,20},{1,9},{5... | collective-permute-start | bytes 49160 | tf_op jit(solution)/shard_map/ppermute | solution.py:217
  10.6 4.7 %collective-permute-start.5 = (bf16[32,256]{1,0:T(8,128)(2,1)S(1)}, bf16[32,256]{1,0:T(8,128)(2,1)S(1)}, u32[]{:S(2)}, u32[]{:S(2)}) collective-permute-start(bf16[32,256]{1,0:T(8,128)(2,1)S(1)} %get-tuple-element.35), channel_id=1, source_target_pairs={{0,16},{4,20},{8,24},{12,28},{16,0},{20,4},{24,8},{28,12},{1,17},{... | collective-permute-start | bytes 49160 | tf_op jit(solution)/shard_map/ppermute | solution.py:217
  12.7 4.6 %collective-permute-start.6 = (bf16[32,256]{1,0:T(8,128)(2,1)S(1)}, bf16[32,256]{1,0:T(8,128)(2,1)S(1)}, u32[]{:S(2)}, u32[]{:S(2)}) collective-permute-start(bf16[32,256]{1,0:T(8,128)(2,1)S(1)} %get-tuple-element.36), channel_id=1, source_target_pairs={{0,24},{4,28},{8,16},{12,20},{16,8},{20,12},{24,0},{28,4},{1,25},{... | collective-permute-start | bytes 49160 | tf_op jit(solution)/shard_map/ppermute | solution.py:217
  19.4 2.1 %collective-permute-start.7 = (bf16[192,256]{1,0:T(8,128)(2,1)S(1)}, bf16[192,256]{1,0:T(8,128)(2,1)S(1)}, u32[]{:S(2)}, u32[]{:S(2)}) collective-permute-start(bf16[192,256]{1,0:T(8,128)(2,1)S(1)} %get-tuple-element.43), channel_id=1, source_target_pairs={{0,4},{4,0},{8,12},{12,8},{16,20},{20,16},{24,28},{28,24},{1,5},{5... | collective-permute-start | bytes 294920 | tf_op jit(solution)/shard_map/ppermute | solution.py:217
  20.5 16.2 %collective-permute-start.11 = (bf16[512,256]{1,0:T(8,128)(2,1)S(1)}, bf16[512,256]{1,0:T(8,128)(2,1)S(1)}, u32[]{:S(2)}, u32[]{:S(2)}) collective-permute-start(bf16[512,256]{1,0:T(8,128)(2,1)S(1)} %get-tuple-element.48), channel_id=1, source_target_pairs={{0,1},{1,0},{2,3},{3,2},{4,5},{5,4},{6,7},{7,6},{8,9},{9,8},{10,11... | collective-permute-start | bytes 786440 | tf_op jit(solution)/shard_map/ppermute | solution.py:214
  21.5 4.0 %collective-permute-start.8 = (bf16[64,256]{1,0:T(8,128)(2,1)S(1)}, bf16[64,256]{1,0:T(8,128)(2,1)S(1)}, u32[]{:S(2)}, u32[]{:S(2)}) collective-permute-start(bf16[64,256]{1,0:T(8,128)(2,1)S(1)} %get-tuple-element.45), channel_id=1, source_target_pairs={{0,8},{4,12},{8,0},{12,4},{16,24},{20,28},{24,16},{28,20},{1,9},{5... | collective-permute-start | bytes 98312 | tf_op jit(solution)/shard_map/ppermute | solution.py:217
  23.1 3.9 %collective-permute-start.9 = (bf16[64,256]{1,0:T(8,128)(2,1)S(1)}, bf16[64,256]{1,0:T(8,128)(2,1)S(1)}, u32[]{:S(2)}, u32[]{:S(2)}) collective-permute-start(bf16[64,256]{1,0:T(8,128)(2,1)S(1)} %get-tuple-element.46), channel_id=1, source_target_pairs={{0,16},{4,20},{8,24},{12,28},{16,0},{20,4},{24,8},{28,12},{1,17},{... | collective-permute-start | bytes 98312 | tf_op jit(solution)/shard_map/ppermute | solution.py:217
  24.6 4.8 %collective-permute-start.10 = (bf16[64,256]{1,0:T(8,128)(2,1)S(1)}, bf16[64,256]{1,0:T(8,128)(2,1)S(1)}, u32[]{:S(2)}, u32[]{:S(2)}) collective-permute-start(bf16[64,256]{1,0:T(8,128)(2,1)S(1)} %get-tuple-element.47), channel_id=1, source_target_pairs={{0,24},{4,28},{8,16},{12,20},{16,8},{20,12},{24,0},{28,4},{1,25},{... | collective-permute-start | bytes 98312 | tf_op jit(solution)/shard_map/ppermute | solution.py:217
  29.4 3.8 %collective-permute-start.12 = (bf16[32,256]{1,0:T(8,128)(2,1)S(1)}, bf16[32,256]{1,0:T(8,128)(2,1)S(1)}, u32[]{:S(2)}, u32[]{:S(2)}) collective-permute-start(bf16[32,256]{1,0:T(8,128)(2,1)S(1)} %share_sum.1.own_ref), channel_id=1, source_target_pairs={{0,1},{1,0},{2,3},{3,2},{4,5},{5,4},{6,7},{7,6},{8,9},{9,8},{10,11... | collective-permute-start | bytes 49160 | tf_op jit(solution)/shard_map/ppermute | solution.py:214
  33.2 5.9 %collective-permute-start.14 = (bf16[32,256]{1,0:T(8,128)(2,1)S(1)}, bf16[32,256]{1,0:T(8,128)(2,1)S(1)}, u32[]{:S(2)}, u32[]{:S(2)}) collective-permute-start(bf16[32,256]{1,0:T(8,128)(2,1)S(1)} %pair_sum.1.refs_0_.own_ref), channel_id=1, source_target_pairs={{0,2},{1,3},{2,0},{3,1},{4,6},{5,7},{6,4},{7,5},{8,10},{9,11},{10,... | collective-permute-start | bytes 49160 | tf_op jit(solution)/shard_map/ppermute | solution.py:214
  36.7 8.8 %collective-permute-start.13 = (bf16[256,256]{1,0:T(8,128)(2,1)S(1)}, bf16[256,256]{1,0:T(8,128)(2,1)S(1)}, u32[]{:S(2)}, u32[]{:S(2)}) collective-permute-start(bf16[256,256]{1,0:T(8,128)(2,1)S(1)} %relay.1), channel_id=1, source_target_pairs={{0,2},{1,3},{2,0},{3,1},{4,6},{5,7},{6,4},{7,5},{8,10},{9,11},{10,... | collective-permute-start | bytes 393224 | tf_op jit(solution)/shard_map/ppermute | solution.py:214
  39.2 4.6 %collective-permute-start.17 = (bf16[32,256]{1,0:T(8,128)(2,1)S(1)}, bf16[32,256]{1,0:T(8,128)(2,1)S(1)}, u32[]{:S(2)}, u32[]{:S(2)}) collective-permute-start(bf16[32,256]{1,0:T(8,128)(2,1)S(1)} %rep_sum.1.refs_0_), channel_id=1, source_target_pairs={{0,24},{4,28},{8,16},{12,20},{16,8},{20,12},{24,0},{28,4},{1,25},{... | collective-permute-start | bytes 49160 | tf_op jit(solution)/shard_map/ppermute | solution.py:217
  40.8 3.7 %collective-permute-start.16 = (bf16[32,256]{1,0:T(8,128)(2,1)S(1)}, bf16[32,256]{1,0:T(8,128)(2,1)S(1)}, u32[]{:S(2)}, u32[]{:S(2)}) collective-permute-start(bf16[32,256]{1,0:T(8,128)(2,1)S(1)} %rep_sum.1.refs_0_), channel_id=1, source_target_pairs={{0,16},{4,20},{8,24},{12,28},{16,0},{20,4},{24,8},{28,12},{1,17},{... | collective-permute-start | bytes 49160 | tf_op jit(solution)/shard_map/ppermute | solution.py:217
  41.7 3.7 %collective-permute-start.15 = (bf16[32,256]{1,0:T(8,128)(2,1)S(1)}, bf16[32,256]{1,0:T(8,128)(2,1)S(1)}, u32[]{:S(2)}, u32[]{:S(2)}) collective-permute-start(bf16[32,256]{1,0:T(8,128)(2,1)S(1)} %rep_sum.1.refs_0_), channel_id=1, source_target_pairs={{0,8},{4,12},{8,0},{12,4},{16,24},{20,28},{24,16},{28,20},{1,9},{5... | collective-permute-start | bytes 49160 | tf_op jit(solution)/shard_map/ppermute | solution.py:217
  45.4 1.3 %collective-permute-start.18 = (bf16[128,256]{1,0:T(8,128)(2,1)S(1)}, bf16[128,256]{1,0:T(8,128)(2,1)S(1)}, u32[]{:S(2)}, u32[]{:S(2)}) collective-permute-start(bf16[128,256]{1,0:T(8,128)(2,1)S(1)} %half.1.own_ref), channel_id=1, source_target_pairs={{0,4},{4,0},{8,12},{12,8},{16,20},{20,16},{24,28},{28,24},{1,5},{5... | collective-permute-start | bytes 196616 | tf_op jit(solution)/shard_map/ppermute | solution.py:217
